TPU v7x, 512 devices: a whole 4x8x8 slice. The times are simulated.
512 devices in a mesh: gx: 8 (over y), gy: 8 (over x, core), gz: 8 (over z).
Axes of the slice: x: 4, y: 8, z: 8, core: 2. Of those that a mesh axis runs over, the one named last changes fastest.
Arguments:
- positions: float32 [3, 96, 48, 48, 128], P(None, 'gx', 'gy', 'gz'), may hold values from 0 to 96, as said below
- mass: float32 [96, 48, 48, 128], P('gx', 'gy', 'gz'), may hold values from 0.003 to 0.03
- support: float32 [96, 48, 48, 128], P('gx', 'gy', 'gz'), may hold values from 0.5 to 1
- counts: int32 [96, 48, 48], P('gx', 'gy', 'gz'), may hold values from 32 to 128
- entropy: float32 [96, 48, 48, 128], P('gx', 'gy', 'gz'), may hold values from 0.2 to 2
- density_old: float32 [96, 48, 48, 128], P('gx', 'gy', 'gz'), may hold values from 0.3 to 3
- active: int32 [96, 48, 48], P('gx', 'gy', 'gz'), may hold values from 0 to 1, as said below
Outputs:
- density: float32 [96, 48, 48, 128], P('gx', 'gy', 'gz')
- accel: float32 [3, 96, 48, 48, 128], P(None, 'gx', 'gy', 'gz')
Inputs may be any that keep to these rules, and one draw needn't show every extreme that they name: At most 9 cells are active in the block of 12 x 6 x 6 cells of one device, and exactly 9 in some device's block; every device's block has at least one. `positions`: each particle lies in its own cell: the unit cube whose lower corner is the cell's index.
All inputs are finite; a program needn't handle non-finite values.
Results may differ from a plain program's by a relative error of at most 0.0003.
Values sent between devices are 32-bit elements; how exact they have to be, the bound alone decides.
No kernel may reach another device: no remote copies, remote signals or barrier semaphores. Data moves between devices by JAX's collectives and lax.ppermute only.
A program may use at most 64 MiB of HBM per device.

v0:
```python
import math

import jax
import jax.numpy as jnp
from jax import lax
from jax.sharding import PartitionSpec as P

KC = 21.0 / (2.0 * math.pi)


def padded(value, sides, width):
    for axis, dim in sides:
        size, length = (lax.axis_size(axis), value.shape[dim])
        up = [(i, (i + 1) % size) for i in range(size - 1)]
        down = [(j, i) for i, j in up]
        last = lax.slice_in_dim(value, length - width, length, axis=dim)
        initial = lax.slice_in_dim(value, 0, width, axis=dim)
        before = lax.ppermute(last, axis, up)
        after = lax.ppermute(initial, axis, down)
        value = jnp.concatenate([before, value, after], axis=dim)
    return value


def density_terms(own, near):
    diff = own[:3, :, None] - near[:3, None, :]
    dist = jnp.sqrt(jnp.sum(diff * diff, axis=0))
    qval = dist * own[4][:, None]
    wval = jnp.maximum(1.0 - qval, 0.0)
    kern = wval**4 * (1.0 + 4.0 * qval) * own[4][:, None] ** 3
    return KC * jnp.sum(near[3][None, :] * kern, axis=1)


def force_terms(own, own_p, near, near_p):
    diff = own[:3, :, None] - near[:3, None, :]
    dist = jnp.sqrt(jnp.sum(diff * diff, axis=0))
    w_own = jnp.maximum(1.0 - dist * own[4][:, None], 0.0)
    w_near = jnp.maximum(1.0 - dist * near[4][None, :], 0.0)
    g_own = w_own**3 * own[4][:, None] ** 5
    g_near = w_near**3 * near[4][None, :] ** 5
    coef = near[3][None, :] * (own_p[:, None] * g_own + near_p[None, :] * g_near)
    return 20.0 * KC * jnp.sum(coef[None] * diff, axis=2)


def per_device(positions, mass, support, counts, entropy, density_old, active):
    size_x, size_y, size_z, slots = mass.shape
    cells = size_x * size_y * size_z
    valid = jnp.arange(slots, dtype=jnp.int32)[None, None, None, :] < counts[..., None]
    m_eff = jnp.where(valid, mass, jnp.float32(0.0))
    rows = [positions, m_eff[None], (1.0 / support)[None]]
    pack = jnp.concatenate(rows, axis=0)
    extended = padded(pack, (("gx", 1), ("gy", 2), ("gz", 3)), 1)
    flat = active.reshape(cells)
    capacity = max(2, cells // 48)
    rank = jnp.cumsum(flat) - 1
    picked = (rank[None, :] == jnp.arange(capacity, dtype=jnp.int32)[:, None]) & (flat[None, :] > 0)
    picked_int = picked.astype(jnp.int32)
    cell_ids = jnp.sum(picked_int * jnp.arange(cells, dtype=jnp.int32)[None, :], axis=1)
    selector = picked.astype(jnp.float32)

    def corner(cell):
        return (cell // (size_y * size_z), cell // size_z % size_y, cell % size_z)

    def dens_one(cell):
        a, b, d = corner(cell)
        zero = jnp.int32(0)
        near = lax.dynamic_slice(extended, (zero, a, b, d, zero), (5, 3, 3, 3, slots)).reshape(
            5, 27 * slots
        )
        own = lax.dynamic_slice(
            extended, (zero, a + 1, b + 1, d + 1, zero), (5, 1, 1, 1, slots)
        ).reshape(5, slots)
        return density_terms(own, near)

    fresh = lax.map(dens_one, cell_ids)
    grid_new = jnp.dot(selector.T, fresh, precision=lax.Precision.HIGHEST).reshape(
        size_x, size_y, size_z, slots
    )
    act = (active > 0)[..., None]
    density = jnp.where(act & valid, grid_new, density_old)
    pterm = entropy * density ** (-1.0 / 3.0)
    p_ext = padded(pterm, (("gx", 0), ("gy", 1), ("gz", 2)), 1)

    def force_one(cell):
        a, b, d = corner(cell)
        zero = jnp.int32(0)
        near = lax.dynamic_slice(extended, (zero, a, b, d, zero), (5, 3, 3, 3, slots)).reshape(
            5, 27 * slots
        )
        own = lax.dynamic_slice(
            extended, (zero, a + 1, b + 1, d + 1, zero), (5, 1, 1, 1, slots)
        ).reshape(5, slots)
        near_p = lax.dynamic_slice(p_ext, (a, b, d, zero), (3, 3, 3, slots)).reshape(27 * slots)
        own_p = lax.dynamic_slice(p_ext, (a + 1, b + 1, d + 1, zero), (1, 1, 1, slots)).reshape(
            slots
        )
        return force_terms(own, own_p, near, near_p)

    pushes = lax.map(force_one, cell_ids)
    grid_acc = jnp.einsum("kc,kvs->vcs", selector, pushes, precision=lax.Precision.HIGHEST)
    accel = grid_acc.reshape(3, size_x, size_y, size_z, slots) * valid[None].astype(jnp.float32)
    return (density, accel)


def solution(mesh):
    return jax.shard_map(
        per_device,
        mesh=mesh,
        in_specs=(
            P(None, "gx", "gy", "gz", None),
            P("gx", "gy", "gz", None),
            P("gx", "gy", "gz", None),
            P("gx", "gy", "gz"),
            P("gx", "gy", "gz", None),
            P("gx", "gy", "gz", None),
            P("gx", "gy", "gz"),
        ),
        out_specs=(P("gx", "gy", "gz", None), P(None, "gx", "gy", "gz", None)),
        check_vma=False,
    )
```

profile of v0, /device:TPU:83, one launch (start us, length us, event | category | flops | bytes accessed | tf_op | source)
XLA Modules:
  0.0 253.2 jit_solution(9587580570876815338)
XLA Ops:
  2.8 3.2 %collective-permute-start = (f32[5,1,6,6,128]{4,3,2,1,0:T(8,128)S(1)}, f32[5,1,6,6,128]{4,3,2,1,0:T(8,128)S(1)}, u32[]{:S(2)}, u32[]{:S(2)}) collective-permute-start(f32[5,1,6,6,128]{4,3,2,1,0:T(8,128)S(1)} %get-tuple-element.224), channel_id=1, source_target_pairs={{0,64},{64,128},{128,192},{192,256},{256,320},{320,384},{384,448},... | collective-permute-start | bytes 276488 | tf_op jit(solution)/shard_map/ppermute | solution.py:18
  6.0 2.1 collective-permute-start.1
  9.2 4.0 %collective-permute-done.1 = f32[5,1,6,6,128]{4,3,2,1,0:T(8,128)S(1)} collective-permute-done((f32[5,1,6,6,128]{4,3,2,1,0:T(8,128)S(1)}, f32[5,1,6,6,128]{4,3,2,1,0:T(8,128)S(1)}, u32[]{:S(2)}, u32[]{:S(2)}) %collective-permute-start.1) | collective-permute-done | bytes 92192 | tf_op jit(solution)/shard_map/ppermute | solution.py:19
  13.2 4.6 %collective-permute-start.2 = (f32[5,14,1,6,128]{4,3,2,1,0:T(8,128)S(1)}, f32[5,14,1,6,128]{4,3,2,1,0:T(8,128)S(1)}, u32[]{:S(2)}, u32[]{:S(2)}) collective-permute-start(f32[5,14,1,6,128]{4,3,2,1,0:T(8,128)S(1)} %get-tuple-element.222), channel_id=1, source_target_pairs={{0,8},{8,16},{16,24},{24,32},{32,40},{40,48},{48,56},{1,9},{9,17},... | collective-permute-start | bytes 645128 | tf_op jit(solution)/shard_map/ppermute | solution.py:18
  17.8 1.9 collective-permute-start.3
  19.7 1.6 collective-permute-done.2
  21.4 4.4 %collective-permute-done.3 = f32[5,14,1,6,128]{4,3,2,1,0:T(8,128)S(1)} collective-permute-done((f32[5,14,1,6,128]{4,3,2,1,0:T(8,128)S(1)}, f32[5,14,1,6,128]{4,3,2,1,0:T(8,128)S(1)}, u32[]{:S(2)}, u32[]{:S(2)}) %collective-permute-start.3) | collective-permute-done | bytes 215072 | tf_op jit(solution)/shard_map/ppermute | solution.py:19
  26.9 4.0 %collective-permute-start.4 = (f32[5,14,8,1,128]{4,3,2,1,0:T(1,128)S(1)}, f32[5,14,8,1,128]{4,3,2,1,0:T(1,128)S(1)}, u32[]{:S(2)}, u32[]{:S(2)}) collective-permute-start(f32[5,14,8,1,128]{4,3,2,1,0:T(1,128)S(1)} %get-tuple-element.220), channel_id=1, source_target_pairs={{0,1},{1,2},{2,3},{3,4},{4,5},{5,6},{6,7},{8,9},{9,10},{10,11},{11... | collective-permute-start | bytes 860168 | tf_op jit(solution)/shard_map/ppermute | solution.py:18
  30.9 1.9 collective-permute-start.5
  33.0 3.9 %collective-permute-done.4 = f32[5,14,8,1,128]{4,3,2,1,0:T(1,128)S(1)} collective-permute-done((f32[5,14,8,1,128]{4,3,2,1,0:T(1,128)S(1)}, f32[5,14,8,1,128]{4,3,2,1,0:T(1,128)S(1)}, u32[]{:S(2)}, u32[]{:S(2)}) %collective-permute-start.4) | collective-permute-done | bytes 286752 | tf_op jit(solution)/shard_map/ppermute | solution.py:18
  36.8 4.4 %collective-permute-done.5 = f32[5,14,8,1,128]{4,3,2,1,0:T(1,128)S(1)} collective-permute-done((f32[5,14,8,1,128]{4,3,2,1,0:T(1,128)S(1)}, f32[5,14,8,1,128]{4,3,2,1,0:T(1,128)S(1)}, u32[]{:S(2)}, u32[]{:S(2)}) %collective-permute-start.5) | collective-permute-done | bytes 286752 | tf_op jit(solution)/shard_map/ppermute | solution.py:19
  41.2 2.2 pad_maximum_fusion
  43.4 81.3 %while.26 = (s32[]{:T(128)}, f32[9,128]{1,0:T(8,128)S(1)}, s32[9]{0:T(128)S(1)}, f32[5,14,8,8,128]{4,3,2,1,0:T(8,128)}, s32[]{:T(128)}, /*index=5*/s32[1]{0:T(12...) while((s32[]{:T(128)}, f32[9,128]{1,0:T(8,128)S(1)}, ...), condition=%wide.region_6.7_spmd, body=%wide.region_3.6_spmd.sunk | while | flops 8405297 | bytes 3828959 | solution.py:74
  126.3 4.7 %collective-permute-start.6 = (f32[1,6,6,128]{3,2,1,0:T(8,128)S(1)}, f32[1,6,6,128]{3,2,1,0:T(8,128)S(1)}, u32[]{:S(2)}, u32[]{:S(2)}) collective-permute-start(f32[1,6,6,128]{3,2,1,0:T(8,128)S(1)} %get-tuple-element.230), channel_id=1, source_target_pairs={{0,64},{64,128},{128,192},{192,256},{256,320},{320,384},{384,448},... | collective-permute-start | bytes 55304 | tf_op jit(solution)/shard_map/ppermute | solution.py:18
  131.0 1.9 collective-permute-start.7
  132.9 2.6 %collective-permute-done.7 = f32[1,6,6,128]{3,2,1,0:T(8,128)S(1)} collective-permute-done((f32[1,6,6,128]{3,2,1,0:T(8,128)S(1)}, f32[1,6,6,128]{3,2,1,0:T(8,128)S(1)}, u32[]{:S(2)}, u32[]{:S(2)}) %collective-permute-start.7) | collective-permute-done | bytes 18464 | tf_op jit(solution)/shard_map/ppermute | solution.py:19
  135.6 4.7 %collective-permute-start.8 = (f32[14,1,6,128]{3,2,1,0:T(8,128)S(1)}, f32[14,1,6,128]{3,2,1,0:T(8,128)S(1)}, u32[]{:S(2)}, u32[]{:S(2)}) collective-permute-start(f32[14,1,6,128]{3,2,1,0:T(8,128)S(1)} %get-tuple-element.228), channel_id=1, source_target_pairs={{0,8},{8,16},{16,24},{24,32},{32,40},{40,48},{48,56},{1,9},{9,17},... | collective-permute-start | bytes 129032 | tf_op jit(solution)/shard_map/ppermute | solution.py:18
  140.3 1.9 collective-permute-start.9
  142.2 3.6 %collective-permute-done.9 = f32[14,1,6,128]{3,2,1,0:T(8,128)S(1)} collective-permute-done((f32[14,1,6,128]{3,2,1,0:T(8,128)S(1)}, f32[14,1,6,128]{3,2,1,0:T(8,128)S(1)}, u32[]{:S(2)}, u32[]{:S(2)}) %collective-permute-start.9) | collective-permute-done | bytes 43040 | tf_op jit(solution)/shard_map/ppermute | solution.py:19
  145.9 5.2 %collective-permute-start.10 = (f32[14,8,1,128]{3,2,1,0:T(1,128)S(1)}, f32[14,8,1,128]{3,2,1,0:T(1,128)S(1)}, u32[]{:S(2)}, u32[]{:S(2)}) collective-permute-start(f32[14,8,1,128]{3,2,1,0:T(1,128)S(1)} %get-tuple-element.226), channel_id=1, source_target_pairs={{0,1},{1,2},{2,3},{3,4},{4,5},{5,6},{6,7},{8,9},{9,10},{10,11},{11... | collective-permute-start | bytes 172040 | tf_op jit(solution)/shard_map/ppermute | solution.py:18
  151.1 1.9 collective-permute-start.11
  153.2 4.5 %collective-permute-done.11 = f32[14,8,1,128]{3,2,1,0:T(1,128)S(1)} collective-permute-done((f32[14,8,1,128]{3,2,1,0:T(1,128)S(1)}, f32[14,8,1,128]{3,2,1,0:T(1,128)S(1)}, u32[]{:S(2)}, u32[]{:S(2)}) %collective-permute-start.11) | collective-permute-done | bytes 57376 | tf_op jit(solution)/shard_map/ppermute | solution.py:19
  157.8 93.8 %while.27 = (s32[]{:T(128)}, f32[9,3,128]{2,0,1:T(8,128)S(1)}, s32[9]{0:T(128)S(1)}, f32[5,14,8,8,128]{4,3,2,1,0:T(8,128)}, f32[14,8,8,128]{3,2,1,0:T(8,128)S(1)...) while((s32[]{:T(128)}, f32[9,3,128]{2,0,1:T(8,128)S(1)}, ...), condition=%wide.region_10.11_spmd, body=%wide.region_7.10_spmd.sunk | while | flops 14608945 | bytes 7600387 | solution.py:98
  166.1 1.4 fusion.35
  176.5 1.4 fusion.35
  186.9 1.4 fusion.35
  197.4 1.4 fusion.35
  207.8 1.4 fusion.35
  218.2 1.4 fusion.35
  228.6 1.4 fusion.35
  239.0 1.4 fusion.35
  249.5 1.4 fusion.35
  (313 shorter events, 107.9 us)
Async XLA Ops:
  0.6 2.2 copy-start
  0.6 7.5 %copy-start.3 = (s32[12,6,6]{0,2,1:T(8,128)S(1)}, s32[12,6,6]{0,2,1:T(8,128)}, u32[]{:S(2)}) copy-start(s32[12,6,6]{0,2,1:T(8,128)} %param.17) | copy-start | bytes 5188
  2.8 6.4 %collective-permute-start = (f32[5,1,6,6,128]{4,3,2,1,0:T(8,128)S(1)}, f32[5,1,6,6,128]{4,3,2,1,0:T(8,128)S(1)}, u32[]{:S(2)}, u32[]{:S(2)}) collective-permute-start(f32[5,1,6,6,128]{4,3,2,1,0:T(8,128)S(1)} %get-tuple-element.224), channel_id=1, source_target_pairs={{0,64},{64,128},{128,192},{192,256},{256,320},{320,384},{384,448},... | collective-permute-start | bytes 276488 | tf_op jit(solution)/shard_map/ppermute | solution.py:18
  6.0 7.1 %collective-permute-start.1 = (f32[5,1,6,6,128]{4,3,2,1,0:T(8,128)S(1)}, f32[5,1,6,6,128]{4,3,2,1,0:T(8,128)S(1)}, u32[]{:S(2)}, u32[]{:S(2)}) collective-permute-start(f32[5,1,6,6,128]{4,3,2,1,0:T(8,128)S(1)} %get-tuple-element.225), channel_id=1, source_target_pairs={{64,0},{128,64},{192,128},{256,192},{320,256},{384,320},{448,384},... | collective-permute-start | bytes 276488 | tf_op jit(solution)/shard_map/ppermute | solution.py:19
  13.2 8.1 %collective-permute-start.2 = (f32[5,14,1,6,128]{4,3,2,1,0:T(8,128)S(1)}, f32[5,14,1,6,128]{4,3,2,1,0:T(8,128)S(1)}, u32[]{:S(2)}, u32[]{:S(2)}) collective-permute-start(f32[5,14,1,6,128]{4,3,2,1,0:T(8,128)S(1)} %get-tuple-element.222), channel_id=1, source_target_pairs={{0,8},{8,16},{16,24},{24,32},{32,40},{40,48},{48,56},{1,9},{9,17},... | collective-permute-start | bytes 645128 | tf_op jit(solution)/shard_map/ppermute | solution.py:18
  17.8 8.0 %collective-permute-start.3 = (f32[5,14,1,6,128]{4,3,2,1,0:T(8,128)S(1)}, f32[5,14,1,6,128]{4,3,2,1,0:T(8,128)S(1)}, u32[]{:S(2)}, u32[]{:S(2)}) collective-permute-start(f32[5,14,1,6,128]{4,3,2,1,0:T(8,128)S(1)} %get-tuple-element.223), channel_id=1, source_target_pairs={{8,0},{16,8},{24,16},{32,24},{40,32},{48,40},{56,48},{9,1},{17,9},... | collective-permute-start | bytes 645128 | tf_op jit(solution)/shard_map/ppermute | solution.py:19
  26.9 9.9 %collective-permute-start.4 = (f32[5,14,8,1,128]{4,3,2,1,0:T(1,128)S(1)}, f32[5,14,8,1,128]{4,3,2,1,0:T(1,128)S(1)}, u32[]{:S(2)}, u32[]{:S(2)}) collective-permute-start(f32[5,14,8,1,128]{4,3,2,1,0:T(1,128)S(1)} %get-tuple-element.220), channel_id=1, source_target_pairs={{0,1},{1,2},{2,3},{3,4},{4,5},{5,6},{6,7},{8,9},{9,10},{10,11},{11... | collective-permute-start | bytes 860168 | tf_op jit(solution)/shard_map/ppermute | solution.py:18
  30.9 10.3 %collective-permute-start.5 = (f32[5,14,8,1,128]{4,3,2,1,0:T(1,128)S(1)}, f32[5,14,8,1,128]{4,3,2,1,0:T(1,128)S(1)}, u32[]{:S(2)}, u32[]{:S(2)}) collective-permute-start(f32[5,14,8,1,128]{4,3,2,1,0:T(1,128)S(1)} %get-tuple-element.221), channel_id=1, source_target_pairs={{1,0},{2,1},{3,2},{4,3},{5,4},{6,5},{7,6},{9,8},{10,9},{11,10},{12... | collective-permute-start | bytes 860168 | tf_op jit(solution)/shard_map/ppermute | solution.py:19
  43.4 81.8 %copy-start.1 = (f32[12,6,6,128]{3,2,1,0:T(8,128)S(1)}, f32[12,6,6,128]{3,2,1,0:T(8,128)}, u32[]{:S(2)}) copy-start(f32[12,6,6,128]{3,2,1,0:T(8,128)} %param.15) | copy-start | bytes 663556
  43.4 81.8 %copy-start.2 = (f32[12,6,6,128]{3,2,1,0:T(8,128)S(1)}, f32[12,6,6,128]{3,2,1,0:T(8,128)}, u32[]{:S(2)}) copy-start(f32[12,6,6,128]{3,2,1,0:T(8,128)} %param.16) | copy-start | bytes 663556
  126.3 6.6 %collective-permute-start.6 = (f32[1,6,6,128]{3,2,1,0:T(8,128)S(1)}, f32[1,6,6,128]{3,2,1,0:T(8,128)S(1)}, u32[]{:S(2)}, u32[]{:S(2)}) collective-permute-start(f32[1,6,6,128]{3,2,1,0:T(8,128)S(1)} %get-tuple-element.230), channel_id=1, source_target_pairs={{0,64},{64,128},{128,192},{192,256},{256,320},{320,384},{384,448},... | collective-permute-start | bytes 55304 | tf_op jit(solution)/shard_map/ppermute | solution.py:18
  131.0 4.6 %collective-permute-start.7 = (f32[1,6,6,128]{3,2,1,0:T(8,128)S(1)}, f32[1,6,6,128]{3,2,1,0:T(8,128)S(1)}, u32[]{:S(2)}, u32[]{:S(2)}) collective-permute-start(f32[1,6,6,128]{3,2,1,0:T(8,128)S(1)} %get-tuple-element.231), channel_id=1, source_target_pairs={{64,0},{128,64},{192,128},{256,192},{320,256},{384,320},{448,384},... | collective-permute-start | bytes 55304 | tf_op jit(solution)/shard_map/ppermute | solution.py:19
  135.6 6.6 %collective-permute-start.8 = (f32[14,1,6,128]{3,2,1,0:T(8,128)S(1)}, f32[14,1,6,128]{3,2,1,0:T(8,128)S(1)}, u32[]{:S(2)}, u32[]{:S(2)}) collective-permute-start(f32[14,1,6,128]{3,2,1,0:T(8,128)S(1)} %get-tuple-element.228), channel_id=1, source_target_pairs={{0,8},{8,16},{16,24},{24,32},{32,40},{40,48},{48,56},{1,9},{9,17},... | collective-permute-start | bytes 129032 | tf_op jit(solution)/shard_map/ppermute | solution.py:18
  140.3 5.5 %collective-permute-start.9 = (f32[14,1,6,128]{3,2,1,0:T(8,128)S(1)}, f32[14,1,6,128]{3,2,1,0:T(8,128)S(1)}, u32[]{:S(2)}, u32[]{:S(2)}) collective-permute-start(f32[14,1,6,128]{3,2,1,0:T(8,128)S(1)} %get-tuple-element.229), channel_id=1, source_target_pairs={{8,0},{16,8},{24,16},{32,24},{40,32},{48,40},{56,48},{9,1},{17,9},... | collective-permute-start | bytes 129032 | tf_op jit(solution)/shard_map/ppermute | solution.py:19
  145.9 7.3 %collective-permute-start.10 = (f32[14,8,1,128]{3,2,1,0:T(1,128)S(1)}, f32[14,8,1,128]{3,2,1,0:T(1,128)S(1)}, u32[]{:S(2)}, u32[]{:S(2)}) collective-permute-start(f32[14,8,1,128]{3,2,1,0:T(1,128)S(1)} %get-tuple-element.226), channel_id=1, source_target_pairs={{0,1},{1,2},{2,3},{3,4},{4,5},{5,6},{6,7},{8,9},{9,10},{10,11},{11... | collective-permute-start | bytes 172040 | tf_op jit(solution)/shard_map/ppermute | solution.py:18
  151.1 6.6 %collective-permute-start.11 = (f32[14,8,1,128]{3,2,1,0:T(1,128)S(1)}, f32[14,8,1,128]{3,2,1,0:T(1,128)S(1)}, u32[]{:S(2)}, u32[]{:S(2)}) collective-permute-start(f32[14,8,1,128]{3,2,1,0:T(1,128)S(1)} %get-tuple-element.227), channel_id=1, source_target_pairs={{1,0},{2,1},{3,2},{4,3},{5,4},{6,5},{7,6},{9,8},{10,9},{11,10},{12... | collective-permute-start | bytes 172040 | tf_op jit(solution)/shard_map/ppermute | solution.py:19
where the time goes:
time: 258 us; the launch traced here: 253 us
  loops' own time  63 us (24%)
  other arithmetic  62.5 us (24%)
  local copies, waits for them, and re-layouts  59 us (23%)
  starting transfers between devices  38 us (15%)
  waiting for transfers between devices  28.9 us (11%)
    another operation x1, loops' own time, per_device(): pushes = lax.map(force_one, cell_ids)  32.7 us
    another operation x1, loops' own time, per_device(): fresh = lax.map(dens_one, cell_ids)  30.3 us
    ppermute x6, starting transfers between devices, padded(): before = lax.ppermute(last, axis, up)  26.3 us
    ppermute x6, waiting for transfers between devices, padded(): after = lax.ppermute(initial, axis, down)  23.4 us
    slice x18, local copies, waits for them, and re-layouts, force_terms(): diff = own[:3, :, None] - near[:3, None, :]  14.8 us
    slice x18, local copies, waits for them, and re-layouts, density_terms(): diff = own[:3, :, None] - near[:3, None, :]  14.8 us
    mul x9, other arithmetic, force_terms(): near[3][None, :] * (own_p[:, None] * g_own + near_p[None, :] * g_near)  12.3 us
    ppermute x6, starting transfers between devices, padded(): after = lax.ppermute(initial, axis, down)  11.7 us
  transfers between devices with their start and end apart: 12, of which 8 were waited for; matrix products, arithmetic and copies ran while one was open for 1% of the time, Pallas kernels for 0%

commit v1 on v0

v1 whole, which is shorter than its diff:
```python
import math

import jax
import jax.numpy as jnp
from jax import lax
from jax.experimental import pallas as pl
from jax.experimental.pallas import tpu as pltpu
from jax.sharding import PartitionSpec as P

KC = 21.0 / (2.0 * math.pi)
HALO = 2


def padded(value, sides, width):
    for axis, dim in sides:
        size, length = (lax.axis_size(axis), value.shape[dim])
        up = [(i, (i + 1) % size) for i in range(size - 1)]
        down = [(j, i) for i, j in up]
        last = lax.slice_in_dim(value, length - width, length, axis=dim)
        initial = lax.slice_in_dim(value, 0, width, axis=dim)
        before = lax.ppermute(last, axis, up)
        after = lax.ppermute(initial, axis, down)
        value = jnp.concatenate([before, value, after], axis=dim)
    return value


def kernel(dims, flags_ref, ext_ref, old_ref, dens_ref, acc_ref, ids_ref, cols_ref, pt_ref):
    size_x, size_y, size_z = dims
    near_y, near_z = size_y + 2, size_z + 2
    total = (size_x + 2) * near_y * near_z

    def scan(k, n):
        ids_ref[n] = k
        return n + flags_ref[k]

    number = lax.fori_loop(0, total, scan, jnp.int32(0), unroll=8)

    def place(slot):
        k = ids_ref[slot]
        a = lax.div(k, near_y * near_z)
        b = lax.rem(lax.div(k, near_z), near_y)
        return a, b, lax.rem(k, near_z)

    def row(c, a, b, d):
        return ext_ref[c, a, b, pl.ds(d, 1), :]

    def load_columns(a, b, d):
        for n, c in enumerate((0, 1, 2, 4)):
            cols_ref[n] = jnp.broadcast_to(row(c, a + 1, b + 1, d + 1), (128, 128)).T

    def lane_sum(value):
        ones = jnp.ones((8, 128), jnp.float32)
        dims_ = (((1,), (1,)), ((), ()))
        out = lax.dot_general(
            ones, value, dims_, precision=lax.Precision.HIGHEST, preferred_element_type=jnp.float32
        )
        return out[0:1]

    pt_ref[...] = ext_ref[5, 1 : size_x + 3, 1 : size_y + 3]
    dens_ref[...] = old_ref[...]
    acc_ref[...] = jnp.zeros(acc_ref.shape, jnp.float32)

    def is_own(a, b, d):
        return (
            (a >= 1) & (a <= size_x) & (b >= 1) & (b <= size_y) & (d >= 1) & (d <= size_z)
        )

    def density(slot, _):
        a, b, d = place(slot)
        load_columns(a, b, d)

        def near(k, acc):
            na, nb, nd = a + lax.div(k, 9), b + lax.rem(lax.div(k, 3), 3), d + lax.rem(k, 3)
            dx = cols_ref[0] - row(0, na, nb, nd)
            dy = cols_ref[1] - row(1, na, nb, nd)
            dz = cols_ref[2] - row(2, na, nb, nd)
            sq = jnp.maximum(dx * dx + dy * dy + dz * dz, 1e-30)
            qv = sq * lax.rsqrt(sq) * cols_ref[3]
            w = jnp.maximum(1.0 - qv, 0.0)
            w2 = w * w
            return acc + row(3, na, nb, nd) * (w2 * w2 * (1.0 + 4.0 * qv))

        acc = lax.fori_loop(0, 27, near, jnp.zeros((128, 128), jnp.float32))
        inv = row(4, a + 1, b + 1, d + 1)
        fresh = KC * lane_sum(acc) * (inv * inv * inv)
        good = row(3, a + 1, b + 1, d + 1) > 0.0
        safe = jnp.where(good, fresh, 1.0)
        pt_ref[a, b, pl.ds(d + 1, 1), :] = row(5, a + 1, b + 1, d + 1) * jnp.exp(
            jnp.log(safe) * (-1.0 / 3.0)
        )

        @pl.when(is_own(a, b, d))
        def _():
            spot = (a - 1, b - 1, pl.ds(d - 1, 1), slice(None))
            dens_ref[spot] = jnp.where(good, fresh, old_ref[spot])

        return 0

    lax.fori_loop(0, number, density, 0)

    def force(slot, _):
        a, b, d = place(slot)

        @pl.when(is_own(a, b, d))
        def _():
            load_columns(a, b, d)
            inv = row(4, a + 1, b + 1, d + 1)
            inv2 = inv * inv
            own = pt_ref[a, b, pl.ds(d + 1, 1), :] * (inv2 * inv2 * inv)
            cols_ref[4] = jnp.broadcast_to(own, (128, 128)).T
            outs = [[], [], []]
            for half in range(2):
                part = slice(64 * half, 64 * half + 64)

                def near(k, sums):
                    na, nb, nd = a + lax.div(k, 9), b + lax.rem(lax.div(k, 3), 3), d + lax.rem(k, 3)
                    dx = cols_ref[0, part] - row(0, na, nb, nd)
                    dy = cols_ref[1, part] - row(1, na, nb, nd)
                    dz = cols_ref[2, part] - row(2, na, nb, nd)
                    sq = jnp.maximum(dx * dx + dy * dy + dz * dz, 1e-30)
                    dist = sq * lax.rsqrt(sq)
                    near_inv = row(4, na, nb, nd)
                    near_m = row(3, na, nb, nd)
                    near_2 = near_inv * near_inv
                    weight = (
                        near_m
                        * pt_ref[na - 1, nb - 1, pl.ds(nd, 1), :]
                        * (near_2 * near_2 * near_inv)
                    )
                    wi = jnp.maximum(1.0 - dist * cols_ref[3, part], 0.0)
                    wj = jnp.maximum(1.0 - dist * near_inv, 0.0)
                    coef = near_m * (cols_ref[4, part] * (wi * wi * wi)) + weight * (wj * wj * wj)
                    sx, sy, sz = sums
                    return sx + coef * dx, sy + coef * dy, sz + coef * dz

                zero = jnp.zeros((64, 128), jnp.float32)
                sums = lax.fori_loop(0, 27, near, (zero, zero, zero))
                for n in range(3):
                    outs[n].append(sums[n])
            good = row(3, a + 1, b + 1, d + 1) > 0.0
            for n in range(3):
                total_n = lane_sum(jnp.concatenate(outs[n], axis=0)) * (20.0 * KC)
                acc_ref[n, a - 1, b - 1, pl.ds(d - 1, 1), :] = jnp.where(good, total_n, 0.0)

        return 0

    lax.fori_loop(0, number, force, 0)


def per_device(positions, mass, support, counts, entropy, density_old, active):
    size_x, size_y, size_z, slots = mass.shape
    shape = mass.shape
    valid = jnp.arange(slots, dtype=jnp.int32)[None, None, None, :] < counts[..., None]
    m_eff = jnp.where(valid, mass, jnp.float32(0.0))
    act = (active > 0)[..., None]
    term = jnp.where(act, entropy, entropy * density_old ** (-1.0 / 3.0))
    flag = jnp.broadcast_to(act.astype(jnp.float32), shape)
    pack = jnp.concatenate(
        [positions, m_eff[None], (1.0 / support)[None], term[None], flag[None]], axis=0
    )
    extended = padded(pack, (("gz", 3), ("gx", 1), ("gy", 2)), HALO)
    flags = extended[6, 1 : size_x + 3, 1 : size_y + 3, 1 : size_z + 3, 0].astype(jnp.int32)
    total = (size_x + 2) * (size_y + 2) * (size_z + 2)
    import functools

    vmem = pl.BlockSpec(memory_space=pltpu.VMEM)
    return pl.pallas_call(
        functools.partial(kernel, (size_x, size_y, size_z)),
        out_shape=(
            jax.ShapeDtypeStruct(shape, jnp.float32),
            jax.ShapeDtypeStruct((3, *shape), jnp.float32),
        ),
        in_specs=[pl.BlockSpec(memory_space=pltpu.SMEM), vmem, vmem],
        out_specs=(vmem, vmem),
        scratch_shapes=[
            pltpu.SMEM((total + 1,), jnp.int32),
            pltpu.VMEM((5, 128, 128), jnp.float32),
            pltpu.VMEM((size_x + 2, size_y + 2, size_z + 4, slots), jnp.float32),
        ],
        compiler_params=pltpu.CompilerParams(vmem_limit_bytes=48 * 1024 * 1024),
    )(flags.reshape(total), extended, density_old)


def solution(mesh):
    return jax.shard_map(
        per_device,
        mesh=mesh,
        in_specs=(
            P(None, "gx", "gy", "gz", None),
            P("gx", "gy", "gz", None),
            P("gx", "gy", "gz", None),
            P("gx", "gy", "gz"),
            P("gx", "gy", "gz", None),
            P("gx", "gy", "gz", None),
            P("gx", "gy", "gz"),
        ),
        out_specs=(P("gx", "gy", "gz", None), P(None, "gx", "gy", "gz", None)),
        check_vma=False,
    )
```

time: 258 us -> 135 us (0.52)
  the two profiles are of different devices: /device:TPU:83 before, /device:TPU:291 now
where the time goes in v1:
time: 135 us
  Pallas kernels  65.1 us (48%)
  waiting for transfers between devices  32.2 us (24%)
  starting transfers between devices  19.8 us (15%)
  local copies, waits for them, and re-layouts  9.48 us (7%)
  other arithmetic  7.08 us (5%)
    pallas_call x1, Pallas kernels, per_device(): pl.pallas_call(functools.partial(kernel, (size_x, size_y, size_z)), out_s...  65.1 us
    ppermute x3, waiting for transfers between devices, padded(): after = lax.ppermute(initial, axis, down)  18.6 us
    ppermute x3, waiting for transfers between devices, padded(): before = lax.ppermute(last, axis, up)  13.6 us
    ppermute x3, starting transfers between devices, padded(): after = lax.ppermute(initial, axis, down)  10.4 us
    ppermute x3, starting transfers between devices, padded(): before = lax.ppermute(last, axis, up)  9.32 us
    unnamed x12, local copies, waits for them, and re-layouts  5.66 us
    concatenate x1, other arithmetic, padded(): value = jnp.concatenate([before, value, after], axis=dim)  2.75 us
  transfers between devices with their start and end apart: 6, of which 6 were waited for; matrix products, arithmetic and copies ran while one was open for 1% of the time, Pallas kernels for 0%

profile of v1, /device:TPU:291, one launch (start us, length us, event | category | flops | bytes accessed | tf_op | source)
XLA Modules:
  0.0 134.5 jit_solution(8810452392602568553)
XLA Ops:
  0.7 0.8 fusion.3
  1.5 0.2 copy.16
  1.7 0.1 copy.17
  1.8 0.9 copy.15
  2.7 1.2 constant_dynamic-update-slice_fusion
  3.9 0.1 bitcast_dynamic-update-slice_fusion.1
  4.1 0.4 fusion.2
  4.6 0.4 fusion.4
  5.1 3.1 %collective-permute-start = (f32[7,12,6,2,128]{4,3,2,1,0:T(2,128)S(1)}, f32[7,12,6,2,128]{4,3,2,1,0:T(2,128)S(1)}, u32[]{:S(2)}, u32[]{:S(2)}) collective-permute-start(f32[7,12,6,2,128]{4,3,2,1,0:T(2,128)S(1)} %get-tuple-element.8), channel_id=1, source_target_pairs={{0,1},{1,2},{2,3},{3,4},{4,5},{5,6},{6,7},{8,9},{9,10},{10,11},{11... | collective-permute-start | bytes 1548296 | tf_op jit(solution)/shard_map/ppermute | solution.py:21
  8.2 3.4 %collective-permute-start.1 = (f32[7,12,6,2,128]{4,3,2,1,0:T(2,128)S(1)}, f32[7,12,6,2,128]{4,3,2,1,0:T(2,128)S(1)}, u32[]{:S(2)}, u32[]{:S(2)}) collective-permute-start(f32[7,12,6,2,128]{4,3,2,1,0:T(2,128)S(1)} %get-tuple-element.9), channel_id=1, source_target_pairs={{1,0},{2,1},{3,2},{4,3},{5,4},{6,5},{7,6},{9,8},{10,9},{11,10},{12... | collective-permute-start | bytes 1548296 | tf_op jit(solution)/shard_map/ppermute | solution.py:22
  11.6 9.2 %collective-permute-done = f32[7,12,6,2,128]{4,3,2,1,0:T(2,128)S(1)} collective-permute-done((f32[7,12,6,2,128]{4,3,2,1,0:T(2,128)S(1)}, f32[7,12,6,2,128]{4,3,2,1,0:T(2,128)S(1)}, u32[]{:S(2)}, u32[]{:S(2)}) %collective-permute-start) | collective-permute-done | bytes 516128 | tf_op jit(solution)/shard_map/ppermute | solution.py:21
  20.8 1.6 %collective-permute-done.1 = f32[7,12,6,2,128]{4,3,2,1,0:T(2,128)S(1)} collective-permute-done((f32[7,12,6,2,128]{4,3,2,1,0:T(2,128)S(1)}, f32[7,12,6,2,128]{4,3,2,1,0:T(2,128)S(1)}, u32[]{:S(2)}, u32[]{:S(2)}) %collective-permute-start.1) | collective-permute-done | bytes 516128 | tf_op jit(solution)/shard_map/ppermute | solution.py:22
  22.4 0.3 pad_maximum_fusion.8
  22.6 0.3 copy.19
  23.0 2.1 %collective-permute-start.3 = (f32[7,2,6,10,128]{4,1,3,2,0:T(2,128)S(1)}, f32[7,2,6,10,128]{4,1,3,2,0:T(2,128)S(1)}, u32[]{:S(2)}, u32[]{:S(2)}) collective-permute-start(f32[7,2,6,10,128]{4,1,3,2,0:T(2,128)S(1)} %copy.19), channel_id=1, source_target_pairs={{64,0},{128,64},{192,128},{256,192},{320,256},{384,320},{448,384},... | collective-permute-start | bytes 1290248 | tf_op jit(solution)/shard_map/ppermute | solution.py:22
  25.1 0.3 copy.18
  25.4 3.2 %collective-permute-start.2 = (f32[7,2,6,10,128]{4,1,3,2,0:T(2,128)S(1)}, f32[7,2,6,10,128]{4,1,3,2,0:T(2,128)S(1)}, u32[]{:S(2)}, u32[]{:S(2)}) collective-permute-start(f32[7,2,6,10,128]{4,1,3,2,0:T(2,128)S(1)} %copy.18), channel_id=1, source_target_pairs={{0,64},{64,128},{128,192},{192,256},{256,320},{320,384},{384,448},... | collective-permute-start | bytes 1290248 | tf_op jit(solution)/shard_map/ppermute | solution.py:21
  28.6 5.8 %collective-permute-done.3 = f32[7,2,6,10,128]{4,1,3,2,0:T(2,128)S(1)} collective-permute-done((f32[7,2,6,10,128]{4,1,3,2,0:T(2,128)S(1)}, f32[7,2,6,10,128]{4,1,3,2,0:T(2,128)S(1)}, u32[]{:S(2)}, u32[]{:S(2)}) %collective-permute-start.3) | collective-permute-done | bytes 430112 | tf_op jit(solution)/shard_map/ppermute | solution.py:22
  34.5 3.3 %collective-permute-done.2 = f32[7,2,6,10,128]{4,1,3,2,0:T(2,128)S(1)} collective-permute-done((f32[7,2,6,10,128]{4,1,3,2,0:T(2,128)S(1)}, f32[7,2,6,10,128]{4,1,3,2,0:T(2,128)S(1)}, u32[]{:S(2)}, u32[]{:S(2)}) %collective-permute-start.2) | collective-permute-done | bytes 430112 | tf_op jit(solution)/shard_map/ppermute | solution.py:21
  37.9 0.7 pad_maximum_fusion.5
  38.6 0.7 copy.23
  39.2 5.0 %collective-permute-start.5 = (f32[7,16,2,10,128]{4,1,3,2,0:T(8,128)S(1)}, f32[7,16,2,10,128]{4,1,3,2,0:T(8,128)S(1)}, u32[]{:S(2)}, u32[]{:S(2)}) collective-permute-start(f32[7,16,2,10,128]{4,1,3,2,0:T(8,128)S(1)} %copy.23), channel_id=1, source_target_pairs={{8,0},{16,8},{24,16},{32,24},{40,32},{48,40},{56,48},{9,1},{17,9},... | collective-permute-start | bytes 3440648 | tf_op jit(solution)/shard_map/ppermute | solution.py:22
  44.2 0.7 copy.22
  44.9 3.0 %collective-permute-start.4 = (f32[7,16,2,10,128]{4,1,3,2,0:T(8,128)S(1)}, f32[7,16,2,10,128]{4,1,3,2,0:T(8,128)S(1)}, u32[]{:S(2)}, u32[]{:S(2)}) collective-permute-start(f32[7,16,2,10,128]{4,1,3,2,0:T(8,128)S(1)} %copy.22), channel_id=1, source_target_pairs={{0,8},{8,16},{16,24},{24,32},{32,40},{40,48},{48,56},{1,9},{9,17},... | collective-permute-start | bytes 3440648 | tf_op jit(solution)/shard_map/ppermute | solution.py:21
  47.9 11.2 %collective-permute-done.5 = f32[7,16,2,10,128]{4,1,3,2,0:T(8,128)S(1)} collective-permute-done((f32[7,16,2,10,128]{4,1,3,2,0:T(8,128)S(1)}, f32[7,16,2,10,128]{4,1,3,2,0:T(8,128)S(1)}, u32[]{:S(2)}, u32[]{:S(2)}) %collective-permute-start.5) | collective-permute-done | bytes 1146912 | tf_op jit(solution)/shard_map/ppermute | solution.py:22
  59.1 0.4 copy.25
  59.5 1.2 collective-permute-done.4
  60.7 0.4 copy.24
  61.1 2.8 %pad_maximum_fusion.ext_ref = f32[7,16,10,10,128]{4,3,2,1,0:T(8,128)S(1)} fusion(f32[7,16,2,10,128]{4,3,2,1,0:T(8,128)S(1)} %copy.25, f32[7,2,6,10,128]{4,3,2,1,0:T(8,128)S(1)} %copy.21, f32[7,12,6,2,128]{4,3,2,1,0:T(2,128)S(1)} %collective-permute-done.1, f32[7,12,6,6,128]{4,3,2,1,0:T(8,128)S(1)} %broadcast_dynamic-update-slice_fusion, ...), kind=kLoop, calls=%fused_computation | loop fusion | flops 8601600 | bytes 11468800 | tf_op jit(solution)/shard_map/concatenate | solution.py:23
  63.8 3.5 %copy-done.1 = f32[7,16,10,10,128]{4,3,2,1,0:T(8,128)} copy-done((f32[7,16,10,10,128]{4,3,2,1,0:T(8,128)}, f32[7,16,10,10,128]{4,3,2,1,0:T(8,128)S(1)}, u32[]{:S(2)}) %copy-start.1) | copy-done | bytes 5734424
  67.4 2.0 %fusion = s32[14,8,8]{2,1,0:T(8,128)S(1)} fusion(f32[7,16,10,10,128]{4,3,2,1,0:T(8,128)S(1)} %pad_maximum_fusion.ext_ref), kind=kLoop, calls=%fused_computation.10 | loop fusion | flops 896 | bytes 7168 | tf_op jit(solution)/shard_map/convert_element_type | solution.py:162
  69.4 65.1 %shard_map.86 = (f32[12,6,6,128]{3,2,1,0:T(8,128)}, f32[3,12,6,6,128]{4,3,2,1,0:T(8,128)}) custom-call(s32[896]{0:T(1024)S(1)} %convert_element_type.13.flags_ref, f32[7,16,10,10,128]{4,3,2,1,0:T(8,128)} %copy-done.1, f32[12,6,6,128]{3,2,1,0:T(8,128)S(1)} %copy-done), custom_call_target="tpu_custom_call" | custom-call | tf_op jit(solution)/shard_map/pallas_call | solution.py:167
  (14 shorter events, 0.4 us)
Async XLA Ops:
  0.6 3.3 %copy-start.3 = (f32[12,6,6,128]{3,2,1,0:T(8,128)S(1)}, f32[12,6,6,128]{3,2,1,0:T(8,128)}, u32[]{:S(2)}) copy-start(f32[12,6,6,128]{3,2,1,0:T(8,128)} %param.8) | copy-start | bytes 663556
  0.6 3.4 %copy-start.4 = (f32[12,6,6,128]{3,2,1,0:T(8,128)S(1)}, f32[12,6,6,128]{3,2,1,0:T(8,128)}, u32[]{:S(2)}) copy-start(f32[12,6,6,128]{3,2,1,0:T(8,128)} %param.9) | copy-start | bytes 663556
  0.7 3.5 %copy-start = (f32[12,6,6,128]{3,2,1,0:T(8,128)S(1)}, f32[12,6,6,128]{3,2,1,0:T(8,128)}, u32[]{:S(2)}) copy-start(f32[12,6,6,128]{3,2,1,0:T(8,128)} %old_ref.1) | copy-start | bytes 663556
  0.7 3.5 %copy-start.2 = (f32[12,6,6,128]{3,2,1,0:T(8,128)S(1)}, f32[12,6,6,128]{3,2,1,0:T(8,128)}, u32[]{:S(2)}) copy-start(f32[12,6,6,128]{3,2,1,0:T(8,128)} %param.11) | copy-start | bytes 663556
  5.1 15.7 %collective-permute-start = (f32[7,12,6,2,128]{4,3,2,1,0:T(2,128)S(1)}, f32[7,12,6,2,128]{4,3,2,1,0:T(2,128)S(1)}, u32[]{:S(2)}, u32[]{:S(2)}) collective-permute-start(f32[7,12,6,2,128]{4,3,2,1,0:T(2,128)S(1)} %get-tuple-element.8), channel_id=1, source_target_pairs={{0,1},{1,2},{2,3},{3,4},{4,5},{5,6},{6,7},{8,9},{9,10},{10,11},{11... | collective-permute-start | bytes 1548296 | tf_op jit(solution)/shard_map/ppermute | solution.py:21
  8.2 14.2 %collective-permute-start.1 = (f32[7,12,6,2,128]{4,3,2,1,0:T(2,128)S(1)}, f32[7,12,6,2,128]{4,3,2,1,0:T(2,128)S(1)}, u32[]{:S(2)}, u32[]{:S(2)}) collective-permute-start(f32[7,12,6,2,128]{4,3,2,1,0:T(2,128)S(1)} %get-tuple-element.9), channel_id=1, source_target_pairs={{1,0},{2,1},{3,2},{4,3},{5,4},{6,5},{7,6},{9,8},{10,9},{11,10},{12... | collective-permute-start | bytes 1548296 | tf_op jit(solution)/shard_map/ppermute | solution.py:22
  23.0 11.4 %collective-permute-start.3 = (f32[7,2,6,10,128]{4,1,3,2,0:T(2,128)S(1)}, f32[7,2,6,10,128]{4,1,3,2,0:T(2,128)S(1)}, u32[]{:S(2)}, u32[]{:S(2)}) collective-permute-start(f32[7,2,6,10,128]{4,1,3,2,0:T(2,128)S(1)} %copy.19), channel_id=1, source_target_pairs={{64,0},{128,64},{192,128},{256,192},{320,256},{384,320},{448,384},... | collective-permute-start | bytes 1290248 | tf_op jit(solution)/shard_map/ppermute | solution.py:22
  25.4 12.4 %collective-permute-start.2 = (f32[7,2,6,10,128]{4,1,3,2,0:T(2,128)S(1)}, f32[7,2,6,10,128]{4,1,3,2,0:T(2,128)S(1)}, u32[]{:S(2)}, u32[]{:S(2)}) collective-permute-start(f32[7,2,6,10,128]{4,1,3,2,0:T(2,128)S(1)} %copy.18), channel_id=1, source_target_pairs={{0,64},{64,128},{128,192},{192,256},{256,320},{320,384},{384,448},... | collective-permute-start | bytes 1290248 | tf_op jit(solution)/shard_map/ppermute | solution.py:21
  39.2 19.9 %collective-permute-start.5 = (f32[7,16,2,10,128]{4,1,3,2,0:T(8,128)S(1)}, f32[7,16,2,10,128]{4,1,3,2,0:T(8,128)S(1)}, u32[]{:S(2)}, u32[]{:S(2)}) collective-permute-start(f32[7,16,2,10,128]{4,1,3,2,0:T(8,128)S(1)} %copy.23), channel_id=1, source_target_pairs={{8,0},{16,8},{24,16},{32,24},{40,32},{48,40},{56,48},{9,1},{17,9},... | collective-permute-start | bytes 3440648 | tf_op jit(solution)/shard_map/ppermute | solution.py:22
  44.9 15.8 %collective-permute-start.4 = (f32[7,16,2,10,128]{4,1,3,2,0:T(8,128)S(1)}, f32[7,16,2,10,128]{4,1,3,2,0:T(8,128)S(1)}, u32[]{:S(2)}, u32[]{:S(2)}) collective-permute-start(f32[7,16,2,10,128]{4,1,3,2,0:T(8,128)S(1)} %copy.22), channel_id=1, source_target_pairs={{0,8},{8,16},{16,24},{24,32},{32,40},{40,48},{48,56},{1,9},{9,17},... | collective-permute-start | bytes 3440648 | tf_op jit(solution)/shard_map/ppermute | solution.py:21
  63.8 3.5 %copy-start.1 = (f32[7,16,10,10,128]{4,3,2,1,0:T(8,128)}, f32[7,16,10,10,128]{4,3,2,1,0:T(8,128)S(1)}, u32[]{:S(2)}) copy-start(f32[7,16,10,10,128]{4,3,2,1,0:T(8,128)S(1)} %pad_maximum_fusion.ext_ref) | copy-start | bytes 17203204

commit v2 on v0

v2 whole, which is shorter than its diff:
```python
import functools
import math

import jax
import jax.numpy as jnp
from jax import lax
from jax.experimental import pallas as pl
from jax.experimental.pallas import tpu as pltpu
from jax.sharding import PartitionSpec as P

KC = 21.0 / (2.0 * math.pi)
SX, SY, SZ, S = 12, 6, 6, 128
MOST = 9
CELLS = SX * SY * SZ

ZERO = CELLS * 8
OWN_TAIL = ZERO + 8
OWN_ROWS = OWN_TAIL + 8

Z_TWO, Z_FAR, Z_TAIL, Z_ROWS = 288, 432, 720, 728
X_TWO, X_FAR, X_TAIL, X_ROWS = 240, 336, 576, 584
Y_TWO, Y_SUM, Y_TAIL, Y_ROWS = 640, 864, 976, 992

ZLO = OWN_ROWS
ZHI = ZLO + Z_ROWS
XLO = ZHI + Z_ROWS
XHI = XLO + X_ROWS
SLAB = XHI + X_ROWS

SLAB_MOST = 96
ALL_MOST = 256

VMEM = pl.BlockSpec(memory_space=pltpu.VMEM)
SMEM = pl.BlockSpec(memory_space=pltpu.SMEM)
GROUPS = 2
NEAR = 3
PARAMS = pltpu.CompilerParams(vmem_limit_bytes=40 * 1024 * 1024)

BLOCKS = [(0, 0), (0, -1), (0, 1), (-1, 0), (-1, -1), (-1, 1), (1, 0), (1, -1), (1, 1)]


def step(mode, i, near, sums):
    xi, yi, zi, hi, bi = i
    xj, yj, zj, mj, hj, wj = near
    dx, dy, dz = xi - xj, yi - yj, zi - zj
    sq = jnp.maximum(dx * dx + dy * dy + dz * dz, 1e-30)
    dist = sq * lax.rsqrt(sq)
    out = []
    if mode != "near":
        wi = jnp.maximum(hi - dist, 0.0)
        own = mj * (wi * wi * wi)
        out.append(sums[0] + own * (wi * (bi - wi)))
        if mode == "all":
            out += [sums[1] + own * dx, sums[2] + own * dy, sums[3] + own * dz]
    if mode != "density":
        wj_ = jnp.maximum(hj - dist, 0.0)
        other = wj * (wj_ * wj_ * wj_)
        last = sums[-3:]
        out += [last[0] + other * dx, last[1] + other * dy, last[2] + other * dz]
    return tuple(out)


WIDTH = {"all": 7, "density": 1, "near": 3}
FIRST = {"all": 0, "density": 0, "near": 4}


def pairs(mode, src, four, two, use, count, tile, cols, table):
    for u in range(NEAR - 1):
        four[count + u] = jnp.int32(0)
        two[count + u] = jnp.int32(0)
        use[count + u] = jnp.float32(0.0)
    steps = lax.div(count + (NEAR - 1), NEAR)
    used = jnp.sum(jnp.where(tile[3:4] > 0.0, 1.0, 0.0)).astype(jnp.int32)
    cols[:, 0:8] = tile.T
    width = WIDTH[mode]
    lane = lax.broadcasted_iota(jnp.int32, (8, 128), 1)
    zero = jnp.zeros((8, 128), jnp.float32)

    def group(g, _):
        spots, own = [], []
        for v in range(GROUPS):
            spot = pl.ds(pl.multiple_of((g * GROUPS + v) * 8, 8), 8)
            block = cols[spot, :]
            x, y, z, h = [
                jnp.broadcast_to(block[:, c : c + 1], (8, 128)) for c in (0, 1, 2, 4)
            ]
            spots.append(spot)
            own.append((x, y, z, h, 1.25 * h))

        def body(q, sums):
            sums = list(sums)
            for u in range(NEAR):
                at = q * NEAR + u
                f = four[at]
                near = [
                    jnp.broadcast_to(src[pl.ds(f + c, 1), :], (8, 128)) for c in range(4)
                ]
                flag = use[at]
                if mode != "near":
                    near[3] = near[3] * jnp.where(flag >= 0.5, 1.0, 0.0)
                if mode != "density":
                    t = two[at]
                    near.append(jnp.broadcast_to(src[pl.ds(t, 1), :], (8, 128)))
                    weight = jnp.broadcast_to(src[pl.ds(t + 1, 1), :], (8, 128))
                    near.append(weight * jnp.where(flag == 1.0, 1.0, 0.0))
                else:
                    near += [None, None]
                for v in range(GROUPS):
                    sums[v] = step(mode, own[v], near, sums[v])
            return tuple(sums)

        sums = lax.fori_loop(0, steps, body, ((zero,) * width,) * GROUPS)
        for v in range(GROUPS):
            line = zero
            for c in range(width):
                total = jnp.sum(sums[v][c], axis=1, keepdims=True)
                line = jnp.where(lane == FIRST[mode] + c, total, line)
            table[spots[v], :] = line
        return 0

    lax.fori_loop(0, lax.div(used + (8 * GROUPS - 1), 8 * GROUPS), group, 0)
    return table[...].T[0:8]


def corner(k):
    return lax.div(k, SY * SZ), lax.rem(lax.div(k, SZ), SY), lax.rem(k, SZ)


def pack(counts, active, pos, mass, support, entropy, old, own, up, down, ids):
    def scan(q, n):
        y, z = lax.div(q, SZ), lax.rem(q, SZ)
        for x in range(SX):
            ids[n] = (x * SY + y) * SZ + z
            n = n + active[y, z, x]
        return n

    number = lax.fori_loop(0, SY * SZ, scan, jnp.int32(0))
    for s in range(MOST, 15):
        ids[s] = jnp.int32(0)
    ids[15] = number
    lane = lax.broadcasted_iota(jnp.int32, (8, 128), 1)
    tail = jnp.zeros((8, 128), jnp.int32)
    for s in range(MOST):
        tail = jnp.where(lane == s, ids[s], tail)
    tail = jnp.where(lane == 15, number, tail).astype(jnp.float32)
    own[ZERO : ZERO + 8] = jnp.zeros((8, 128), jnp.float32)
    own[OWN_TAIL : OWN_TAIL + 8] = tail
    up[Z_TAIL : Z_TAIL + 8] = tail
    down[Z_TAIL : Z_TAIL + 8] = tail
    sub = lax.broadcasted_iota(jnp.int32, (SZ, 128), 0)
    slot = lax.broadcasted_iota(jnp.int32, (SZ, 128), 1)

    def cells(x2, _):
        for u in range(2):
            x = x2 * 2 + u
            for y in range(SY):
                many = jnp.zeros((SZ, 128), jnp.int32)
                act = jnp.zeros((SZ, 128), jnp.int32)
                for z in range(SZ):
                    many = jnp.where(sub == z, counts[y, z, x], many)
                    act = jnp.where(sub == z, active[y, z, x], act)
                h = support[x, y]
                inv = 1.0 / h
                inv2 = inv * inv
                inv4 = inv2 * inv2
                m = jnp.where(slot < many, mass[x, y], 0.0)
                gain = entropy[x, y] * (inv4 * inv4)
                power = jnp.exp(jnp.log(old[x, y]) * (-1.0 / 3.0))
                weight = m * gain * jnp.where(act > 0, 1.0, power)
                base = pl.multiple_of(x2 * (2 * SY * SZ * 8), 8) + (u * SY + y) * SZ * 8
                for c, value in enumerate(
                    (pos[0, x, y], pos[1, x, y], pos[2, x, y], m, h, weight, gain)
                ):
                    own[pl.ds(base + c, SZ, stride=8), :] = value
                four = pl.multiple_of(x2 * (2 * SY * 4), 8) + (u * SY + y) * 4
                two = pl.multiple_of(x2 * (2 * SY * 2), 8) + (u * SY + y) * 2
                for out, z1, z2 in ((up, SZ - 1, SZ - 2), (down, 0, 1)):
                    out[pl.ds(four, 4), :] = own[pl.ds(base + z1 * 8, 4), :]
                    out[pl.ds(two + Z_TWO, 2), :] = own[pl.ds(base + z1 * 8 + 4, 2), :]
                    out[pl.ds(four + Z_FAR, 4), :] = own[pl.ds(base + z2 * 8, 4), :]
        return 0

    lax.fori_loop(0, SX // 2, cells, 0)


def own_row(x, y, z):
    return ((x * SY + y) * SZ + z) * 8


def local(part, ids, own, before, sums, four, two, use, flags, cols, table):
    number = ids[15]
    half = lax.div(number + 1, 2)

    def clear(k, _):
        flags[k] = jnp.int32(0)
        return 0

    lax.fori_loop(0, CELLS, clear, 0, unroll=16)

    def mark(s, _):
        flags[ids[s]] = jnp.int32(1)
        return 0

    lax.fori_loop(0, number, mark, 0)
    if before is not None:
        sums[...] = before[...]

    def slot(s, _):
        k = ids[s]
        a, b, d = corner(k)
        count = jnp.int32(0)
        for ea in (-1, 0, 1):
            for eb in (-1, 0, 1):
                for ed in (-1, 0, 1):
                    na, nb, nd = a + ea, b + eb, d + ed
                    inside = (
                        (na >= 0) & (na < SX) & (nb >= 0) & (nb < SY) & (nd >= 0) & (nd < SZ)
                    )
                    cell = k + (ea * SY + eb) * SZ + ed
                    four[count] = cell * 8
                    two[count] = cell * 8 + 4
                    known = flags[jnp.where(inside, cell, 0)]
                    use[count] = jnp.where(known > 0, jnp.float32(0.5), jnp.float32(1.0))
                    count = count + inside.astype(jnp.int32)
        row = pl.multiple_of(k * 8, 8)
        tile = own[pl.ds(row, 8), :]
        sums[s] = pairs("all", own, four, two, use, count, tile, cols, table)
        return 0

    if part == 0:
        lax.fori_loop(0, half, slot, 0)
    else:
        lax.fori_loop(half, number, slot, 0)


def local_first(ids, own, sums, *scratch):
    local(0, ids, own, None, sums, *scratch)


def local_second(ids, own, before, _, sums, *scratch):
    local(1, ids, own, before, sums, *scratch)


def pack_x(own, zlo, zhi, up, down):
    for out, x1, x2 in ((up, SX - 1, SX - 2), (down, 0, 1)):
        for y in range(SY):
            for z in range(-2, SZ + 2):
                for x, base in ((x1, 0), (x2, X_FAR)):
                    spot = base + (y * (SZ + 4) + z + 2) * 4
                    if 0 <= z < SZ:
                        row = own_row(x, y, z)
                        out[spot : spot + 4] = own[row : row + 4]
                    else:
                        src = zlo if z < 0 else zhi
                        far = Z_FAR if z in (-2, SZ + 1) else 0
                        row = far + (x * SY + y) * 4
                        out[spot : spot + 4] = src[row : row + 4]
                if -1 <= z <= SZ:
                    spot = X_TWO + (y * (SZ + 2) + z + 1) * 2
                    if 0 <= z < SZ:
                        row = own_row(x1, y, z) + 4
                        out[spot : spot + 2] = own[row : row + 2]
                    else:
                        src = zlo if z < 0 else zhi
                        row = Z_TWO + (x1 * SY + y) * 2
                        out[spot : spot + 2] = src[row : row + 2]
        out[X_TAIL : X_TAIL + 8] = jnp.zeros((8, 128), jnp.float32)
        out[X_TAIL : X_TAIL + 1] = own[OWN_TAIL : OWN_TAIL + 1]
        out[X_TAIL + 1 : X_TAIL + 2] = zlo[Z_TAIL : Z_TAIL + 1]
        out[X_TAIL + 2 : X_TAIL + 3] = zhi[Z_TAIL : Z_TAIL + 1]


def slab_rows(x, y, z):
    k = x * SY + y
    four = own_row(x, y, z)
    two = four + 4
    zbase = jnp.where(z < 0, ZLO, ZHI)
    zfar = (z == -2) | (z == SZ + 1)
    zout = (z < 0) | (z >= SZ)
    four = jnp.where(zout, zbase + jnp.where(zfar, Z_FAR, 0) + k * 4, four)
    two = jnp.where(zout, zbase + Z_TWO + k * 2, two)
    xbase = jnp.where(x < 0, XLO, XHI)
    xfar = (x == -2) | (x == SX + 1)
    xout = (x < 0) | (x >= SX)
    four = jnp.where(xout, xbase + jnp.where(xfar, X_FAR, 0) + (y * (SZ + 4) + z + 2) * 4, four)
    two = jnp.where(xout, xbase + X_TWO + (y * (SZ + 2) + z + 1) * 2, two)
    return four, two


def slab_rows_at(x, y, z):
    if 0 <= x < SX and 0 <= z < SZ:
        return own_row(x, y, z), own_row(x, y, z) + 4
    if 0 <= x < SX:
        base, far, k = ZLO if z < 0 else ZHI, z in (-2, SZ + 1), x * SY + y
        return base + (Z_FAR if far else 0) + k * 4, base + Z_TWO + k * 2
    base, far = XLO if x < 0 else XHI, x in (-2, SX + 1)
    four = base + (X_FAR if far else 0) + (y * (SZ + 4) + z + 2) * 4
    return four, base + X_TWO + (y * (SZ + 2) + z + 1) * 2


def slab(
    ids, own, zlo, zhi, xlo, xhi, before, up, down, tiles, sums, places,
    rows, tails, lists, sem, four, two, use, flags, cols, table,
):
    rows[0:OWN_ROWS] = own[...]
    rows[ZLO:ZHI] = zlo[...]
    rows[ZHI:XLO] = zhi[...]
    rows[XLO:XHI] = xlo[...]
    rows[XHI:SLAB] = xhi[...]
    tails[...] = jnp.zeros(tails.shape, jnp.int32)
    tails[0:1] = own[OWN_TAIL : OWN_TAIL + 1].astype(jnp.int32)
    tails[1:2] = zlo[Z_TAIL : Z_TAIL + 1].astype(jnp.int32)
    tails[2:3] = zhi[Z_TAIL : Z_TAIL + 1].astype(jnp.int32)
    tails[3:6] = xlo[X_TAIL : X_TAIL + 3].astype(jnp.int32)
    tails[6:9] = xhi[X_TAIL : X_TAIL + 3].astype(jnp.int32)
    copy = pltpu.make_async_copy(tails, lists, sem)
    copy.start()

    def clear(k, _):
        flags[k] = jnp.int32(0)
        return 0

    lax.fori_loop(0, (SX + 2) * SY * (SZ + 2), clear, 0, unroll=16)
    for out, y in ((up, SY - 1), (down, 0)):
        for x in range(-2, SX + 2):
            for z in range(-2, SZ + 2):
                row4, row2 = slab_rows_at(x, y, z)
                spot = ((x + 2) * (SZ + 4) + z + 2) * 4
                out[spot : spot + 4] = rows[row4 : row4 + 4]
                if -1 <= x <= SX and -1 <= z <= SZ:
                    spot = Y_TWO + ((x + 1) * (SZ + 2) + z + 1) * 2
                    out[spot : spot + 2] = rows[row2 : row2 + 2]
        out[Y_SUM:Y_TAIL] = jnp.zeros((Y_TAIL - Y_SUM, 128), jnp.float32)
        out[Y_TAIL:Y_ROWS] = jnp.zeros((Y_ROWS - Y_TAIL, 128), jnp.float32)
        out[Y_TAIL : Y_TAIL + 1] = own[OWN_TAIL : OWN_TAIL + 1]
        out[Y_TAIL + 1 : Y_TAIL + 2] = zlo[Z_TAIL : Z_TAIL + 1]
        out[Y_TAIL + 2 : Y_TAIL + 3] = zhi[Z_TAIL : Z_TAIL + 1]
        out[Y_TAIL + 3 : Y_TAIL + 6] = xlo[X_TAIL : X_TAIL + 3]
        out[Y_TAIL + 6 : Y_TAIL + 9] = xhi[X_TAIL : X_TAIL + 3]
    copy.wait()

    def flag_at(x, y, z):
        return ((x + 1) * SY + y) * (SZ + 2) + z + 1

    number = jnp.int32(0)
    for q, (bx, bz) in enumerate(BLOCKS):

        def one(s, n, q=q, bx=bx, bz=bz):
            a, b, d = corner(lists[q, s])
            x, z = a + bx * SX, d + bz * SZ
            inside = (x >= -1) & (x <= SX) & (z >= -1) & (z <= SZ)
            places[0, n] = x
            places[1, n] = b
            places[2, n] = z

            @pl.when(inside)
            def _():
                flags[flag_at(x, b, z)] = jnp.int32(1)

            return n + inside.astype(jnp.int32)

        number = lax.fori_loop(0, lists[q, 15], one, number)
    places[3, 0] = number
    places[3, 1] = lists[0, 15]
    mine = lists[0, 15]

    def slot(s, _):
        x, y, z = places[0, s], places[1, s], places[2, s]
        row4, row2 = slab_rows(x, y, z)
        first = rows[pl.ds(row4, 4), :]
        second = rows[pl.ds(row2, 2), :]
        tile = jnp.concatenate([first, second, jnp.zeros((2, 128), jnp.float32)], axis=0)
        is_mine = s < mine
        count = jnp.int32(0)
        for ea in (-1, 0, 1):
            for eb in (-1, 0, 1):
                for ed in (-1, 0, 1):
                    na, nb, nd = x + ea, y + eb, z + ed
                    n4, n2 = slab_rows(na, nb, nd)
                    outer = (na < 0) | (na >= SX) | (nd < 0) | (nd >= SZ)
                    wanted = (nb >= 0) & (nb < SY) & (outer | jnp.logical_not(is_mine))
                    four[count] = n4
                    two[count] = n2
                    seen = wanted & is_mine
                    known = flags[jnp.where(seen, flag_at(na, nb, nd), 0)]
                    use[count] = jnp.where(known > 0, jnp.float32(0.5), jnp.float32(1.0))
                    count = count + wanted.astype(jnp.int32)

        @pl.when(is_mine)
        def _():
            sums[s] = before[s]

            @pl.when(count > 0)
            def _():
                sums[s] = sums[s] + pairs("all", rows, four, two, use, count, tile, cols, table)

            tiles[s] = tile
            tiles[s, 6:7] = sums[s, 0:1]
            sums[s, 7:8] = rows[pl.ds(row4 + 6, 1), :]

        @pl.when(jnp.logical_not(is_mine))
        def _():
            result = pairs("density", rows, four, two, use, count, tile, cols, table)
            tiles[s] = tile
            tiles[s, 6:7] = result[0:1]

        spot = Y_SUM + (x + 1) * (SZ + 2) + z + 1

        @pl.when(y == 0)
        def _():
            down[pl.ds(spot, 1), :] = tiles[s, 6:7]

        @pl.when(y == SY - 1)
        def _():
            up[pl.ds(spot, 1), :] = tiles[s, 6:7]

        return 0

    lax.fori_loop(0, number, slot, 0)


def finish(
    places, ylo, yhi, up, down, tiles, sums, old, density, accel,
    rows, cells, final, spots, tails, lists, sem, four, two, use, flags, cols, table,
):
    rows[0:Y_ROWS] = ylo[...]
    rows[Y_ROWS : 2 * Y_ROWS] = yhi[...]
    rows[2 * Y_ROWS : 3 * Y_ROWS] = down[...]
    rows[3 * Y_ROWS : 4 * Y_ROWS] = up[...]
    tails[0:16] = ylo[Y_TAIL:Y_ROWS].astype(jnp.int32)
    tails[16:32] = yhi[Y_TAIL:Y_ROWS].astype(jnp.int32)
    copy = pltpu.make_async_copy(tails, lists, sem)
    copy.start()
    density[...] = old[...]
    accel[...] = jnp.zeros(accel.shape, jnp.float32)
    wide = (SX + 2) * (SZ + 2)

    def clear(k, _):
        flags[k] = jnp.int32(0)
        return 0

    lax.fori_loop(0, 2 * wide, clear, 0, unroll=16)
    number, mine = places[3, 0], places[3, 1]

    def take(s, _):
        for c in range(3):
            spots[c, s] = places[c, s]
        cells[pl.ds(pl.multiple_of(s * 8, 8), 8), :] = tiles[s]

        @pl.when(s < mine)
        def _():
            final[s] = sums[s]

        return 0

    lax.fori_loop(0, number, take, 0)
    copy.wait()
    total = number
    for side in range(2):
        for q, (bx, bz) in enumerate(BLOCKS):
            row = side * 16 + q

            def one(s, n, row=row, side=side, bx=bx, bz=bz):
                a, b, d = corner(lists[row, s])
                x, z = a + bx * SX, d + bz * SZ
                edge = (SY - 1) if side == 0 else 0
                inside = (x >= -1) & (x <= SX) & (z >= -1) & (z <= SZ) & (b == edge)

                @pl.when(inside)
                def _():
                    spots[0, n] = x
                    spots[1, n] = jnp.int32(-1 if side == 0 else SY)
                    spots[2, n] = z
                    at = (x + 1) * (SZ + 2) + z + 1
                    flags[side * wide + at] = jnp.int32(1)
                    base = side * Y_ROWS
                    spot = pl.multiple_of(n * 8, 8)
                    row4 = base + ((x + 2) * (SZ + 4) + z + 2) * 4
                    row2 = base + Y_TWO + at * 2
                    cells[pl.ds(spot, 8), :] = jnp.concatenate(
                        [
                            rows[pl.ds(row4, 4), :],
                            rows[pl.ds(row2, 2), :],
                            rows[pl.ds(base + Y_SUM + at, 1), :],
                            jnp.zeros((1, 128), jnp.float32),
                        ],
                        axis=0,
                    )

                return n + inside.astype(jnp.int32)

            total = lax.fori_loop(0, lists[row, 15], one, total)

    def across(s, _):
        x, y, z = spots[0, s], spots[1, s], spots[2, s]
        is_mine = s < mine
        low = (y == 0) | (y == -1)
        high = (y == SY - 1) | (y == SY)
        outer = (y == -1) | (y == SY)
        base = jnp.where(outer, 2 * Y_ROWS, 0) + jnp.where(high, Y_ROWS, 0)
        side = jnp.where(high, wide, 0)

        @pl.when(low | high)
        def _():
            for e, (ea, ed) in enumerate((p, q) for p in (-1, 0, 1) for q in (-1, 0, 1)):
                na, nd = x + ea, z + ed
                at = (na + 1) * (SZ + 2) + nd + 1
                four[e] = base + ((na + 2) * (SZ + 4) + nd + 2) * 4
                two[e] = base + Y_TWO + at * 2
                known = flags[jnp.where(is_mine, side + at, 0)]
                use[e] = jnp.where(known > 0, jnp.float32(0.5), jnp.float32(1.0))
            spot = pl.multiple_of(s * 8, 8)
            tile = cells[pl.ds(spot, 8), :]
            count = jnp.int32(9)

            @pl.when(is_mine)
            def _():
                result = pairs("all", rows, four, two, use, count, tile, cols, table)
                final[s, 0:7] = final[s, 0:7] + result[0:7]
                cells[pl.ds(spot + 6, 1), :] = tile[6:7] + result[0:1]

            @pl.when(jnp.logical_not(is_mine))
            def _():
                result = pairs("density", rows, four, two, use, count, tile, cols, table)
                cells[pl.ds(spot + 6, 1), :] = tile[6:7] + result[0:1]

        return 0

    lax.fori_loop(0, total, across, 0)

    def weigh(s, _):
        spot = pl.multiple_of(s * 8, 8)
        tile = cells[pl.ds(spot, 8), :]
        inv = 1.0 / jnp.where(tile[3:4] > 0.0, tile[4:5], 1.0)
        inv2 = inv * inv
        inv4 = inv2 * inv2
        fresh = (4.0 * KC) * (inv4 * inv4) * tile[6:7]
        safe = jnp.where(tile[3:4] > 0.0, fresh, 1.0)
        power = jnp.exp(jnp.log(safe) * (-1.0 / 3.0))
        cells[pl.ds(spot + 5, 1), :] = tile[5:6] * power
        cells[pl.ds(spot + 6, 1), :] = safe
        cells[pl.ds(spot + 7, 1), :] = power
        return 0

    lax.fori_loop(0, total, weigh, 0)

    def last(s, _):
        x, y, z = spots[0, s], spots[1, s], spots[2, s]

        def check(t, n):
            close = (
                (jnp.abs(spots[0, t] - x) <= 1)
                & (jnp.abs(spots[1, t] - y) <= 1)
                & (jnp.abs(spots[2, t] - z) <= 1)
            )
            four[n] = t * 8
            two[n] = t * 8 + 4
            use[n] = jnp.float32(1.0)
            return n + close.astype(jnp.int32)

        count = lax.fori_loop(0, total, check, jnp.int32(0))
        spot = pl.multiple_of(s * 8, 8)
        tile = cells[pl.ds(spot, 8), :]
        result = final[s] + pairs("near", cells, four, two, use, count, tile, cols, table)
        good = tile[3:4] > 0.0
        own = final[s, 7:8] * tile[7:8]
        place = (x, y, pl.ds(z, 1), slice(None))
        density[place] = jnp.where(good, tile[6:7], old[place])
        for c in range(3):
            push = (20.0 * KC) * (own * final[s, 1 + c : 2 + c] + result[4 + c : 5 + c])
            accel[(c, *place)] = jnp.where(good, push, 0.0)
        return 0

    lax.fori_loop(0, mine, last, 0)


def f32(*shape):
    return jax.ShapeDtypeStruct(shape, jnp.float32)


def i32(*shape):
    return jax.ShapeDtypeStruct(shape, jnp.int32)


def neighbours(up, down, axis):
    size = lax.axis_size(axis)
    pairs_ = [(i, i + 1) for i in range(size - 1)]
    low = lax.ppermute(up, axis, pairs_)
    high = lax.ppermute(down, axis, [(j, i) for i, j in pairs_])
    return low, high


def work(flags, near):
    return [
        pltpu.SMEM((near,), jnp.int32),
        pltpu.SMEM((near,), jnp.int32),
        pltpu.SMEM((near,), jnp.float32),
        pltpu.SMEM((flags,), jnp.int32),
        pltpu.VMEM((128, 128), jnp.float32),
        pltpu.VMEM((128, 128), jnp.float32),
    ]


def cost(us):
    return pl.CostEstimate(flops=us * 10_000_000, bytes_accessed=us * 2_000_000, transcendentals=0)


def call(body, outs, out_specs, in_specs, scratch, us):
    return pl.pallas_call(
        body,
        out_shape=outs,
        in_specs=in_specs,
        out_specs=out_specs,
        scratch_shapes=scratch,
        compiler_params=PARAMS,
        cost_estimate=cost(us),
    )


def per_device(positions, mass, support, counts, entropy, density_old, active):
    small = [jnp.transpose(v, (1, 2, 0)) for v in (counts, active)]
    own, z_up, z_down, ids = call(
        pack,
        (f32(OWN_ROWS, S), f32(Z_ROWS, S), f32(Z_ROWS, S), i32(16)),
        (VMEM, VMEM, VMEM, SMEM),
        [SMEM, SMEM] + [VMEM] * 5,
        [],
        2,
    )(*small, positions, mass, support, entropy, density_old)
    zlo, zhi = neighbours(z_up, z_down, "gz")
    first = call(
        local_first, f32(16, 8, S), VMEM, [SMEM, VMEM], work(CELLS, 32), 8
    )(ids, own)
    x_up, x_down = call(
        pack_x, (f32(X_ROWS, S), f32(X_ROWS, S)), (VMEM, VMEM), [VMEM] * 3, [], 1
    )(own, zlo, zhi)
    xlo, xhi = neighbours(x_up, x_down, "gx")
    second = call(
        local_second,
        f32(16, 8, S),
        VMEM,
        [SMEM, VMEM, VMEM, pl.BlockSpec(memory_space=pl.ANY)],
        work(CELLS, 32),
        8,
    )(ids, own, first, x_up)
    y_up, y_down, tiles, sums, places = call(
        slab,
        (f32(Y_ROWS, S), f32(Y_ROWS, S), f32(SLAB_MOST, 8, S), f32(16, 8, S), i32(4, 128)),
        (VMEM, VMEM, VMEM, VMEM, SMEM),
        [SMEM] + [VMEM] * 6,
        [
            pltpu.VMEM((SLAB, S), jnp.float32),
            pltpu.VMEM((16, S), jnp.int32),
            pltpu.SMEM((16, S), jnp.int32),
            pltpu.SemaphoreType.DMA,
        ]
        + work((SX + 2) * SY * (SZ + 2), 32),
        4,
    )(ids, own, zlo, zhi, xlo, xhi, second)
    ylo, yhi = neighbours(y_up, y_down, "gy")
    return call(
        finish,
        (f32(SX, SY, SZ, S), f32(3, SX, SY, SZ, S)),
        (VMEM, VMEM),
        [SMEM] + [VMEM] * 7,
        [
            pltpu.VMEM((4 * Y_ROWS, S), jnp.float32),
            pltpu.VMEM((ALL_MOST * 8, S), jnp.float32),
            pltpu.VMEM((16, 8, S), jnp.float32),
            pltpu.SMEM((4, ALL_MOST), jnp.int32),
            pltpu.VMEM((32, S), jnp.int32),
            pltpu.SMEM((32, S), jnp.int32),
            pltpu.SemaphoreType.DMA,
        ]
        + work(2 * (SX + 2) * (SZ + 2), ALL_MOST + 16),
        8,
    )(places, ylo, yhi, y_up, y_down, tiles, sums, density_old)


def solution(mesh):
    return jax.shard_map(
        per_device,
        mesh=mesh,
        in_specs=(
            P(None, "gx", "gy", "gz", None),
            P("gx", "gy", "gz", None),
            P("gx", "gy", "gz", None),
            P("gx", "gy", "gz"),
            P("gx", "gy", "gz", None),
            P("gx", "gy", "gz", None),
            P("gx", "gy", "gz"),
        ),
        out_specs=(P("gx", "gy", "gz", None), P(None, "gx", "gy", "gz", None)),
        check_vma=False,
    )
```

time: 258 us -> 118 us (0.46)
  the two profiles are of different devices: /device:TPU:83 before, /device:TPU:352 now
where the time goes in v2:
time: 118 us
  Pallas kernels  84.2 us (71%)
  starting transfers between devices  14.3 us (12%)
  waiting for transfers between devices  12.1 us (10%)
  local copies, waits for them, and re-layouts  6.48 us (5%)
    pallas_call x1, Pallas kernels, per_device(): call(slab, (f32(Y_ROWS, S), f32(Y_ROWS, S), f32(SLAB_MOST, 8, S), f32(16,...  39.8 us
    pallas_call x1, Pallas kernels, per_device(): call(finish, (f32(SX, SY, SZ, S), f32(3, SX, SY, SZ, S)), (VMEM, VMEM), [...  25.1 us
    pallas_call x1, Pallas kernels, per_device(): call(local_first, f32(16, 8, S), VMEM, [SMEM, VMEM], work(CELLS, 32), 8)  8.28 us
    ppermute x3, starting transfers between devices, neighbours(): low = lax.ppermute(up, axis, pairs_)  8.19 us
    pallas_call x1, Pallas kernels, per_device(): call(local_second, f32(16, 8, S), VMEM, [SMEM, VMEM, VMEM, pl.BlockSpec(m...  6.92 us
    ppermute x3, waiting for transfers between devices, neighbours(): low = lax.ppermute(up, axis, pairs_)  6.64 us
    unnamed x16, local copies, waits for them, and re-layouts  6.48 us
    ppermute x3, starting transfers between devices, neighbours(): high = lax.ppermute(down, axis, [(j, i) for i, j in pairs_])  6.11 us
  transfers between devices with their start and end apart: 6, of which 4 were waited for; matrix products, arithmetic and copies ran while one was open for 0% of the time, Pallas kernels for 13%

profile of v2, /device:TPU:352, one launch (start us, length us, event | category | flops | bytes accessed | tf_op | source)
XLA Modules:
  0.0 117.8 jit_solution(5038212198811397091)
XLA Ops:
  0.6 0.0 copy-start
  0.6 1.0 copy-done
  1.6 0.0 copy-start.2
  1.6 1.2 copy-done.2
  2.8 0.0 copy-start.3
  2.8 1.0 copy-done.3
  3.7 0.0 copy-start.4
  3.7 1.0 copy-done.4
  4.7 0.0 copy-start.5
  4.7 1.0 copy-done.5
  5.7 0.0 copy-start.6
  5.7 0.7 copy-done.6
  6.4 0.7 copy-done.7
  7.1 4.0 %shard_map.86 = (f32[3472,128]{1,0:T(8,128)S(1)}, f32[728,128]{1,0:T(8,128)S(1)}, f32[728,128]{1,0:T(8,128)S(1)}, s32[16]{0:T(128)S(1)}) custom-call(s32[6,6,12]{2,1,0:T(8,128)S(1)} %bitcast.2, s32[6,6,12]{2,1,0:T(8,128)S(1)} %bitcast.3, f32[3,12,6,6,128]{4,3,2,1,0:T(8,128)S(1)} %copy-done.2, f32[12,6,6,128]{3,2,1,0:T(8,128)S(1)} %copy-done.3, ...), custom_call_target="tpu_custom_call" | custom-call | flops 20000000 | bytes 4000000 | tf_op jit(solution)/shard_map/pallas_call | solution.py:622
  11.2 3.4 %collective-permute-start = (f32[728,128]{1,0:T(8,128)S(1)}, f32[728,128]{1,0:T(8,128)S(1)}, u32[]{:S(2)}, u32[]{:S(2)}) collective-permute-start(f32[728,128]{1,0:T(8,128)S(1)} %get-tuple-element.15), channel_id=1, source_target_pairs={{0,1},{1,2},{2,3},{3,4},{4,5},{5,6},{6,7},{8,9},{9,10},{10,11},{11... | collective-permute-start | bytes 1118216 | tf_op jit(solution)/shard_map/ppermute | solution.py:588
  14.6 2.5 %collective-permute-start.1 = (f32[728,128]{1,0:T(8,128)S(1)}, f32[728,128]{1,0:T(8,128)S(1)}, u32[]{:S(2)}, u32[]{:S(2)}) collective-permute-start(f32[728,128]{1,0:T(8,128)S(1)} %get-tuple-element.16), channel_id=1, source_target_pairs={{1,0},{2,1},{3,2},{4,3},{5,4},{6,5},{7,6},{9,8},{10,9},{11,10},{12... | collective-permute-start | bytes 1118216 | tf_op jit(solution)/shard_map/ppermute | solution.py:589
  17.0 6.5 %collective-permute-done.zlo = f32[728,128]{1,0:T(8,128)S(1)} collective-permute-done((f32[728,128]{1,0:T(8,128)S(1)}, f32[728,128]{1,0:T(8,128)S(1)}, u32[]{:S(2)}, u32[]{:S(2)}) %collective-permute-start) | collective-permute-done | bytes 372768 | tf_op jit(solution)/shard_map/ppermute | solution.py:588
  23.5 3.1 %collective-permute-done.1.zhi = f32[728,128]{1,0:T(8,128)S(1)} collective-permute-done((f32[728,128]{1,0:T(8,128)S(1)}, f32[728,128]{1,0:T(8,128)S(1)}, u32[]{:S(2)}, u32[]{:S(2)}) %collective-permute-start.1) | collective-permute-done | bytes 372768 | tf_op jit(solution)/shard_map/ppermute | solution.py:589
  26.6 0.1 shard_map.87
  26.7 2.4 %collective-permute-start.3 = (f32[584,128]{1,0:T(8,128)S(1)}, f32[584,128]{1,0:T(8,128)S(1)}, u32[]{:S(2)}, u32[]{:S(2)}) collective-permute-start(f32[584,128]{1,0:T(8,128)S(1)} %get-tuple-element.18), channel_id=1, source_target_pairs={{64,0},{128,64},{192,128},{256,192},{320,256},{384,320},{448,384},... | collective-permute-start | bytes 897032 | tf_op jit(solution)/shard_map/ppermute | solution.py:589
  29.1 3.5 %collective-permute-start.2 = (f32[584,128]{1,0:T(8,128)S(1)}, f32[584,128]{1,0:T(8,128)S(1)}, u32[]{:S(2)}, u32[]{:S(2)}) collective-permute-start(f32[584,128]{1,0:T(8,128)S(1)} %get-tuple-element.17._), channel_id=1, source_target_pairs={{0,64},{64,128},{128,192},{192,256},{256,320},{320,384},{384,448},... | collective-permute-start | bytes 897032 | tf_op jit(solution)/shard_map/ppermute | solution.py:588
  32.6 8.3 %shard_map.88.before = f32[16,8,128]{2,1,0:T(8,128)S(1)} custom-call(s32[16]{0:T(128)S(1)} %get-tuple-element.13.ids, f32[3472,128]{1,0:T(8,128)S(1)} %get-tuple-element.14.own), custom_call_target="tpu_custom_call" | custom-call | flops 80000000 | bytes 16000000 | tf_op jit(solution)/shard_map/pallas_call | solution.py:631
  40.9 6.9 %shard_map.89.before = f32[16,8,128]{2,1,0:T(8,128)S(1)} custom-call(s32[16]{0:T(128)S(1)} %get-tuple-element.13.ids, f32[3472,128]{1,0:T(8,128)S(1)} %get-tuple-element.14.own, f32[16,8,128]{2,1,0:T(8,128)S(1)} %shard_map.88.before, f32[584,128]{1,0:T(8,128)S(1)} %get-tuple-element.17._), custom_call_target="tpu_custom_call" | custom-call | flops 80000000 | bytes 16000000 | tf_op jit(solution)/shard_map/pallas_call | solution.py:638
  47.8 0.0 collective-permute-done.3.xhi
  47.8 0.0 collective-permute-done.2.xlo
  47.8 39.8 %shard_map.90 = (f32[992,128]{1,0:T(8,128)S(1)}, f32[992,128]{1,0:T(8,128)S(1)}, f32[96,8,128]{2,1,0:T(8,128)S(1)}, f32[16,8,128]{2,1,0:T(8,128)S(1)}, s32[4,128]{1,0:T(4,128)S(1)}) custom-call(s32[16]{0:T(128)S(1)} %get-tuple-element.13.ids, f32[3472,128]{1,0:T(8,128)S(1)} %get-tuple-element.14.own, f32[728,128]{1,0:T(8,128)S(1)} %collective-permute-done.zlo, ...), custom_call_target="tpu_custom_call" | custom-call | flops 40000000 | bytes 8000000 | tf_op jit(solution)/shard_map/pallas_call | solution.py:646
  87.6 1.3 %collective-permute-start.4 = (f32[992,128]{1,0:T(8,128)S(1)}, f32[992,128]{1,0:T(8,128)S(1)}, u32[]{:S(2)}, u32[]{:S(2)}) collective-permute-start(f32[992,128]{1,0:T(8,128)S(1)} %get-tuple-element.20.up), channel_id=1, source_target_pairs={{0,8},{8,16},{16,24},{24,32},{32,40},{40,48},{48,56},{1,9},{9,17},... | collective-permute-start | bytes 1523720 | tf_op jit(solution)/shard_map/ppermute | solution.py:588
  88.9 1.3 %collective-permute-start.5 = (f32[992,128]{1,0:T(8,128)S(1)}, f32[992,128]{1,0:T(8,128)S(1)}, u32[]{:S(2)}, u32[]{:S(2)}) collective-permute-start(f32[992,128]{1,0:T(8,128)S(1)} %get-tuple-element.21.down), channel_id=1, source_target_pairs={{8,0},{16,8},{24,16},{32,24},{40,32},{48,40},{56,48},{9,1},{17,9},... | collective-permute-start | bytes 1523720 | tf_op jit(solution)/shard_map/ppermute | solution.py:589
  90.2 0.2 collective-permute-done.4.ylo
  90.4 2.3 %collective-permute-done.5.yhi = f32[992,128]{1,0:T(8,128)S(1)} collective-permute-done((f32[992,128]{1,0:T(8,128)S(1)}, f32[992,128]{1,0:T(8,128)S(1)}, u32[]{:S(2)}, u32[]{:S(2)}) %collective-permute-start.5) | collective-permute-done | bytes 507936 | tf_op jit(solution)/shard_map/ppermute | solution.py:589
  92.7 0.0 copy-done.1
  92.7 25.1 %shard_map.91 = (f32[12,6,6,128]{3,2,1,0:T(8,128)}, f32[3,12,6,6,128]{4,3,2,1,0:T(8,128)}) custom-call(s32[4,128]{1,0:T(4,128)S(1)} %get-tuple-element.19.places, f32[992,128]{1,0:T(8,128)S(1)} %collective-permute-done.4.ylo, f32[992,128]{1,0:T(8,128)S(1)} %collective-permute-done.5.yhi, f32[992,128]{1,0:T(8,128)S(1)} %get-tuple-element.20.up, ...), custom_call_target="tpu_custom_call" | custom-call | flops 80000000 | bytes 16000000 | tf_op jit(solution)/shard_map/pallas_call | solution.py:661
  (2 shorter events, 0.0 us)
Async XLA Ops:
  0.6 1.0 copy-start
  1.6 1.2 copy-start.2
  2.8 1.0 copy-start.3
  3.7 1.0 copy-start.4
  4.7 1.0 copy-start.5
  5.7 0.7 copy-start.6
  6.4 0.7 copy-start.7
  11.2 12.3 %collective-permute-start = (f32[728,128]{1,0:T(8,128)S(1)}, f32[728,128]{1,0:T(8,128)S(1)}, u32[]{:S(2)}, u32[]{:S(2)}) collective-permute-start(f32[728,128]{1,0:T(8,128)S(1)} %get-tuple-element.15), channel_id=1, source_target_pairs={{0,1},{1,2},{2,3},{3,4},{4,5},{5,6},{6,7},{8,9},{9,10},{10,11},{11... | collective-permute-start | bytes 1118216 | tf_op jit(solution)/shard_map/ppermute | solution.py:588
  14.6 12.0 %collective-permute-start.1 = (f32[728,128]{1,0:T(8,128)S(1)}, f32[728,128]{1,0:T(8,128)S(1)}, u32[]{:S(2)}, u32[]{:S(2)}) collective-permute-start(f32[728,128]{1,0:T(8,128)S(1)} %get-tuple-element.16), channel_id=1, source_target_pairs={{1,0},{2,1},{3,2},{4,3},{5,4},{6,5},{7,6},{9,8},{10,9},{11,10},{12... | collective-permute-start | bytes 1118216 | tf_op jit(solution)/shard_map/ppermute | solution.py:589
  26.7 21.1 %collective-permute-start.3 = (f32[584,128]{1,0:T(8,128)S(1)}, f32[584,128]{1,0:T(8,128)S(1)}, u32[]{:S(2)}, u32[]{:S(2)}) collective-permute-start(f32[584,128]{1,0:T(8,128)S(1)} %get-tuple-element.18), channel_id=1, source_target_pairs={{64,0},{128,64},{192,128},{256,192},{320,256},{384,320},{448,384},... | collective-permute-start | bytes 897032 | tf_op jit(solution)/shard_map/ppermute | solution.py:589
  29.1 18.7 %collective-permute-start.2 = (f32[584,128]{1,0:T(8,128)S(1)}, f32[584,128]{1,0:T(8,128)S(1)}, u32[]{:S(2)}, u32[]{:S(2)}) collective-permute-start(f32[584,128]{1,0:T(8,128)S(1)} %get-tuple-element.17._), channel_id=1, source_target_pairs={{0,64},{64,128},{128,192},{192,256},{256,320},{320,384},{384,448},... | collective-permute-start | bytes 897032 | tf_op jit(solution)/shard_map/ppermute | solution.py:588
  47.8 44.9 %copy-start.1 = (f32[12,6,6,128]{3,2,1,0:T(8,128)S(1)}, f32[12,6,6,128]{3,2,1,0:T(8,128)}, u32[]{:S(2)}) copy-start(f32[12,6,6,128]{3,2,1,0:T(8,128)} %old.3) | copy-start | bytes 663556
  87.6 2.8 %collective-permute-start.4 = (f32[992,128]{1,0:T(8,128)S(1)}, f32[992,128]{1,0:T(8,128)S(1)}, u32[]{:S(2)}, u32[]{:S(2)}) collective-permute-start(f32[992,128]{1,0:T(8,128)S(1)} %get-tuple-element.20.up), channel_id=1, source_target_pairs={{0,8},{8,16},{16,24},{24,32},{32,40},{40,48},{48,56},{1,9},{9,17},... | collective-permute-start | bytes 1523720 | tf_op jit(solution)/shard_map/ppermute | solution.py:588
  88.9 3.8 %collective-permute-start.5 = (f32[992,128]{1,0:T(8,128)S(1)}, f32[992,128]{1,0:T(8,128)S(1)}, u32[]{:S(2)}, u32[]{:S(2)}) collective-permute-start(f32[992,128]{1,0:T(8,128)S(1)} %get-tuple-element.21.down), channel_id=1, source_target_pairs={{8,0},{16,8},{24,16},{32,24},{40,32},{48,40},{56,48},{9,1},{17,9},... | collective-permute-start | bytes 1523720 | tf_op jit(solution)/shard_map/ppermute | solution.py:589

commit v3 on v2

v3 whole, which is shorter than its diff:
```python
import functools
import math

import jax
import jax.numpy as jnp
from jax import lax
from jax.experimental import pallas as pl
from jax.experimental.pallas import tpu as pltpu
from jax.sharding import PartitionSpec as P

KC = 21.0 / (2.0 * math.pi)
SX, SY, SZ, S = 12, 6, 6, 128
MOST = 9
CELLS = SX * SY * SZ

ZERO = CELLS * 8
OWN_TAIL = ZERO + 8
OWN_ROWS = OWN_TAIL + 8

Z_TWO, Z_FAR, Z_TAIL, Z_ROWS = 288, 432, 720, 728
X_TWO, X_FAR, X_TAIL, X_ROWS = 240, 336, 576, 584
Y_TWO, Y_SUM, Y_TAIL, Y_ROWS = 640, 864, 976, 984

ZLO = OWN_ROWS
ZHI = ZLO + Z_ROWS
XLO = ZHI + Z_ROWS
XHI = XLO + X_ROWS
SLAB = XHI + X_ROWS

SLAB_MOST = 96
ALL_MOST = 256

VMEM = pl.BlockSpec(memory_space=pltpu.VMEM)
SMEM = pl.BlockSpec(memory_space=pltpu.SMEM)
ANY = pl.BlockSpec(memory_space=pl.ANY)
PARAMS = pltpu.CompilerParams(vmem_limit_bytes=40 * 1024 * 1024)

BLOCKS = [(0, 0), (0, -1), (0, 1), (-1, 0), (-1, -1), (-1, 1), (1, 0), (1, -1), (1, 1)]


def step(mode, i, near, sums):
    xi, yi, zi, hi, bi = i
    xj, yj, zj, mj, hj, wj = near
    dx, dy, dz = xi - xj, yi - yj, zi - zj
    sq = jnp.maximum(dx * dx + dy * dy + dz * dz, 1e-30)
    dist = sq * lax.rsqrt(sq)
    out = []
    if mode != "near":
        wi = jnp.maximum(hi - dist, 0.0)
        own = mj * (wi * wi * wi)
        out.append(sums[0] + own * (wi * (bi - wi)))
        if mode == "all":
            out += [sums[1] + own * dx, sums[2] + own * dy, sums[3] + own * dz]
    if mode != "density":
        wj_ = jnp.maximum(hj - dist, 0.0)
        other = wj * (wj_ * wj_ * wj_)
        last = sums[-3:]
        out += [last[0] + other * dx, last[1] + other * dy, last[2] + other * dz]
    return tuple(out)


WIDTH = {"all": 7, "density": 1, "near": 3}
FIRST = {"all": 0, "density": 0, "near": 4}
NEAR = {"all": 3, "density": 9, "near": 1}
GROUPS = {"all": 2, "density": 2, "near": 8}


def pairs(mode, src, four, two, use, count, tile, cols, table):
    many, regs = NEAR[mode], GROUPS[mode]
    for u in range(many - 1):
        four[count + u] = jnp.int32(0)
        two[count + u] = jnp.int32(0)
        use[count + u] = jnp.float32(0.0)
    steps = lax.div(count + (many - 1), many)
    used = jnp.sum(jnp.where(tile[3:4] > 0.0, 1.0, 0.0)).astype(jnp.int32)
    for n, c in enumerate((0, 1, 2, 4)):
        if mode == "near" and n == 3:
            break
        cols[n] = jnp.broadcast_to(tile[c : c + 1], (128, 128)).T
    width = WIDTH[mode]
    zero = jnp.zeros((8, 128), jnp.float32)

    def group(g, _):
        spots, own = [], []
        for v in range(regs):
            spot = pl.ds(pl.multiple_of((g * regs + v) * 8, 8), 8)
            x, y, z = [cols[n, spot, :] for n in range(3)]
            h = cols[3, spot, :] if mode != "near" else None
            spots.append(spot)
            own.append((x, y, z, h, 1.25 * h if mode != "near" else None))

        def body(q, sums):
            sums = list(sums)
            for u in range(many):
                at = q * many + u
                f = four[at]
                near = [
                    jnp.broadcast_to(src[pl.ds(f + c, 1), :], (8, 128)) for c in range(4)
                ]
                flag = use[at]
                if mode != "near":
                    near[3] = near[3] * jnp.where(flag >= 0.5, 1.0, 0.0)
                if mode != "density":
                    t = two[at]
                    near.append(jnp.broadcast_to(src[pl.ds(t, 1), :], (8, 128)))
                    weight = jnp.broadcast_to(src[pl.ds(t + 1, 1), :], (8, 128))
                    near.append(weight * jnp.where(flag == 1.0, 1.0, 0.0))
                else:
                    near += [None, None]
                for v in range(regs):
                    sums[v] = step(mode, own[v], near, sums[v])
            return tuple(sums)

        sums = lax.fori_loop(0, steps, body, ((zero,) * width,) * regs)
        for v in range(regs):
            for c in range(width):
                table[c, spots[v], :] = sums[v][c]
        return 0

    lax.fori_loop(0, lax.div(used + (8 * regs - 1), 8 * regs), group, 0)
    lines = [jnp.sum(table[c].T, axis=0, keepdims=True) for c in range(width)]
    if mode == "density":
        return lines[0]
    before = [jnp.zeros((1, 128), jnp.float32)] * FIRST[mode]
    after = [jnp.zeros((1, 128), jnp.float32)] * (8 - FIRST[mode] - width)
    return jnp.concatenate(before + lines + after, axis=0)


def bit(word, at):
    return lax.shift_right_logical(word, at) & 1


def clear(words, count):
    def one(k, _):
        words[k] = jnp.int32(0)
        return 0

    lax.fori_loop(0, count, one, 0, unroll=14)


def mark(words, at, place):
    words[at] = words[at] | lax.shift_left(jnp.int32(1), place)


def corner(k):
    return lax.div(k, SY * SZ), lax.rem(lax.div(k, SZ), SY), lax.rem(k, SZ)


def pack(
    counts_in, active_in, pos_in, mass_in, support_in, entropy_in, old_in, own, up, down, ids,
    counts, active, pos, mass, support, entropy, old, sems,
):
    given = (active_in, counts_in, pos_in, mass_in, support_in, entropy_in, old_in)
    held = (active, counts, pos, mass, support, entropy, old)
    copies = [pltpu.make_async_copy(a, b, sems.at[n]) for n, (a, b) in enumerate(zip(given, held))]
    for copy in copies:
        copy.start()
    copies[0].wait()

    def scan(q, n):
        y, z = lax.div(q, SZ), lax.rem(q, SZ)
        for x in range(SX):
            ids[n] = (x * SY + y) * SZ + z
            n = n + active[y, z, x]
        return n

    number = lax.fori_loop(0, SY * SZ, scan, jnp.int32(0))
    for s in range(MOST, 15):
        ids[s] = jnp.int32(0)
    ids[15] = number
    lane = lax.broadcasted_iota(jnp.int32, (8, 128), 1)
    tail = jnp.zeros((8, 128), jnp.int32)
    for s in range(MOST):
        tail = jnp.where(lane == s, ids[s], tail)
    tail = jnp.where(lane == 15, number, tail).astype(jnp.float32)
    own[ZERO : ZERO + 8] = jnp.zeros((8, 128), jnp.float32)
    own[OWN_TAIL : OWN_TAIL + 8] = tail
    up[Z_TAIL : Z_TAIL + 8] = tail
    down[Z_TAIL : Z_TAIL + 8] = tail
    for copy in copies[1:]:
        copy.wait()
    sub = lax.broadcasted_iota(jnp.int32, (SZ, 128), 0)
    slot = lax.broadcasted_iota(jnp.int32, (SZ, 128), 1)

    def cells(x, _):
        for y in range(SY):
            many = jnp.zeros((SZ, 128), jnp.int32)
            act = jnp.zeros((SZ, 128), jnp.int32)
            for z in range(SZ):
                many = jnp.where(sub == z, counts[y, z, x], many)
                act = jnp.where(sub == z, active[y, z, x], act)
            h = support[x, y]
            inv = 1.0 / h
            inv2 = inv * inv
            inv4 = inv2 * inv2
            m = jnp.where(slot < many, mass[x, y], 0.0)
            gain = entropy[x, y] * (inv4 * inv4)
            power = jnp.exp(jnp.log(old[x, y]) * (-1.0 / 3.0))
            weight = m * gain * jnp.where(act > 0, 1.0, power)
            base = pl.multiple_of(x * (SY * SZ * 8), 8) + y * SZ * 8
            for c, value in enumerate(
                (pos[0, x, y], pos[1, x, y], pos[2, x, y], m, h, weight, gain)
            ):
                own[pl.ds(base + c, SZ, stride=8), :] = value
        return 0

    lax.fori_loop(0, SX, cells, 0)

    def faces(x2, _):
        for u in range(2):
            for y in range(SY):
                base = pl.multiple_of(x2 * (2 * SY * SZ * 8), 8) + (u * SY + y) * SZ * 8
                four = pl.multiple_of(x2 * (2 * SY * 4), 8) + (u * SY + y) * 4
                two = pl.multiple_of(x2 * (2 * SY * 2), 8) + (u * SY + y) * 2
                for out, z1, z2 in ((up, SZ - 1, SZ - 2), (down, 0, 1)):
                    out[pl.ds(four, 4), :] = own[pl.ds(base + z1 * 8, 4), :]
                    out[pl.ds(two + Z_TWO, 2), :] = own[pl.ds(base + z1 * 8 + 4, 2), :]
                    out[pl.ds(four + Z_FAR, 4), :] = own[pl.ds(base + z2 * 8, 4), :]
        return 0

    lax.fori_loop(0, SX // 2, faces, 0)


def own_row(x, y, z):
    return ((x * SY + y) * SZ + z) * 8


def local(part, ids, own, before, sums, four, two, use, flags, cols, table):
    number = ids[15]
    half = lax.div(number + 1, 2)

    clear(flags, SX * SY)

    def one(s, _):
        k = ids[s]
        mark(flags, lax.div(k, SZ), lax.rem(k, SZ))
        return 0

    lax.fori_loop(0, number, one, 0)
    if before is not None:
        sums[...] = before[...]

    def slot(s, _):
        k = ids[s]
        a, b, d = corner(k)
        count = jnp.int32(0)
        in_z = [(d + ed >= 0) & (d + ed < SZ) for ed in (-1, 0, 1)]
        for ea in (-1, 0, 1):
            for eb in (-1, 0, 1):
                na, nb = a + ea, b + eb
                inside = (na >= 0) & (na < SX) & (nb >= 0) & (nb < SY)
                column = na * SY + nb
                word = flags[jnp.where(inside, column, 0)]
                row = column * (SZ * 8) + d * 8
                for n, ed in enumerate((-1, 0, 1)):
                    four[count] = row + ed * 8
                    two[count] = row + (ed * 8 + 4)
                    known = bit(word, jnp.maximum(d + ed, 0))
                    use[count] = jnp.where(known > 0, jnp.float32(0.5), jnp.float32(1.0))
                    count = count + (inside & in_z[n]).astype(jnp.int32)
        row = pl.multiple_of(k * 8, 8)
        tile = own[pl.ds(row, 8), :]
        sums[s] = pairs("all", own, four, two, use, count, tile, cols, table)
        return 0

    if part == 0:
        lax.fori_loop(0, half, slot, 0)
    else:
        lax.fori_loop(half, number, slot, 0)


def local_first(ids, own, sums, *scratch):
    local(0, ids, own, None, sums, *scratch)


def local_second(ids, own, before, _, sums, *scratch):
    local(1, ids, own, before, sums, *scratch)


def pack_x(own, zlo, zhi, _, up, down):
    for out, x1, x2 in ((up, SX - 1, SX - 2), (down, 0, 1)):
        for y in range(SY):
            for z in range(-2, SZ + 2):
                for x, base in ((x1, 0), (x2, X_FAR)):
                    spot = base + (y * (SZ + 4) + z + 2) * 4
                    if 0 <= z < SZ:
                        row = own_row(x, y, z)
                        out[spot : spot + 4] = own[row : row + 4]
                    else:
                        src = zlo if z < 0 else zhi
                        far = Z_FAR if z in (-2, SZ + 1) else 0
                        row = far + (x * SY + y) * 4
                        out[spot : spot + 4] = src[row : row + 4]
                if -1 <= z <= SZ:
                    spot = X_TWO + (y * (SZ + 2) + z + 1) * 2
                    if 0 <= z < SZ:
                        row = own_row(x1, y, z) + 4
                        out[spot : spot + 2] = own[row : row + 2]
                    else:
                        src = zlo if z < 0 else zhi
                        row = Z_TWO + (x1 * SY + y) * 2
                        out[spot : spot + 2] = src[row : row + 2]
        out[X_TAIL : X_TAIL + 8] = jnp.zeros((8, 128), jnp.float32)
        out[X_TAIL : X_TAIL + 1] = own[OWN_TAIL : OWN_TAIL + 1]
        out[X_TAIL + 1 : X_TAIL + 2] = zlo[Z_TAIL : Z_TAIL + 1]
        out[X_TAIL + 2 : X_TAIL + 3] = zhi[Z_TAIL : Z_TAIL + 1]


def slab_rows(x, z):
    zlow, xlow = z < 0, x < 0
    zout = zlow | (z >= SZ)
    xout = xlow | (x >= SX)
    zbase = jnp.where(zlow, ZLO, ZHI)
    zfar = jnp.where((z == -2) | (z == SZ + 1), Z_FAR, 0)
    xbase = jnp.where(xlow, XLO, XHI)
    xfar = jnp.where((x == -2) | (x == SX + 1), X_FAR, 0)
    four = jnp.where(zout, zbase + zfar + x * (SY * 4), x * (SY * SZ * 8) + z * 8)
    two = jnp.where(zout, zbase + Z_TWO + x * (SY * 2), x * (SY * SZ * 8) + z * 8 + 4)
    four = jnp.where(xout, xbase + xfar + (z + 2) * 4, four)
    two = jnp.where(xout, xbase + X_TWO + (z + 1) * 2, two)
    add4 = jnp.where(xout, (SZ + 4) * 4, jnp.where(zout, 4, SZ * 8))
    add2 = jnp.where(xout, (SZ + 2) * 2, jnp.where(zout, 2, SZ * 8))
    return four, two, add4, add2


def slab_rows_at(x, y, z):
    if 0 <= x < SX and 0 <= z < SZ:
        return own_row(x, y, z), own_row(x, y, z) + 4
    if 0 <= x < SX:
        base, far, k = ZLO if z < 0 else ZHI, z in (-2, SZ + 1), x * SY + y
        return base + (Z_FAR if far else 0) + k * 4, base + Z_TWO + k * 2
    base, far = XLO if x < 0 else XHI, x in (-2, SX + 1)
    four = base + (X_FAR if far else 0) + (y * (SZ + 4) + z + 2) * 4
    return four, base + X_TWO + (y * (SZ + 2) + z + 1) * 2


def slab(
    ids, own, zlo, zhi, xlo, xhi, before, up, down, tiles, sums, places,
    rows, tails, lists, sem, four, two, use, flags, cols, table,
):
    rows[0:OWN_ROWS] = own[...]
    rows[ZLO:ZHI] = zlo[...]
    rows[ZHI:XLO] = zhi[...]
    rows[XLO:XHI] = xlo[...]
    rows[XHI:SLAB] = xhi[...]
    tails[...] = jnp.zeros(tails.shape, jnp.int32)
    tails[0:1] = own[OWN_TAIL : OWN_TAIL + 1].astype(jnp.int32)
    tails[1:2] = zlo[Z_TAIL : Z_TAIL + 1].astype(jnp.int32)
    tails[2:3] = zhi[Z_TAIL : Z_TAIL + 1].astype(jnp.int32)
    tails[3:6] = xlo[X_TAIL : X_TAIL + 3].astype(jnp.int32)
    tails[6:9] = xhi[X_TAIL : X_TAIL + 3].astype(jnp.int32)
    copy = pltpu.make_async_copy(tails, lists, sem)
    copy.start()

    clear(flags, (SX + 2) * SY)
    for out, y in ((up, SY - 1), (down, 0)):
        for x in range(-2, SX + 2):
            for z in range(-2, SZ + 2):
                row4, row2 = slab_rows_at(x, y, z)
                spot = ((x + 2) * (SZ + 4) + z + 2) * 4
                out[spot : spot + 4] = rows[row4 : row4 + 4]
                if -1 <= x <= SX and -1 <= z <= SZ:
                    spot = Y_TWO + ((x + 1) * (SZ + 2) + z + 1) * 2
                    out[spot : spot + 2] = rows[row2 : row2 + 2]
        out[Y_SUM:Y_TAIL] = jnp.zeros((Y_TAIL - Y_SUM, 128), jnp.float32)
    copy.wait()

    number = jnp.int32(0)
    for q, (bx, bz) in enumerate(BLOCKS):

        def one(s, n, q=q, bx=bx, bz=bz):
            a, b, d = corner(lists[q, s])
            x, z = a + bx * SX, d + bz * SZ
            inside = (x >= -1) & (x <= SX) & (z >= -1) & (z <= SZ)
            places[0, n] = x
            places[1, n] = b
            places[2, n] = z

            @pl.when(inside)
            def _():
                mark(flags, (x + 1) * SY + b, z + 1)

            return n + inside.astype(jnp.int32)

        number = lax.fori_loop(0, lists[q, 15], one, number)
    places[3, 0] = number
    places[3, 1] = lists[0, 15]
    mine = lists[0, 15]

    lane = lax.broadcasted_iota(jnp.int32, (8, 128), 1)
    line = lax.broadcasted_iota(jnp.int32, (8, 128), 0)

    def tell(s, state):
        lists_, numbers = list(state[0]), list(state[1])
        x, y, z = places[0, s], places[1, s], places[2, s]
        for n, edge in enumerate((SY - 1, 0)):
            here = y == edge
            at = jnp.where(here, numbers[n], 126)
            value = jnp.where(line == 0, x, z)
            lists_[n] = jnp.where(lane == at, value, lists_[n])
            numbers[n] = numbers[n] + here.astype(jnp.int32)
        return tuple(lists_), tuple(numbers)

    nothing = jnp.zeros((8, 128), jnp.int32)
    told, numbers = lax.fori_loop(
        0, number, tell, ((nothing, nothing), (jnp.int32(0), jnp.int32(0)))
    )
    for n, out in enumerate((up, down)):
        out[Y_TAIL:Y_ROWS] = jnp.where(lane == 127, numbers[n], told[n]).astype(jnp.float32)

    def near_list(x, y, z, own_cell):
        count = jnp.int32(0)
        for ea in (-1, 0, 1):
            for ed in (-1, 0, 1):
                na, nd = x + ea, z + ed
                f4, f2, add4, add2 = slab_rows(na, nd)
                if own_cell:
                    outer = (na < 0) | (na >= SX) | (nd < 0) | (nd >= SZ)
                for eb in (-1, 0, 1):
                    nb = y + eb
                    wanted = (nb >= 0) & (nb < SY)
                    four[count] = f4 + nb * add4
                    if own_cell:
                        wanted = wanted & outer
                        two[count] = f2 + nb * add2
                        word = flags[(na + 1) * SY + jnp.where(wanted, nb, 0)]
                        known = bit(word, nd + 1)
                        use[count] = jnp.where(known > 0, jnp.float32(0.5), jnp.float32(1.0))
                    else:
                        use[count] = jnp.float32(1.0)
                    count = count + wanted.astype(jnp.int32)
        return count

    def cell(x, y, z):
        f4, f2, add4, add2 = slab_rows(x, z)
        first = rows[pl.ds(f4 + y * add4, 4), :]
        second = rows[pl.ds(f2 + y * add2, 2), :]
        return jnp.concatenate([first, second, jnp.zeros((2, 128), jnp.float32)], axis=0)

    def send_sum(s, x, y, z):
        spot = Y_SUM + (x + 1) * (SZ + 2) + z + 1

        @pl.when(y == 0)
        def _():
            down[pl.ds(spot, 1), :] = tiles[s, 6:7]

        @pl.when(y == SY - 1)
        def _():
            up[pl.ds(spot, 1), :] = tiles[s, 6:7]

    def own_slot(s, _):
        x, y, z = places[0, s], places[1, s], places[2, s]
        sums[s] = before[s]

        @pl.when((x == 0) | (x == SX - 1) | (z == 0) | (z == SZ - 1))
        def _():
            count = near_list(x, y, z, True)
            tile = cell(x, y, z)
            sums[s] = sums[s] + pairs("all", rows, four, two, use, count, tile, cols, table)

        row = pl.multiple_of(own_row(x, y, z), 8)
        whole = rows[pl.ds(row, 8), :]
        tiles[s] = whole
        tiles[s, 6:7] = sums[s, 0:1]
        sums[s, 7:8] = whole[6:7]
        send_sum(s, x, y, z)
        return 0

    def halo_slot(s, _):
        x, y, z = places[0, s], places[1, s], places[2, s]
        count = near_list(x, y, z, False)
        tile = cell(x, y, z)
        tiles[s] = tile
        tiles[s, 6:7] = pairs("density", rows, four, two, use, count, tile, cols, table)
        send_sum(s, x, y, z)
        return 0

    lax.fori_loop(0, mine, own_slot, 0)
    lax.fori_loop(mine, number, halo_slot, 0)


def finish(
    places, ylo, yhi, up, down, tiles, sums, old, density, accel,
    rows, cells, final, spots, tails, lists, sem, four, two, use, flags, cols, table,
):
    tails[0:8] = ylo[Y_TAIL:Y_ROWS].astype(jnp.int32)
    tails[8:16] = yhi[Y_TAIL:Y_ROWS].astype(jnp.int32)
    copy = pltpu.make_async_copy(tails, lists, sem)
    copy.start()
    rows[0:Y_ROWS] = ylo[...]
    rows[Y_ROWS : 2 * Y_ROWS] = yhi[...]
    rows[2 * Y_ROWS : 3 * Y_ROWS] = down[...]
    rows[3 * Y_ROWS : 4 * Y_ROWS] = up[...]
    density[...] = old[...]
    accel[...] = jnp.zeros(accel.shape, jnp.float32)
    clear(flags, 2 * (SX + 2))
    number, mine = places[3, 0], places[3, 1]

    def take(s, _):
        for c in range(3):
            spots[c, s] = places[c, s]
        cells[pl.ds(pl.multiple_of(s * 8, 8), 8), :] = tiles[s]
        return 0

    lax.fori_loop(0, number, take, 0)
    final[...] = sums[...]
    copy.wait()
    total = number
    for side in range(2):

        def one(s, n, side=side):
            x, z = lists[side * 8, s], lists[side * 8 + 1, s]
            spots[0, n] = x
            spots[1, n] = jnp.int32(-1 if side == 0 else SY)
            spots[2, n] = z
            mark(flags, side * (SX + 2) + x + 1, z + 1)
            at = (x + 1) * (SZ + 2) + z + 1
            base = side * Y_ROWS
            row4 = base + ((x + 2) * (SZ + 4) + z + 2) * 4
            row2 = base + Y_TWO + at * 2
            cells[pl.ds(pl.multiple_of(n * 8, 8), 8), :] = jnp.concatenate(
                [
                    rows[pl.ds(row4, 4), :],
                    rows[pl.ds(row2, 2), :],
                    rows[pl.ds(base + Y_SUM + at, 1), :],
                    jnp.zeros((1, 128), jnp.float32),
                ],
                axis=0,
            )
            return n + 1

        total = lax.fori_loop(0, lists[side * 8, 127], one, total)

    def near_list(s, own_cell):
        x, y, z = spots[0, s], spots[1, s], spots[2, s]
        high = y >= SY - 1
        outer = (y == -1) | (y == SY)
        base = jnp.where(outer, 2 * Y_ROWS, 0) + jnp.where(high, Y_ROWS, 0)
        for e, (ea, ed) in enumerate((p, q) for p in (-1, 0, 1) for q in (-1, 0, 1)):
            na, nd = x + ea, z + ed
            four[e] = base + ((na + 2) * (SZ + 4) + nd + 2) * 4
            use[e] = jnp.float32(1.0)
            if own_cell:
                two[e] = base + Y_TWO + ((na + 1) * (SZ + 2) + nd + 1) * 2
                word = flags[jnp.where(high, SX + 2, 0) + na + 1]
                use[e] = jnp.where(bit(word, nd + 1) > 0, jnp.float32(0.5), jnp.float32(1.0))

    def across_own(s, _):
        y = spots[1, s]

        @pl.when((y <= 0) | (y >= SY - 1))
        def _():
            near_list(s, True)
            spot = pl.multiple_of(s * 8, 8)
            tile = cells[pl.ds(spot, 8), :]
            count = jnp.int32(9)
            result = pairs("all", rows, four, two, use, count, tile, cols, table)
            final[s, 0:7] = final[s, 0:7] + result[0:7]
            cells[pl.ds(spot + 6, 1), :] = tile[6:7] + result[0:1]

        return 0

    def across_halo(s, _):
        y = spots[1, s]

        @pl.when((y <= 0) | (y >= SY - 1))
        def _():
            near_list(s, False)
            spot = pl.multiple_of(s * 8, 8)
            tile = cells[pl.ds(spot, 8), :]
            count = jnp.int32(9)
            result = pairs("density", rows, four, two, use, count, tile, cols, table)
            cells[pl.ds(spot + 6, 1), :] = tile[6:7] + result

        return 0

    lax.fori_loop(0, mine, across_own, 0)
    lax.fori_loop(mine, total, across_halo, 0)

    def weigh(q, _):
        base = pl.multiple_of(q * 64, 64)

        def get(c):
            return cells[pl.ds(base + c, 8, stride=8), :]

        good = get(3) > 0.0
        inv = 1.0 / jnp.where(good, get(4), 1.0)
        inv2 = inv * inv
        inv4 = inv2 * inv2
        fresh = (4.0 * KC) * (inv4 * inv4) * get(6)
        safe = jnp.where(good, fresh, 1.0)
        power = jnp.exp(jnp.log(safe) * (-1.0 / 3.0))
        weight = get(5) * power
        cells[pl.ds(base + 5, 8, stride=8), :] = jnp.where(good, weight, 0.0)
        cells[pl.ds(base + 6, 8, stride=8), :] = safe
        cells[pl.ds(base + 7, 8, stride=8), :] = power
        return 0

    lax.fori_loop(0, lax.div(total + 7, 8), weigh, 0)

    def last(s, _):
        x, y, z = spots[0, s], spots[1, s], spots[2, s]

        def check(t, n):
            close = (
                (jnp.abs(spots[0, t] - x) <= 1)
                & (jnp.abs(spots[1, t] - y) <= 1)
                & (jnp.abs(spots[2, t] - z) <= 1)
            )
            four[n] = t * 8
            two[n] = t * 8 + 4
            use[n] = jnp.float32(1.0)
            return n + close.astype(jnp.int32)

        count = lax.fori_loop(0, total, check, jnp.int32(0))
        spot = pl.multiple_of(s * 8, 8)
        tile = cells[pl.ds(spot, 8), :]
        result = final[s] + pairs("near", cells, four, two, use, count, tile, cols, table)
        good = tile[3:4] > 0.0
        own = final[s, 7:8] * tile[7:8]
        place = (x, y, pl.ds(z, 1), slice(None))
        density[place] = jnp.where(good, tile[6:7], old[place])
        for c in range(3):
            push = (20.0 * KC) * (own * final[s, 1 + c : 2 + c] + result[4 + c : 5 + c])
            accel[(c, *place)] = jnp.where(good, push, 0.0)
        return 0

    lax.fori_loop(0, mine, last, 0)


def f32(*shape):
    return jax.ShapeDtypeStruct(shape, jnp.float32)


def i32(*shape):
    return jax.ShapeDtypeStruct(shape, jnp.int32)


def neighbours(up, down, axis):
    size = lax.axis_size(axis)
    pairs_ = [(i, i + 1) for i in range(size - 1)]
    low = lax.ppermute(up, axis, pairs_)
    high = lax.ppermute(down, axis, [(j, i) for i, j in pairs_])
    return low, high


def work(flags, near):
    return [
        pltpu.SMEM((near,), jnp.int32),
        pltpu.SMEM((near,), jnp.int32),
        pltpu.SMEM((near,), jnp.float32),
        pltpu.SMEM((flags,), jnp.int32),
        pltpu.VMEM((4, 128, 128), jnp.float32),
        pltpu.VMEM((7, 128, 128), jnp.float32),
    ]


def cost(us):
    return pl.CostEstimate(flops=us * 10_000_000, bytes_accessed=us * 2_000_000, transcendentals=0)


def call(body, outs, out_specs, in_specs, scratch, us):
    return pl.pallas_call(
        body,
        out_shape=outs,
        in_specs=in_specs,
        out_specs=out_specs,
        scratch_shapes=scratch,
        compiler_params=PARAMS,
        cost_estimate=cost(us),
    )


def per_device(positions, mass, support, counts, entropy, density_old, active):
    small = [jnp.transpose(v, (1, 2, 0)) for v in (counts, active)]
    own, z_up, z_down, ids = call(
        pack,
        (f32(OWN_ROWS, S), f32(Z_ROWS, S), f32(Z_ROWS, S), i32(16)),
        (VMEM, VMEM, VMEM, SMEM),
        [ANY] * 7,
        [
            pltpu.SMEM((SY, SZ, SX), jnp.int32),
            pltpu.SMEM((SY, SZ, SX), jnp.int32),
            pltpu.VMEM((3, SX, SY, SZ, S), jnp.float32),
        ]
        + [pltpu.VMEM((SX, SY, SZ, S), jnp.float32)] * 4
        + [pltpu.SemaphoreType.DMA((7,))],
        2,
    )(*small, positions, mass, support, entropy, density_old)
    zlo, zhi = neighbours(z_up, z_down, "gz")
    first = call(
        local_first, f32(16, 8, S), VMEM, [SMEM, VMEM], work(SX * SY, 48), 8
    )(ids, own)
    x_up, x_down = call(
        pack_x, (f32(X_ROWS, S), f32(X_ROWS, S)), (VMEM, VMEM), [VMEM] * 3 + [ANY], [], 1
    )(own, zlo, zhi, first)
    xlo, xhi = neighbours(x_up, x_down, "gx")
    second = call(
        local_second,
        f32(16, 8, S),
        VMEM,
        [SMEM, VMEM, VMEM, ANY],
        work(SX * SY, 48),
        8,
    )(ids, own, first, x_up)
    y_up, y_down, tiles, sums, places = call(
        slab,
        (f32(Y_ROWS, S), f32(Y_ROWS, S), f32(SLAB_MOST, 8, S), f32(16, 8, S), i32(4, 128)),
        (VMEM, VMEM, VMEM, VMEM, SMEM),
        [SMEM] + [VMEM] * 6,
        [
            pltpu.VMEM((SLAB, S), jnp.float32),
            pltpu.VMEM((16, S), jnp.int32),
            pltpu.SMEM((16, S), jnp.int32),
            pltpu.SemaphoreType.DMA,
        ]
        + work((SX + 2) * SY, 48),
        4,
    )(ids, own, zlo, zhi, xlo, xhi, second)
    ylo, yhi = neighbours(y_up, y_down, "gy")
    return call(
        finish,
        (f32(SX, SY, SZ, S), f32(3, SX, SY, SZ, S)),
        (VMEM, VMEM),
        [SMEM] + [VMEM] * 7,
        [
            pltpu.VMEM((4 * Y_ROWS, S), jnp.float32),
            pltpu.VMEM((ALL_MOST * 8, S), jnp.float32),
            pltpu.VMEM((16, 8, S), jnp.float32),
            pltpu.SMEM((4, ALL_MOST), jnp.int32),
            pltpu.VMEM((16, S), jnp.int32),
            pltpu.SMEM((16, S), jnp.int32),
            pltpu.SemaphoreType.DMA,
        ]
        + work(2 * (SX + 2), ALL_MOST + 16),
        8,
    )(places, ylo, yhi, y_up, y_down, tiles, sums, density_old)


def solution(mesh):
    return jax.shard_map(
        per_device,
        mesh=mesh,
        in_specs=(
            P(None, "gx", "gy", "gz", None),
            P("gx", "gy", "gz", None),
            P("gx", "gy", "gz", None),
            P("gx", "gy", "gz"),
            P("gx", "gy", "gz", None),
            P("gx", "gy", "gz", None),
            P("gx", "gy", "gz"),
        ),
        out_specs=(P("gx", "gy", "gz", None), P(None, "gx", "gy", "gz", None)),
        check_vma=False,
    )
```

time: 118 us -> 80 us (0.68)
  the two profiles are of different devices: /device:TPU:352 before, /device:TPU:242 now
where the time goes in v3:
time: 80 us; the launch traced here: 79.5 us
  Pallas kernels  41.9 us (52%)
  starting transfers between devices  18.8 us (24%)
  waiting for transfers between devices  11.5 us (14%)
  local copies, waits for them, and re-layouts  6.49 us (8%)
    pallas_call x1, Pallas kernels, per_device(): call(finish, (f32(SX, SY, SZ, S), f32(3, SX, SY, SZ, S)), (VMEM, VMEM), [...  13.2 us
    pallas_call x1, Pallas kernels, per_device(): call(slab, (f32(Y_ROWS, S), f32(Y_ROWS, S), f32(SLAB_MOST, 8, S), f32(16,...  12 us
    ppermute x3, starting transfers between devices, neighbours(): low = lax.ppermute(up, axis, pairs_)  10 us
    ppermute x3, starting transfers between devices, neighbours(): high = lax.ppermute(down, axis, [(j, i) for i, j in pairs_])  8.82 us
    pallas_call x1, Pallas kernels, per_device(): call(local_first, f32(16, 8, S), VMEM, [SMEM, VMEM], work(SX * SY, 48), 8)  8.14 us
    ppermute x3, waiting for transfers between devices, neighbours(): low = lax.ppermute(up, axis, pairs_)  6.59 us
    unnamed x16, local copies, waits for them, and re-layouts  6.49 us
    ppermute x3, waiting for transfers between devices, neighbours(): high = lax.ppermute(down, axis, [(j, i) for i, j in pairs_])  4.92 us
  transfers between devices with their start and end apart: 6, of which 4 were waited for; matrix products, arithmetic and copies ran while one was open for 0% of the time, Pallas kernels for 16%

profile of v3, /device:TPU:242, one launch (start us, length us, event | category | flops | bytes accessed | tf_op | source)
XLA Modules:
  0.0 79.5 jit_solution(16682236618407619452)
XLA Ops:
  0.6 0.0 copy-start
  0.6 1.0 %copy-done = f32[12,6,6,128]{3,2,1,0:T(8,128)S(1)} copy-done((f32[12,6,6,128]{3,2,1,0:T(8,128)S(1)}, f32[12,6,6,128]{3,2,1,0:T(8,128)}, u32[]{:S(2)}) %copy-start) | copy-done | bytes 221208
  1.6 0.0 copy-start.2
  1.6 1.2 %copy-done.2 = f32[3,12,6,6,128]{4,3,2,1,0:T(8,128)S(1)} copy-done((f32[3,12,6,6,128]{4,3,2,1,0:T(8,128)S(1)}, f32[3,12,6,6,128]{4,3,2,1,0:T(8,128)}, u32[]{:S(2)}) %copy-start.2) | copy-done | bytes 663576
  2.8 0.0 copy-start.3
  2.8 1.0 %copy-done.3 = f32[12,6,6,128]{3,2,1,0:T(8,128)S(1)} copy-done((f32[12,6,6,128]{3,2,1,0:T(8,128)S(1)}, f32[12,6,6,128]{3,2,1,0:T(8,128)}, u32[]{:S(2)}) %copy-start.3) | copy-done | bytes 221208
  3.7 0.0 copy-start.4
  3.7 1.0 %copy-done.4 = f32[12,6,6,128]{3,2,1,0:T(8,128)S(1)} copy-done((f32[12,6,6,128]{3,2,1,0:T(8,128)S(1)}, f32[12,6,6,128]{3,2,1,0:T(8,128)}, u32[]{:S(2)}) %copy-start.4) | copy-done | bytes 221208
  4.7 0.0 copy-start.5
  4.7 1.0 %copy-done.5 = f32[12,6,6,128]{3,2,1,0:T(8,128)S(1)} copy-done((f32[12,6,6,128]{3,2,1,0:T(8,128)S(1)}, f32[12,6,6,128]{3,2,1,0:T(8,128)}, u32[]{:S(2)}) %copy-start.5) | copy-done | bytes 221208
  5.7 0.7 copy-done.6
  6.4 0.7 copy-done.7
  7.1 3.6 %shard_map.86 = (f32[3472,128]{1,0:T(8,128)S(1)}, f32[728,128]{1,0:T(8,128)S(1)}, f32[728,128]{1,0:T(8,128)S(1)}, s32[16]{0:T(128)S(1)}) custom-call(s32[6,6,12]{2,1,0:T(8,128)S(1)} %bitcast.2, s32[6,6,12]{2,1,0:T(8,128)S(1)} %bitcast.3, f32[3,12,6,6,128]{4,3,2,1,0:T(8,128)S(1)} %copy-done.2, f32[12,6,6,128]{3,2,1,0:T(8,128)S(1)} %copy-done.3, ...), custom_call_target="tpu_custom_call" | custom-call | flops 20000000 | bytes 4000000 | tf_op jit(solution)/shard_map/pallas_call | solution.py:676
  10.8 5.5 %collective-permute-start = (f32[728,128]{1,0:T(8,128)S(1)}, f32[728,128]{1,0:T(8,128)S(1)}, u32[]{:S(2)}, u32[]{:S(2)}) collective-permute-start(f32[728,128]{1,0:T(8,128)S(1)} %get-tuple-element.15), channel_id=1, source_target_pairs={{0,1},{1,2},{2,3},{3,4},{4,5},{5,6},{6,7},{8,9},{9,10},{10,11},{11... | collective-permute-start | bytes 1118216 | tf_op jit(solution)/shard_map/ppermute | solution.py:642
  16.3 1.9 %collective-permute-start.1 = (f32[728,128]{1,0:T(8,128)S(1)}, f32[728,128]{1,0:T(8,128)S(1)}, u32[]{:S(2)}, u32[]{:S(2)}) collective-permute-start(f32[728,128]{1,0:T(8,128)S(1)} %get-tuple-element.16), channel_id=1, source_target_pairs={{1,0},{2,1},{3,2},{4,3},{5,4},{6,5},{7,6},{9,8},{10,9},{11,10},{12... | collective-permute-start | bytes 1118216 | tf_op jit(solution)/shard_map/ppermute | solution.py:643
  18.2 8.1 %shard_map.87._.before = f32[16,8,128]{2,1,0:T(8,128)S(1)} custom-call(s32[16]{0:T(128)S(1)} %get-tuple-element.13.ids, f32[3472,128]{1,0:T(8,128)S(1)} %get-tuple-element.14.own), custom_call_target="tpu_custom_call" | custom-call | flops 80000000 | bytes 16000000 | tf_op jit(solution)/shard_map/pallas_call | solution.py:691
  26.3 0.0 collective-permute-done.zlo
  26.3 3.2 %collective-permute-done.1.zhi = f32[728,128]{1,0:T(8,128)S(1)} collective-permute-done((f32[728,128]{1,0:T(8,128)S(1)}, f32[728,128]{1,0:T(8,128)S(1)}, u32[]{:S(2)}, u32[]{:S(2)}) %collective-permute-start.1) | collective-permute-done | bytes 372768 | tf_op jit(solution)/shard_map/ppermute | solution.py:643
  29.5 0.1 shard_map.88
  29.6 3.3 %collective-permute-start.3 = (f32[584,128]{1,0:T(8,128)S(1)}, f32[584,128]{1,0:T(8,128)S(1)}, u32[]{:S(2)}, u32[]{:S(2)}) collective-permute-start(f32[584,128]{1,0:T(8,128)S(1)} %get-tuple-element.18), channel_id=1, source_target_pairs={{64,0},{128,64},{192,128},{256,192},{320,256},{384,320},{448,384},... | collective-permute-start | bytes 897032 | tf_op jit(solution)/shard_map/ppermute | solution.py:643
  32.9 2.6 %collective-permute-start.2 = (f32[584,128]{1,0:T(8,128)S(1)}, f32[584,128]{1,0:T(8,128)S(1)}, u32[]{:S(2)}, u32[]{:S(2)}) collective-permute-start(f32[584,128]{1,0:T(8,128)S(1)} %get-tuple-element.17._), channel_id=1, source_target_pairs={{0,64},{64,128},{128,192},{192,256},{256,320},{320,384},{384,448},... | collective-permute-start | bytes 897032 | tf_op jit(solution)/shard_map/ppermute | solution.py:642
  35.5 4.7 %shard_map.89.before = f32[16,8,128]{2,1,0:T(8,128)S(1)} custom-call(s32[16]{0:T(128)S(1)} %get-tuple-element.13.ids, f32[3472,128]{1,0:T(8,128)S(1)} %get-tuple-element.14.own, f32[16,8,128]{2,1,0:T(8,128)S(1)} %shard_map.87._.before, f32[584,128]{1,0:T(8,128)S(1)} %get-tuple-element.17._), custom_call_target="tpu_custom_call" | custom-call | flops 80000000 | bytes 16000000 | tf_op jit(solution)/shard_map/pallas_call | solution.py:698
  40.2 0.0 copy-start.1
  40.3 0.0 collective-permute-done.3.xhi
  40.3 1.9 %collective-permute-done.2.xlo = f32[584,128]{1,0:T(8,128)S(1)} collective-permute-done((f32[584,128]{1,0:T(8,128)S(1)}, f32[584,128]{1,0:T(8,128)S(1)}, u32[]{:S(2)}, u32[]{:S(2)}) %collective-permute-start.2) | collective-permute-done | bytes 299040 | tf_op jit(solution)/shard_map/ppermute | solution.py:642
  42.2 12.0 %shard_map.90 = (f32[984,128]{1,0:T(8,128)S(1)}, f32[984,128]{1,0:T(8,128)S(1)}, f32[96,8,128]{2,1,0:T(8,128)S(1)}, f32[16,8,128]{2,1,0:T(8,128)S(1)}, s32[4,128]{1,0:T(4,128)S(1)}) custom-call(s32[16]{0:T(128)S(1)} %get-tuple-element.13.ids, f32[3472,128]{1,0:T(8,128)S(1)} %get-tuple-element.14.own, f32[728,128]{1,0:T(8,128)S(1)} %collective-permute-done.zlo, ...), custom_call_target="tpu_custom_call" | custom-call | flops 40000000 | bytes 8000000 | tf_op jit(solution)/shard_map/pallas_call | solution.py:706
  54.2 1.9 %collective-permute-start.4 = (f32[984,128]{1,0:T(8,128)S(1)}, f32[984,128]{1,0:T(8,128)S(1)}, u32[]{:S(2)}, u32[]{:S(2)}) collective-permute-start(f32[984,128]{1,0:T(8,128)S(1)} %get-tuple-element.20.up), channel_id=1, source_target_pairs={{0,8},{8,16},{16,24},{24,32},{32,40},{40,48},{48,56},{1,9},{9,17},... | collective-permute-start | bytes 1511432 | tf_op jit(solution)/shard_map/ppermute | solution.py:642
  56.1 3.6 %collective-permute-start.5 = (f32[984,128]{1,0:T(8,128)S(1)}, f32[984,128]{1,0:T(8,128)S(1)}, u32[]{:S(2)}, u32[]{:S(2)}) collective-permute-start(f32[984,128]{1,0:T(8,128)S(1)} %get-tuple-element.21.down), channel_id=1, source_target_pairs={{8,0},{16,8},{24,16},{32,24},{40,32},{48,40},{56,48},{9,1},{17,9},... | collective-permute-start | bytes 1511432 | tf_op jit(solution)/shard_map/ppermute | solution.py:643
  59.8 4.7 %collective-permute-done.4.ylo = f32[984,128]{1,0:T(8,128)S(1)} collective-permute-done((f32[984,128]{1,0:T(8,128)S(1)}, f32[984,128]{1,0:T(8,128)S(1)}, u32[]{:S(2)}, u32[]{:S(2)}) %collective-permute-start.4) | collective-permute-done | bytes 503840 | tf_op jit(solution)/shard_map/ppermute | solution.py:642
  64.5 1.8 %collective-permute-done.5.yhi = f32[984,128]{1,0:T(8,128)S(1)} collective-permute-done((f32[984,128]{1,0:T(8,128)S(1)}, f32[984,128]{1,0:T(8,128)S(1)}, u32[]{:S(2)}, u32[]{:S(2)}) %collective-permute-start.5) | collective-permute-done | bytes 503840 | tf_op jit(solution)/shard_map/ppermute | solution.py:643
  66.2 0.0 copy-done.1
  66.2 13.2 %shard_map.91 = (f32[12,6,6,128]{3,2,1,0:T(8,128)}, f32[3,12,6,6,128]{4,3,2,1,0:T(8,128)}) custom-call(s32[4,128]{1,0:T(4,128)S(1)} %get-tuple-element.19.places, f32[984,128]{1,0:T(8,128)S(1)} %collective-permute-done.4.ylo, f32[984,128]{1,0:T(8,128)S(1)} %collective-permute-done.5.yhi, f32[984,128]{1,0:T(8,128)S(1)} %get-tuple-element.20.up, ...), custom_call_target="tpu_custom_call" | custom-call | flops 80000000 | bytes 16000000 | tf_op jit(solution)/shard_map/pallas_call | solution.py:721
  (2 shorter events, 0.0 us)
Async XLA Ops:
  0.6 1.0 %copy-start = (f32[12,6,6,128]{3,2,1,0:T(8,128)S(1)}, f32[12,6,6,128]{3,2,1,0:T(8,128)}, u32[]{:S(2)}) copy-start(f32[12,6,6,128]{3,2,1,0:T(8,128)} %old.1) | copy-start | bytes 663556
  1.6 1.2 %copy-start.2 = (f32[3,12,6,6,128]{4,3,2,1,0:T(8,128)S(1)}, f32[3,12,6,6,128]{4,3,2,1,0:T(8,128)}, u32[]{:S(2)}) copy-start(f32[3,12,6,6,128]{4,3,2,1,0:T(8,128)} %pos_in.1) | copy-start | bytes 1990660
  2.8 1.0 %copy-start.3 = (f32[12,6,6,128]{3,2,1,0:T(8,128)S(1)}, f32[12,6,6,128]{3,2,1,0:T(8,128)}, u32[]{:S(2)}) copy-start(f32[12,6,6,128]{3,2,1,0:T(8,128)} %mass_in.1) | copy-start | bytes 663556
  3.7 1.0 %copy-start.4 = (f32[12,6,6,128]{3,2,1,0:T(8,128)S(1)}, f32[12,6,6,128]{3,2,1,0:T(8,128)}, u32[]{:S(2)}) copy-start(f32[12,6,6,128]{3,2,1,0:T(8,128)} %support_in.1) | copy-start | bytes 663556
  4.7 1.0 %copy-start.5 = (f32[12,6,6,128]{3,2,1,0:T(8,128)S(1)}, f32[12,6,6,128]{3,2,1,0:T(8,128)}, u32[]{:S(2)}) copy-start(f32[12,6,6,128]{3,2,1,0:T(8,128)} %entropy_in.1) | copy-start | bytes 663556
  5.7 0.7 copy-start.6
  6.4 0.7 copy-start.7
  10.8 15.6 %collective-permute-start = (f32[728,128]{1,0:T(8,128)S(1)}, f32[728,128]{1,0:T(8,128)S(1)}, u32[]{:S(2)}, u32[]{:S(2)}) collective-permute-start(f32[728,128]{1,0:T(8,128)S(1)} %get-tuple-element.15), channel_id=1, source_target_pairs={{0,1},{1,2},{2,3},{3,4},{4,5},{5,6},{6,7},{8,9},{9,10},{10,11},{11... | collective-permute-start | bytes 1118216 | tf_op jit(solution)/shard_map/ppermute | solution.py:642
  16.3 13.2 %collective-permute-start.1 = (f32[728,128]{1,0:T(8,128)S(1)}, f32[728,128]{1,0:T(8,128)S(1)}, u32[]{:S(2)}, u32[]{:S(2)}) collective-permute-start(f32[728,128]{1,0:T(8,128)S(1)} %get-tuple-element.16), channel_id=1, source_target_pairs={{1,0},{2,1},{3,2},{4,3},{5,4},{6,5},{7,6},{9,8},{10,9},{11,10},{12... | collective-permute-start | bytes 1118216 | tf_op jit(solution)/shard_map/ppermute | solution.py:643
  29.6 10.6 %collective-permute-start.3 = (f32[584,128]{1,0:T(8,128)S(1)}, f32[584,128]{1,0:T(8,128)S(1)}, u32[]{:S(2)}, u32[]{:S(2)}) collective-permute-start(f32[584,128]{1,0:T(8,128)S(1)} %get-tuple-element.18), channel_id=1, source_target_pairs={{64,0},{128,64},{192,128},{256,192},{320,256},{384,320},{448,384},... | collective-permute-start | bytes 897032 | tf_op jit(solution)/shard_map/ppermute | solution.py:643
  32.9 9.3 %collective-permute-start.2 = (f32[584,128]{1,0:T(8,128)S(1)}, f32[584,128]{1,0:T(8,128)S(1)}, u32[]{:S(2)}, u32[]{:S(2)}) collective-permute-start(f32[584,128]{1,0:T(8,128)S(1)} %get-tuple-element.17._), channel_id=1, source_target_pairs={{0,64},{64,128},{128,192},{192,256},{256,320},{320,384},{384,448},... | collective-permute-start | bytes 897032 | tf_op jit(solution)/shard_map/ppermute | solution.py:642
  40.2 26.0 %copy-start.1 = (f32[12,6,6,128]{3,2,1,0:T(8,128)S(1)}, f32[12,6,6,128]{3,2,1,0:T(8,128)}, u32[]{:S(2)}) copy-start(f32[12,6,6,128]{3,2,1,0:T(8,128)} %old.1) | copy-start | bytes 663556
  54.2 10.3 %collective-permute-start.4 = (f32[984,128]{1,0:T(8,128)S(1)}, f32[984,128]{1,0:T(8,128)S(1)}, u32[]{:S(2)}, u32[]{:S(2)}) collective-permute-start(f32[984,128]{1,0:T(8,128)S(1)} %get-tuple-element.20.up), channel_id=1, source_target_pairs={{0,8},{8,16},{16,24},{24,32},{32,40},{40,48},{48,56},{1,9},{9,17},... | collective-permute-start | bytes 1511432 | tf_op jit(solution)/shard_map/ppermute | solution.py:642
  56.1 10.1 %collective-permute-start.5 = (f32[984,128]{1,0:T(8,128)S(1)}, f32[984,128]{1,0:T(8,128)S(1)}, u32[]{:S(2)}, u32[]{:S(2)}) collective-permute-start(f32[984,128]{1,0:T(8,128)S(1)} %get-tuple-element.21.down), channel_id=1, source_target_pairs={{8,0},{16,8},{24,16},{32,24},{40,32},{48,40},{56,48},{9,1},{17,9},... | collective-permute-start | bytes 1511432 | tf_op jit(solution)/shard_map/ppermute | solution.py:643

commit v4 on v3

--- a/solution.py
+++ b/solution.py
@@ -334,80 +334,15 @@
     return four, base + X_TWO + (y * (SZ + 2) + z + 1) * 2
 
 
-def slab(
-    ids, own, zlo, zhi, xlo, xhi, before, up, down, tiles, sums, places,
-    rows, tails, lists, sem, four, two, use, flags, cols, table,
-):
+def gather(rows, own, zlo, zhi, xlo, xhi):
     rows[0:OWN_ROWS] = own[...]
     rows[ZLO:ZHI] = zlo[...]
     rows[ZHI:XLO] = zhi[...]
     rows[XLO:XHI] = xlo[...]
     rows[XHI:SLAB] = xhi[...]
-    tails[...] = jnp.zeros(tails.shape, jnp.int32)
-    tails[0:1] = own[OWN_TAIL : OWN_TAIL + 1].astype(jnp.int32)
-    tails[1:2] = zlo[Z_TAIL : Z_TAIL + 1].astype(jnp.int32)
-    tails[2:3] = zhi[Z_TAIL : Z_TAIL + 1].astype(jnp.int32)
-    tails[3:6] = xlo[X_TAIL : X_TAIL + 3].astype(jnp.int32)
-    tails[6:9] = xhi[X_TAIL : X_TAIL + 3].astype(jnp.int32)
-    copy = pltpu.make_async_copy(tails, lists, sem)
-    copy.start()
-
-    clear(flags, (SX + 2) * SY)
-    for out, y in ((up, SY - 1), (down, 0)):
-        for x in range(-2, SX + 2):
-            for z in range(-2, SZ + 2):
-                row4, row2 = slab_rows_at(x, y, z)
-                spot = ((x + 2) * (SZ + 4) + z + 2) * 4
-                out[spot : spot + 4] = rows[row4 : row4 + 4]
-                if -1 <= x <= SX and -1 <= z <= SZ:
-                    spot = Y_TWO + ((x + 1) * (SZ + 2) + z + 1) * 2
-                    out[spot : spot + 2] = rows[row2 : row2 + 2]
-        out[Y_SUM:Y_TAIL] = jnp.zeros((Y_TAIL - Y_SUM, 128), jnp.float32)
-    copy.wait()
-
-    number = jnp.int32(0)
-    for q, (bx, bz) in enumerate(BLOCKS):
-
-        def one(s, n, q=q, bx=bx, bz=bz):
-            a, b, d = corner(lists[q, s])
-            x, z = a + bx * SX, d + bz * SZ
-            inside = (x >= -1) & (x <= SX) & (z >= -1) & (z <= SZ)
-            places[0, n] = x
-            places[1, n] = b
-            places[2, n] = z
-
-            @pl.when(inside)
-            def _():
-                mark(flags, (x + 1) * SY + b, z + 1)
-
-            return n + inside.astype(jnp.int32)
-
-        number = lax.fori_loop(0, lists[q, 15], one, number)
-    places[3, 0] = number
-    places[3, 1] = lists[0, 15]
-    mine = lists[0, 15]
-
-    lane = lax.broadcasted_iota(jnp.int32, (8, 128), 1)
-    line = lax.broadcasted_iota(jnp.int32, (8, 128), 0)
-
-    def tell(s, state):
-        lists_, numbers = list(state[0]), list(state[1])
-        x, y, z = places[0, s], places[1, s], places[2, s]
-        for n, edge in enumerate((SY - 1, 0)):
-            here = y == edge
-            at = jnp.where(here, numbers[n], 126)
-            value = jnp.where(line == 0, x, z)
-            lists_[n] = jnp.where(lane == at, value, lists_[n])
-            numbers[n] = numbers[n] + here.astype(jnp.int32)
-        return tuple(lists_), tuple(numbers)
-
-    nothing = jnp.zeros((8, 128), jnp.int32)
-    told, numbers = lax.fori_loop(
-        0, number, tell, ((nothing, nothing), (jnp.int32(0), jnp.int32(0)))
-    )
-    for n, out in enumerate((up, down)):
-        out[Y_TAIL:Y_ROWS] = jnp.where(lane == 127, numbers[n], told[n]).astype(jnp.float32)
-
+
+
+def slab_tools(rows, four, two, use, flags, cols, table):
     def near_list(x, y, z, own_cell):
         count = jnp.int32(0)
         for ea in (-1, 0, 1):
@@ -437,6 +372,98 @@
         second = rows[pl.ds(f2 + y * add2, 2), :]
         return jnp.concatenate([first, second, jnp.zeros((2, 128), jnp.float32)], axis=0)
 
+    def own_sums(x, y, z):
+        count = near_list(x, y, z, True)
+        return pairs("all", rows, four, two, use, count, cell(x, y, z), cols, table)
+
+    def halo_cell(x, y, z):
+        count = near_list(x, y, z, False)
+        tile = cell(x, y, z)
+        return tile, pairs("density", rows, four, two, use, count, tile, cols, table)
+
+    return own_sums, halo_cell
+
+
+def on_border(x, z):
+    return (x == 0) | (x == SX - 1) | (z == 0) | (z == SZ - 1)
+
+
+def on_face(y):
+    return (y == 0) | (y == SY - 1)
+
+
+def slab_faces(
+    ids, own, zlo, zhi, xlo, xhi, before, up, down, tiles, sums, places,
+    rows, tails, lists, sem, four, two, use, flags, cols, table,
+):
+    tails[...] = jnp.zeros(tails.shape, jnp.int32)
+    tails[0:1] = own[OWN_TAIL : OWN_TAIL + 1].astype(jnp.int32)
+    tails[1:2] = zlo[Z_TAIL : Z_TAIL + 1].astype(jnp.int32)
+    tails[2:3] = zhi[Z_TAIL : Z_TAIL + 1].astype(jnp.int32)
+    tails[3:6] = xlo[X_TAIL : X_TAIL + 3].astype(jnp.int32)
+    tails[6:9] = xhi[X_TAIL : X_TAIL + 3].astype(jnp.int32)
+    copy = pltpu.make_async_copy(tails, lists, sem)
+    copy.start()
+    gather(rows, own, zlo, zhi, xlo, xhi)
+
+    clear(flags, (SX + 2) * SY)
+    for out, y in ((up, SY - 1), (down, 0)):
+        for x in range(-2, SX + 2):
+            for z in range(-2, SZ + 2):
+                row4, row2 = slab_rows_at(x, y, z)
+                spot = ((x + 2) * (SZ + 4) + z + 2) * 4
+                out[spot : spot + 4] = rows[row4 : row4 + 4]
+                if -1 <= x <= SX and -1 <= z <= SZ:
+                    spot = Y_TWO + ((x + 1) * (SZ + 2) + z + 1) * 2
+                    out[spot : spot + 2] = rows[row2 : row2 + 2]
+        out[Y_SUM:Y_TAIL] = jnp.zeros((Y_TAIL - Y_SUM, 128), jnp.float32)
+    copy.wait()
+
+    number = jnp.int32(0)
+    for q, (bx, bz) in enumerate(BLOCKS):
+
+        def one(s, n, q=q, bx=bx, bz=bz):
+            a, b, d = corner(lists[q, s])
+            x, z = a + bx * SX, d + bz * SZ
+            inside = (x >= -1) & (x <= SX) & (z >= -1) & (z <= SZ)
+            places[0, n] = x
+            places[1, n] = b
+            places[2, n] = z
+
+            @pl.when(inside)
+            def _():
+                mark(flags, (x + 1) * SY + b, z + 1)
+
+            return n + inside.astype(jnp.int32)
+
+        number = lax.fori_loop(0, lists[q, 15], one, number)
+    places[3, 0] = number
+    places[3, 1] = lists[0, 15]
+    mine = lists[0, 15]
+
+    lane = lax.broadcasted_iota(jnp.int32, (8, 128), 1)
+    line = lax.broadcasted_iota(jnp.int32, (8, 128), 0)
+
+    def tell(s, state):
+        lists_, numbers = list(state[0]), list(state[1])
+        x, y, z = places[0, s], places[1, s], places[2, s]
+        for n, edge in enumerate((SY - 1, 0)):
+            here = y == edge
+            at = jnp.where(here, numbers[n], 126)
+            value = jnp.where(line == 0, x, z)
+            lists_[n] = jnp.where(lane == at, value, lists_[n])
+            numbers[n] = numbers[n] + here.astype(jnp.int32)
+        return tuple(lists_), tuple(numbers)
+
+    nothing = jnp.zeros((8, 128), jnp.int32)
+    told, numbers = lax.fori_loop(
+        0, number, tell, ((nothing, nothing), (jnp.int32(0), jnp.int32(0)))
+    )
+    for n, out in enumerate((up, down)):
+        out[Y_TAIL:Y_ROWS] = jnp.where(lane == 127, numbers[n], told[n]).astype(jnp.float32)
+
+    own_sums, halo_cell = slab_tools(rows, four, two, use, flags, cols, table)
+
     def send_sum(s, x, y, z):
         spot = Y_SUM + (x + 1) * (SZ + 2) + z + 1
 
@@ -451,28 +478,75 @@
     def own_slot(s, _):
         x, y, z = places[0, s], places[1, s], places[2, s]
         sums[s] = before[s]
-
-        @pl.when((x == 0) | (x == SX - 1) | (z == 0) | (z == SZ - 1))
-        def _():
-            count = near_list(x, y, z, True)
-            tile = cell(x, y, z)
-            sums[s] = sums[s] + pairs("all", rows, four, two, use, count, tile, cols, table)
-
         row = pl.multiple_of(own_row(x, y, z), 8)
         whole = rows[pl.ds(row, 8), :]
         tiles[s] = whole
-        tiles[s, 6:7] = sums[s, 0:1]
+
+        @pl.when(on_face(y))
+        def _():
+            @pl.when(on_border(x, z))
+            def _():
+                sums[s] = sums[s] + own_sums(x, y, z)
+
+            tiles[s, 6:7] = sums[s, 0:1]
+            send_sum(s, x, y, z)
+
         sums[s, 7:8] = whole[6:7]
-        send_sum(s, x, y, z)
         return 0
 
     def halo_slot(s, _):
         x, y, z = places[0, s], places[1, s], places[2, s]
-        count = near_list(x, y, z, False)
-        tile = cell(x, y, z)
-        tiles[s] = tile
-        tiles[s, 6:7] = pairs("density", rows, four, two, use, count, tile, cols, table)
-        send_sum(s, x, y, z)
+
+        @pl.when(on_face(y))
+        def _():
+            tiles[s], total = halo_cell(x, y, z)
+            tiles[s, 6:7] = total
+            send_sum(s, x, y, z)
+
+        return 0
+
+    lax.fori_loop(0, mine, own_slot, 0)
+    lax.fori_loop(mine, number, halo_slot, 0)
+
+
+def slab_inside(
+    places, own, zlo, zhi, xlo, xhi, tiles_in, sums_in, tiles, sums,
+    rows, four, two, use, flags, cols, table,
+):
+    gather(rows, own, zlo, zhi, xlo, xhi)
+    tiles[...] = tiles_in[...]
+    sums[...] = sums_in[...]
+    number, mine = places[3, 0], places[3, 1]
+    clear(flags, (SX + 2) * SY)
+
+    def one(s, _):
+        mark(flags, (places[0, s] + 1) * SY + places[1, s], places[2, s] + 1)
+        return 0
+
+    lax.fori_loop(0, number, one, 0)
+    own_sums, halo_cell = slab_tools(rows, four, two, use, flags, cols, table)
+
+    def own_slot(s, _):
+        x, y, z = places[0, s], places[1, s], places[2, s]
+
+        @pl.when(jnp.logical_not(on_face(y)))
+        def _():
+            @pl.when(on_border(x, z))
+            def _():
+                sums[s, 0:7] = sums[s, 0:7] + own_sums(x, y, z)[0:7]
+
+            tiles[s, 6:7] = sums[s, 0:1]
+
+        return 0
+
+    def halo_slot(s, _):
+        x, y, z = places[0, s], places[1, s], places[2, s]
+
+        @pl.when(jnp.logical_not(on_face(y)))
+        def _():
+            tiles[s], total = halo_cell(x, y, z)
+            tiles[s, 6:7] = total
+
         return 0
 
     lax.fori_loop(0, mine, own_slot, 0)
@@ -659,14 +733,14 @@
     return pl.CostEstimate(flops=us * 10_000_000, bytes_accessed=us * 2_000_000, transcendentals=0)
 
 
-def call(body, outs, out_specs, in_specs, scratch, us):
+def call(body, outs, out_specs, in_specs, scratch, us, limit=40):
     return pl.pallas_call(
         body,
         out_shape=outs,
         in_specs=in_specs,
         out_specs=out_specs,
         scratch_shapes=scratch,
-        compiler_params=PARAMS,
+        compiler_params=pltpu.CompilerParams(vmem_limit_bytes=limit * 1024 * 1024),
         cost_estimate=cost(us),
     )
 
@@ -686,6 +760,7 @@
         + [pltpu.VMEM((SX, SY, SZ, S), jnp.float32)] * 4
         + [pltpu.SemaphoreType.DMA((7,))],
         2,
+        56,
     )(*small, positions, mass, support, entropy, density_old)
     zlo, zhi = neighbours(z_up, z_down, "gz")
     first = call(
@@ -704,7 +779,7 @@
         8,
     )(ids, own, first, x_up)
     y_up, y_down, tiles, sums, places = call(
-        slab,
+        slab_faces,
         (f32(Y_ROWS, S), f32(Y_ROWS, S), f32(SLAB_MOST, 8, S), f32(16, 8, S), i32(4, 128)),
         (VMEM, VMEM, VMEM, VMEM, SMEM),
         [SMEM] + [VMEM] * 6,
@@ -718,6 +793,14 @@
         4,
     )(ids, own, zlo, zhi, xlo, xhi, second)
     ylo, yhi = neighbours(y_up, y_down, "gy")
+    tiles, sums = call(
+        slab_inside,
+        (f32(SLAB_MOST, 8, S), f32(16, 8, S)),
+        (VMEM, VMEM),
+        [SMEM] + [VMEM] * 7,
+        [pltpu.VMEM((SLAB, S), jnp.float32)] + work((SX + 2) * SY, 48),
+        6,
+    )(places, own, zlo, zhi, xlo, xhi, tiles, sums)
     return call(
         finish,
         (f32(SX, SY, SZ, S), f32(3, SX, SY, SZ, S)),

time: 80 us -> 74.2 us (0.927)
  the two profiles are of different devices: /device:TPU:242 before, /device:TPU:452 now
where the time goes in v4:
time: 74.2 us; the launch traced here: 73.9 us
  Pallas kernels  53.7 us (72%)
  starting transfers between devices  17.3 us (23%)
  local copies, waits for them, and re-layouts  2.13 us (3%)
  between operations  0.78 us (1%)
    pallas_call x1, Pallas kernels, per_device(): call(finish, (f32(SX, SY, SZ, S), f32(3, SX, SY, SZ, S)), (VMEM, VMEM), [...  16.1 us
    pallas_call x1, Pallas kernels, per_device(): call(local_first, f32(16, 8, S), VMEM, [SMEM, VMEM], work(SX * SY, 48), 8)  12.7 us
    ppermute x3, starting transfers between devices, neighbours(): high = lax.ppermute(down, axis, [(j, i) for i, j in pairs_])  9.5 us
    pallas_call x1, Pallas kernels, per_device(): call(local_second, f32(16, 8, S), VMEM, [SMEM, VMEM, VMEM, ANY], work(SX...  7.99 us
    ppermute x3, starting transfers between devices, neighbours(): low = lax.ppermute(up, axis, pairs_)  7.78 us
    pallas_call x1, Pallas kernels, per_device(): call(slab_inside, (f32(SLAB_MOST, 8, S), f32(16, 8, S)), (VMEM, VMEM), [S...  6.98 us
    pallas_call x1, Pallas kernels, per_device(): call(slab_faces, (f32(Y_ROWS, S), f32(Y_ROWS, S), f32(SLAB_MOST, 8, S), f...  5.03 us
    pallas_call x1, Pallas kernels, per_device(): call(pack, (f32(OWN_ROWS, S), f32(Z_ROWS, S), f32(Z_ROWS, S), i32(16)), (...  4.68 us
  transfers between devices with their start and end apart: 6, of which 0 were waited for; matrix products, arithmetic and copies ran while one was open for 0% of the time, Pallas kernels for 37%

profile of v4, /device:TPU:452, one launch (start us, length us, event | category | flops | bytes accessed | tf_op | source)
XLA Modules:
  0.0 73.9 jit_solution(18058325663212174853)
XLA Ops:
  0.6 4.7 %shard_map.86 = (f32[3472,128]{1,0:T(8,128)}, f32[728,128]{1,0:T(8,128)}, f32[728,128]{1,0:T(8,128)}, s32[16]{0:T(128)}) custom-call(s32[6,6,12]{2,1,0:T(8,128)} %bitcast.2, s32[6,6,12]{2,1,0:T(8,128)} %bitcast.3, f32[3,12,6,6,128]{4,3,2,1,0:T(8,128)} %pos_in.1, f32[12,6,6,128]{3,2,1,0:T(8,128)} %mass_in.1, f32[12,6,6,128]{3,2,1,0:T(8,128)} %support_in.1, ...), custom_call_target="tpu_custom_call" | custom-call | flops 20000000 | bytes 4000000 | tf_op jit(solution)/shard_map/pallas_call | solution.py:750
  5.3 1.3 %collective-permute-start = (f32[728,128]{1,0:T(8,128)}, f32[728,128]{1,0:T(8,128)S(1)}, u32[]{:S(2)}, u32[]{:S(2)}) collective-permute-start(f32[728,128]{1,0:T(8,128)} %get-tuple-element.17), channel_id=1, source_target_pairs={{0,1},{1,2},{2,3},{3,4},{4,5},{5,6},{6,7},{8,9},{9,10},{10,11},{11... | collective-permute-start | bytes 1118216 | tf_op jit(solution)/shard_map/ppermute | solution.py:716
  6.6 4.6 %collective-permute-start.1 = (f32[728,128]{1,0:T(8,128)}, f32[728,128]{1,0:T(8,128)S(1)}, u32[]{:S(2)}, u32[]{:S(2)}) collective-permute-start(f32[728,128]{1,0:T(8,128)} %get-tuple-element.18), channel_id=1, source_target_pairs={{1,0},{2,1},{3,2},{4,3},{5,4},{6,5},{7,6},{9,8},{10,9},{11,10},{12... | collective-permute-start | bytes 1118216 | tf_op jit(solution)/shard_map/ppermute | solution.py:717
  11.2 0.0 copy-start
  11.2 1.5 %copy-done = f32[3472,128]{1,0:T(8,128)S(1)} copy-done((f32[3472,128]{1,0:T(8,128)S(1)}, f32[3472,128]{1,0:T(8,128)}, u32[]{:S(2)}) %copy-start) | copy-done | bytes 1777688
  12.7 0.0 copy-start.2
  12.7 0.7 copy-done.2
  13.3 12.7 %shard_map.87._.before = f32[16,8,128]{2,1,0:T(8,128)S(1)} custom-call(s32[16]{0:T(128)S(1)} %copy-done.2, f32[3472,128]{1,0:T(8,128)S(1)} %copy-done), custom_call_target="tpu_custom_call" | custom-call | flops 80000000 | bytes 16000000 | tf_op jit(solution)/shard_map/pallas_call | solution.py:766
  26.0 0.0 collective-permute-done.zlo
  26.1 0.0 collective-permute-done.1.zhi
  26.1 0.1 shard_map.88
  26.2 1.3 %collective-permute-start.3 = (f32[584,128]{1,0:T(8,128)S(1)}, f32[584,128]{1,0:T(8,128)S(1)}, u32[]{:S(2)}, u32[]{:S(2)}) collective-permute-start(f32[584,128]{1,0:T(8,128)S(1)} %get-tuple-element.20), channel_id=1, source_target_pairs={{64,0},{128,64},{192,128},{256,192},{320,256},{384,320},{448,384},... | collective-permute-start | bytes 897032 | tf_op jit(solution)/shard_map/ppermute | solution.py:717
  27.5 4.6 %collective-permute-start.2 = (f32[584,128]{1,0:T(8,128)S(1)}, f32[584,128]{1,0:T(8,128)S(1)}, u32[]{:S(2)}, u32[]{:S(2)}) collective-permute-start(f32[584,128]{1,0:T(8,128)S(1)} %get-tuple-element.19._), channel_id=1, source_target_pairs={{0,64},{64,128},{128,192},{192,256},{256,320},{320,384},{384,448},... | collective-permute-start | bytes 897032 | tf_op jit(solution)/shard_map/ppermute | solution.py:716
  32.1 8.0 %shard_map.89.before = f32[16,8,128]{2,1,0:T(8,128)S(1)} custom-call(s32[16]{0:T(128)S(1)} %copy-done.2, f32[3472,128]{1,0:T(8,128)S(1)} %copy-done, f32[16,8,128]{2,1,0:T(8,128)S(1)} %shard_map.87._.before, f32[584,128]{1,0:T(8,128)S(1)} %get-tuple-element.19._), custom_call_target="tpu_custom_call" | custom-call | flops 80000000 | bytes 16000000 | tf_op jit(solution)/shard_map/pallas_call | solution.py:773
  40.1 0.0 collective-permute-done.3.xhi
  40.1 0.0 collective-permute-done.2.xlo
  40.1 5.0 %shard_map.90 = (f32[984,128]{1,0:T(8,128)S(1)}, f32[984,128]{1,0:T(8,128)S(1)}, f32[96,8,128]{2,1,0:T(8,128)S(1)}, f32[16,8,128]{2,1,0:T(8,128)S(1)}, s32[4,128]{1,0:T(4,128)S(1)}) custom-call(s32[16]{0:T(128)S(1)} %copy-done.2, f32[3472,128]{1,0:T(8,128)S(1)} %copy-done, f32[728,128]{1,0:T(8,128)S(1)} %collective-permute-done.zlo, ...), custom_call_target="tpu_custom_call" | custom-call | flops 40000000 | bytes 8000000 | tf_op jit(solution)/shard_map/pallas_call | solution.py:781
  45.1 1.9 %collective-permute-start.4 = (f32[984,128]{1,0:T(8,128)S(1)}, f32[984,128]{1,0:T(8,128)S(1)}, u32[]{:S(2)}, u32[]{:S(2)}) collective-permute-start(f32[984,128]{1,0:T(8,128)S(1)} %get-tuple-element.22.up), channel_id=1, source_target_pairs={{0,8},{8,16},{16,24},{24,32},{32,40},{40,48},{48,56},{1,9},{9,17},... | collective-permute-start | bytes 1511432 | tf_op jit(solution)/shard_map/ppermute | solution.py:716
  47.1 3.6 %collective-permute-start.5 = (f32[984,128]{1,0:T(8,128)S(1)}, f32[984,128]{1,0:T(8,128)S(1)}, u32[]{:S(2)}, u32[]{:S(2)}) collective-permute-start(f32[984,128]{1,0:T(8,128)S(1)} %get-tuple-element.23.down), channel_id=1, source_target_pairs={{8,0},{16,8},{24,16},{32,24},{40,32},{48,40},{56,48},{9,1},{17,9},... | collective-permute-start | bytes 1511432 | tf_op jit(solution)/shard_map/ppermute | solution.py:717
  50.7 0.0 copy-start.1
  50.7 7.0 %shard_map.91 = (f32[96,8,128]{2,1,0:T(8,128)S(1)}, f32[16,8,128]{2,1,0:T(8,128)S(1)}) custom-call(s32[4,128]{1,0:T(4,128)S(1)} %get-tuple-element.21.places, f32[3472,128]{1,0:T(8,128)S(1)} %copy-done, f32[728,128]{1,0:T(8,128)S(1)} %collective-permute-done.zlo, f32[728,128]{1,0:T(8,128)S(1)} %collective-permute-done.1.zhi, ...), custom_call_target="tpu_custom_call" | custom-call | flops 60000000 | bytes 12000000 | tf_op jit(solution)/shard_map/pallas_call | solution.py:796
  57.7 0.0 collective-permute-done.4.ylo
  57.7 0.0 collective-permute-done.5.yhi
  57.7 0.0 copy-done.1
  57.7 16.1 %shard_map.92 = (f32[12,6,6,128]{3,2,1,0:T(8,128)}, f32[3,12,6,6,128]{4,3,2,1,0:T(8,128)}) custom-call(s32[4,128]{1,0:T(4,128)S(1)} %get-tuple-element.21.places, f32[984,128]{1,0:T(8,128)S(1)} %collective-permute-done.4.ylo, f32[984,128]{1,0:T(8,128)S(1)} %collective-permute-done.5.yhi, f32[984,128]{1,0:T(8,128)S(1)} %get-tuple-element.22.up, ...), custom_call_target="tpu_custom_call" | custom-call | flops 80000000 | bytes 16000000 | tf_op jit(solution)/shard_map/pallas_call | solution.py:804
Async XLA Ops:
  5.3 20.7 %collective-permute-start = (f32[728,128]{1,0:T(8,128)}, f32[728,128]{1,0:T(8,128)S(1)}, u32[]{:S(2)}, u32[]{:S(2)}) collective-permute-start(f32[728,128]{1,0:T(8,128)} %get-tuple-element.17), channel_id=1, source_target_pairs={{0,1},{1,2},{2,3},{3,4},{4,5},{5,6},{6,7},{8,9},{9,10},{10,11},{11... | collective-permute-start | bytes 1118216 | tf_op jit(solution)/shard_map/ppermute | solution.py:716
  6.6 19.4 %collective-permute-start.1 = (f32[728,128]{1,0:T(8,128)}, f32[728,128]{1,0:T(8,128)S(1)}, u32[]{:S(2)}, u32[]{:S(2)}) collective-permute-start(f32[728,128]{1,0:T(8,128)} %get-tuple-element.18), channel_id=1, source_target_pairs={{1,0},{2,1},{3,2},{4,3},{5,4},{6,5},{7,6},{9,8},{10,9},{11,10},{12... | collective-permute-start | bytes 1118216 | tf_op jit(solution)/shard_map/ppermute | solution.py:717
  11.2 1.5 %copy-start = (f32[3472,128]{1,0:T(8,128)S(1)}, f32[3472,128]{1,0:T(8,128)}, u32[]{:S(2)}) copy-start(f32[3472,128]{1,0:T(8,128)} %get-tuple-element.16.own) | copy-start | bytes 5332996
  12.7 0.7 copy-start.2
  26.2 13.9 %collective-permute-start.3 = (f32[584,128]{1,0:T(8,128)S(1)}, f32[584,128]{1,0:T(8,128)S(1)}, u32[]{:S(2)}, u32[]{:S(2)}) collective-permute-start(f32[584,128]{1,0:T(8,128)S(1)} %get-tuple-element.20), channel_id=1, source_target_pairs={{64,0},{128,64},{192,128},{256,192},{320,256},{384,320},{448,384},... | collective-permute-start | bytes 897032 | tf_op jit(solution)/shard_map/ppermute | solution.py:717
  27.5 12.6 %collective-permute-start.2 = (f32[584,128]{1,0:T(8,128)S(1)}, f32[584,128]{1,0:T(8,128)S(1)}, u32[]{:S(2)}, u32[]{:S(2)}) collective-permute-start(f32[584,128]{1,0:T(8,128)S(1)} %get-tuple-element.19._), channel_id=1, source_target_pairs={{0,64},{64,128},{128,192},{192,256},{256,320},{320,384},{384,448},... | collective-permute-start | bytes 897032 | tf_op jit(solution)/shard_map/ppermute | solution.py:716
  45.1 12.6 %collective-permute-start.4 = (f32[984,128]{1,0:T(8,128)S(1)}, f32[984,128]{1,0:T(8,128)S(1)}, u32[]{:S(2)}, u32[]{:S(2)}) collective-permute-start(f32[984,128]{1,0:T(8,128)S(1)} %get-tuple-element.22.up), channel_id=1, source_target_pairs={{0,8},{8,16},{16,24},{24,32},{32,40},{40,48},{48,56},{1,9},{9,17},... | collective-permute-start | bytes 1511432 | tf_op jit(solution)/shard_map/ppermute | solution.py:716
  47.1 10.7 %collective-permute-start.5 = (f32[984,128]{1,0:T(8,128)S(1)}, f32[984,128]{1,0:T(8,128)S(1)}, u32[]{:S(2)}, u32[]{:S(2)}) collective-permute-start(f32[984,128]{1,0:T(8,128)S(1)} %get-tuple-element.23.down), channel_id=1, source_target_pairs={{8,0},{16,8},{24,16},{32,24},{40,32},{48,40},{56,48},{9,1},{17,9},... | collective-permute-start | bytes 1511432 | tf_op jit(solution)/shard_map/ppermute | solution.py:717
  50.7 7.0 %copy-start.1 = (f32[12,6,6,128]{3,2,1,0:T(8,128)S(1)}, f32[12,6,6,128]{3,2,1,0:T(8,128)}, u32[]{:S(2)}) copy-start(f32[12,6,6,128]{3,2,1,0:T(8,128)} %old.1) | copy-start | bytes 663556

commit v5 on v4

--- a/solution.py
+++ b/solution.py
@@ -65,14 +65,14 @@
 GROUPS = {"all": 2, "density": 2, "near": 8}
 
 
-def pairs(mode, src, four, two, use, count, tile, cols, table):
+def pairs(mode, src, four, two, use, count, used, tile, cols, table):
     many, regs = NEAR[mode], GROUPS[mode]
     for u in range(many - 1):
         four[count + u] = jnp.int32(0)
-        two[count + u] = jnp.int32(0)
+        if two is not None:
+            two[count + u] = jnp.int32(0)
         use[count + u] = jnp.float32(0.0)
     steps = lax.div(count + (many - 1), many)
-    used = jnp.sum(jnp.where(tile[3:4] > 0.0, 1.0, 0.0)).astype(jnp.int32)
     for n, c in enumerate((0, 1, 2, 4)):
         if mode == "near" and n == 3:
             break
@@ -101,7 +101,7 @@
                 if mode != "near":
                     near[3] = near[3] * jnp.where(flag >= 0.5, 1.0, 0.0)
                 if mode != "density":
-                    t = two[at]
+                    t = f + 4 if two is None else two[at]
                     near.append(jnp.broadcast_to(src[pl.ds(t, 1), :], (8, 128)))
                     weight = jnp.broadcast_to(src[pl.ds(t + 1, 1), :], (8, 128))
                     near.append(weight * jnp.where(flag == 1.0, 1.0, 0.0))
@@ -142,8 +142,8 @@
     words[at] = words[at] | lax.shift_left(jnp.int32(1), place)
 
 
-def corner(k):
-    return lax.div(k, SY * SZ), lax.rem(lax.div(k, SZ), SY), lax.rem(k, SZ)
+def corner(code):
+    return lax.shift_right_logical(code, 6), lax.shift_right_logical(code, 3) & 7, code & 7
 
 
 def pack(
@@ -160,24 +160,28 @@
     def scan(q, n):
         y, z = lax.div(q, SZ), lax.rem(q, SZ)
         for x in range(SX):
-            ids[n] = (x * SY + y) * SZ + z
+            ids[n] = x * 64 + y * 8 + z
             n = n + active[y, z, x]
         return n
 
     number = lax.fori_loop(0, SY * SZ, scan, jnp.int32(0))
-    for s in range(MOST, 15):
-        ids[s] = jnp.int32(0)
     ids[15] = number
+    copies[1].wait()
     lane = lax.broadcasted_iota(jnp.int32, (8, 128), 1)
-    tail = jnp.zeros((8, 128), jnp.int32)
-    for s in range(MOST):
-        tail = jnp.where(lane == s, ids[s], tail)
-    tail = jnp.where(lane == 15, number, tail).astype(jnp.float32)
+
+    def tell(s, tail):
+        code = ids[s]
+        x, y, z = corner(code)
+        ids[16 + s] = counts[y, z, x]
+        tail = jnp.where(lane == s, code, tail)
+        return jnp.where(lane == 16 + s, counts[y, z, x], tail)
+
+    tail = lax.fori_loop(0, number, tell, jnp.where(lane == 15, number, 0)).astype(jnp.float32)
     own[ZERO : ZERO + 8] = jnp.zeros((8, 128), jnp.float32)
     own[OWN_TAIL : OWN_TAIL + 8] = tail
     up[Z_TAIL : Z_TAIL + 8] = tail
     down[Z_TAIL : Z_TAIL + 8] = tail
-    for copy in copies[1:]:
+    for copy in copies[2:]:
         copy.wait()
     sub = lax.broadcasted_iota(jnp.int32, (SZ, 128), 0)
     slot = lax.broadcasted_iota(jnp.int32, (SZ, 128), 1)
@@ -232,8 +236,8 @@
     clear(flags, SX * SY)
 
     def one(s, _):
-        k = ids[s]
-        mark(flags, lax.div(k, SZ), lax.rem(k, SZ))
+        x, y, z = corner(ids[s])
+        mark(flags, x * SY + y, z)
         return 0
 
     lax.fori_loop(0, number, one, 0)
@@ -241,8 +245,7 @@
         sums[...] = before[...]
 
     def slot(s, _):
-        k = ids[s]
-        a, b, d = corner(k)
+        a, b, d = corner(ids[s])
         count = jnp.int32(0)
         in_z = [(d + ed >= 0) & (d + ed < SZ) for ed in (-1, 0, 1)]
         for ea in (-1, 0, 1):
@@ -254,13 +257,11 @@
                 row = column * (SZ * 8) + d * 8
                 for n, ed in enumerate((-1, 0, 1)):
                     four[count] = row + ed * 8
-                    two[count] = row + (ed * 8 + 4)
                     known = bit(word, jnp.maximum(d + ed, 0))
                     use[count] = jnp.where(known > 0, jnp.float32(0.5), jnp.float32(1.0))
                     count = count + (inside & in_z[n]).astype(jnp.int32)
-        row = pl.multiple_of(k * 8, 8)
-        tile = own[pl.ds(row, 8), :]
-        sums[s] = pairs("all", own, four, two, use, count, tile, cols, table)
+        tile = own[pl.ds(pl.multiple_of(own_row(a, b, d), 8), 8), :]
+        sums[s] = pairs("all", own, four, None, use, count, ids[16 + s], tile, cols, table)
         return 0
 
     if part == 0:
@@ -372,16 +373,28 @@
         second = rows[pl.ds(f2 + y * add2, 2), :]
         return jnp.concatenate([first, second, jnp.zeros((2, 128), jnp.float32)], axis=0)
 
-    def own_sums(x, y, z):
+    def own_sums(x, y, z, used):
         count = near_list(x, y, z, True)
-        return pairs("all", rows, four, two, use, count, cell(x, y, z), cols, table)
-
-    def halo_cell(x, y, z):
+        return pairs("all", rows, four, two, use, count, used, cell(x, y, z), cols, table)
+
+    def halo_cell(x, y, z, used):
         count = near_list(x, y, z, False)
         tile = cell(x, y, z)
-        return tile, pairs("density", rows, four, two, use, count, tile, cols, table)
+        return tile, pairs("density", rows, four, None, use, count, used, tile, cols, table)
 
     return own_sums, halo_cell
+
+
+def beside(places, mine, x, y, z):
+    def one(t, found):
+        close = (
+            (jnp.abs(places[0, t] - x) <= 1)
+            & (jnp.abs(places[1, t] - y) <= 1)
+            & (jnp.abs(places[2, t] - z) <= 1)
+        )
+        return found | close.astype(jnp.int32)
+
+    return lax.fori_loop(0, mine, one, jnp.int32(0)) > 0
 
 
 def on_border(x, z):
@@ -393,7 +406,7 @@
 
 
 def slab_faces(
-    ids, own, zlo, zhi, xlo, xhi, before, up, down, tiles, sums, places,
+    own, zlo, zhi, xlo, xhi, before, up, down, tiles, sums, places,
     rows, tails, lists, sem, four, two, use, flags, cols, table,
 ):
     tails[...] = jnp.zeros(tails.shape, jnp.int32)
@@ -429,6 +442,7 @@
             places[0, n] = x
             places[1, n] = b
             places[2, n] = z
+            places[3, n] = lists[q, 16 + s]
 
             @pl.when(inside)
             def _():
@@ -437,8 +451,8 @@
             return n + inside.astype(jnp.int32)
 
         number = lax.fori_loop(0, lists[q, 15], one, number)
-    places[3, 0] = number
-    places[3, 1] = lists[0, 15]
+    places[4, 0] = number
+    places[4, 1] = lists[0, 15]
     mine = lists[0, 15]
 
     lane = lax.broadcasted_iota(jnp.int32, (8, 128), 1)
@@ -450,7 +464,7 @@
         for n, edge in enumerate((SY - 1, 0)):
             here = y == edge
             at = jnp.where(here, numbers[n], 126)
-            value = jnp.where(line == 0, x, z)
+            value = jnp.where(line == 0, x, jnp.where(line == 1, z, places[3, s]))
             lists_[n] = jnp.where(lane == at, value, lists_[n])
             numbers[n] = numbers[n] + here.astype(jnp.int32)
         return tuple(lists_), tuple(numbers)
@@ -486,7 +500,7 @@
         def _():
             @pl.when(on_border(x, z))
             def _():
-                sums[s] = sums[s] + own_sums(x, y, z)
+                sums[s] = sums[s] + own_sums(x, y, z, places[3, s])
 
             tiles[s, 6:7] = sums[s, 0:1]
             send_sum(s, x, y, z)
@@ -499,7 +513,7 @@
 
         @pl.when(on_face(y))
         def _():
-            tiles[s], total = halo_cell(x, y, z)
+            tiles[s], total = halo_cell(x, y, z, places[3, s])
             tiles[s, 6:7] = total
             send_sum(s, x, y, z)
 
@@ -516,7 +530,7 @@
     gather(rows, own, zlo, zhi, xlo, xhi)
     tiles[...] = tiles_in[...]
     sums[...] = sums_in[...]
-    number, mine = places[3, 0], places[3, 1]
+    number, mine = places[4, 0], places[4, 1]
     clear(flags, (SX + 2) * SY)
 
     def one(s, _):
@@ -533,7 +547,7 @@
         def _():
             @pl.when(on_border(x, z))
             def _():
-                sums[s, 0:7] = sums[s, 0:7] + own_sums(x, y, z)[0:7]
+                sums[s, 0:7] = sums[s, 0:7] + own_sums(x, y, z, places[3, s])[0:7]
 
             tiles[s, 6:7] = sums[s, 0:1]
 
@@ -542,9 +556,9 @@
     def halo_slot(s, _):
         x, y, z = places[0, s], places[1, s], places[2, s]
 
-        @pl.when(jnp.logical_not(on_face(y)))
+        @pl.when(jnp.logical_not(on_face(y)) & beside(places, mine, x, y, z))
         def _():
-            tiles[s], total = halo_cell(x, y, z)
+            tiles[s], total = halo_cell(x, y, z, places[3, s])
             tiles[s, 6:7] = total
 
         return 0
@@ -554,13 +568,15 @@
 
 
 def finish(
-    places, ylo, yhi, up, down, tiles, sums, old, density, accel,
-    rows, cells, final, spots, tails, lists, sem, four, two, use, flags, cols, table,
+    places_in, ylo, yhi, up, down, tiles, sums, old, density, accel,
+    places, places_sem, rows, cells, final, spots, tails, lists, sem, four, two, use, flags, cols, table,
 ):
     tails[0:8] = ylo[Y_TAIL:Y_ROWS].astype(jnp.int32)
     tails[8:16] = yhi[Y_TAIL:Y_ROWS].astype(jnp.int32)
     copy = pltpu.make_async_copy(tails, lists, sem)
     copy.start()
+    other = pltpu.make_async_copy(places_in, places, places_sem)
+    other.start()
     rows[0:Y_ROWS] = ylo[...]
     rows[Y_ROWS : 2 * Y_ROWS] = yhi[...]
     rows[2 * Y_ROWS : 3 * Y_ROWS] = down[...]
@@ -568,18 +584,19 @@
     density[...] = old[...]
     accel[...] = jnp.zeros(accel.shape, jnp.float32)
     clear(flags, 2 * (SX + 2))
-    number, mine = places[3, 0], places[3, 1]
-
-    def take(s, _):
-        for c in range(3):
-            spots[c, s] = places[c, s]
-        cells[pl.ds(pl.multiple_of(s * 8, 8), 8), :] = tiles[s]
-        return 0
-
-    lax.fori_loop(0, number, take, 0)
+    other.wait()
+    number, mine = places[4, 0], places[4, 1]
+
+    def take(s, n):
+        for c in range(4):
+            spots[c, n] = places[c, s]
+        cells[pl.ds(pl.multiple_of(n * 8, 8), 8), :] = tiles[s]
+        wanted = beside(places, mine, places[0, s], places[1, s], places[2, s])
+        return n + wanted.astype(jnp.int32)
+
+    total = lax.fori_loop(0, number, take, jnp.int32(0))
     final[...] = sums[...]
     copy.wait()
-    total = number
     for side in range(2):
 
         def one(s, n, side=side):
@@ -587,6 +604,7 @@
             spots[0, n] = x
             spots[1, n] = jnp.int32(-1 if side == 0 else SY)
             spots[2, n] = z
+            spots[3, n] = lists[side * 8 + 2, s]
             mark(flags, side * (SX + 2) + x + 1, z + 1)
             at = (x + 1) * (SZ + 2) + z + 1
             base = side * Y_ROWS
@@ -601,7 +619,8 @@
                 ],
                 axis=0,
             )
-            return n + 1
+            wanted = beside(spots, mine, x, jnp.int32(-1 if side == 0 else SY), z)
+            return n + wanted.astype(jnp.int32)
 
         total = lax.fori_loop(0, lists[side * 8, 127], one, total)
 
@@ -628,7 +647,7 @@
             spot = pl.multiple_of(s * 8, 8)
             tile = cells[pl.ds(spot, 8), :]
             count = jnp.int32(9)
-            result = pairs("all", rows, four, two, use, count, tile, cols, table)
+            result = pairs("all", rows, four, two, use, count, spots[3, s], tile, cols, table)
             final[s, 0:7] = final[s, 0:7] + result[0:7]
             cells[pl.ds(spot + 6, 1), :] = tile[6:7] + result[0:1]
 
@@ -643,7 +662,7 @@
             spot = pl.multiple_of(s * 8, 8)
             tile = cells[pl.ds(spot, 8), :]
             count = jnp.int32(9)
-            result = pairs("density", rows, four, two, use, count, tile, cols, table)
+            result = pairs("density", rows, four, None, use, count, spots[3, s], tile, cols, table)
             cells[pl.ds(spot + 6, 1), :] = tile[6:7] + result
 
         return 0
@@ -682,14 +701,15 @@
                 & (jnp.abs(spots[2, t] - z) <= 1)
             )
             four[n] = t * 8
-            two[n] = t * 8 + 4
             use[n] = jnp.float32(1.0)
             return n + close.astype(jnp.int32)
 
         count = lax.fori_loop(0, total, check, jnp.int32(0))
         spot = pl.multiple_of(s * 8, 8)
         tile = cells[pl.ds(spot, 8), :]
-        result = final[s] + pairs("near", cells, four, two, use, count, tile, cols, table)
+        result = final[s] + pairs(
+            "near", cells, four, None, use, count, spots[3, s], tile, cols, table
+        )
         good = tile[3:4] > 0.0
         own = final[s, 7:8] * tile[7:8]
         place = (x, y, pl.ds(z, 1), slice(None))
@@ -749,7 +769,7 @@
     small = [jnp.transpose(v, (1, 2, 0)) for v in (counts, active)]
     own, z_up, z_down, ids = call(
         pack,
-        (f32(OWN_ROWS, S), f32(Z_ROWS, S), f32(Z_ROWS, S), i32(16)),
+        (f32(OWN_ROWS, S), f32(Z_ROWS, S), f32(Z_ROWS, S), i32(32)),
         (VMEM, VMEM, VMEM, SMEM),
         [ANY] * 7,
         [
@@ -780,9 +800,9 @@
     )(ids, own, first, x_up)
     y_up, y_down, tiles, sums, places = call(
         slab_faces,
-        (f32(Y_ROWS, S), f32(Y_ROWS, S), f32(SLAB_MOST, 8, S), f32(16, 8, S), i32(4, 128)),
+        (f32(Y_ROWS, S), f32(Y_ROWS, S), f32(SLAB_MOST, 8, S), f32(16, 8, S), i32(8, 128)),
         (VMEM, VMEM, VMEM, VMEM, SMEM),
-        [SMEM] + [VMEM] * 6,
+        [VMEM] * 6,
         [
             pltpu.VMEM((SLAB, S), jnp.float32),
             pltpu.VMEM((16, S), jnp.int32),
@@ -791,7 +811,7 @@
         ]
         + work((SX + 2) * SY, 48),
         4,
-    )(ids, own, zlo, zhi, xlo, xhi, second)
+    )(own, zlo, zhi, xlo, xhi, second)
     ylo, yhi = neighbours(y_up, y_down, "gy")
     tiles, sums = call(
         slab_inside,
@@ -805,8 +825,10 @@
         finish,
         (f32(SX, SY, SZ, S), f32(3, SX, SY, SZ, S)),
         (VMEM, VMEM),
-        [SMEM] + [VMEM] * 7,
+        [ANY] + [VMEM] * 7,
         [
+            pltpu.SMEM((8, 128), jnp.int32),
+            pltpu.SemaphoreType.DMA,
             pltpu.VMEM((4 * Y_ROWS, S), jnp.float32),
             pltpu.VMEM((ALL_MOST * 8, S), jnp.float32),
             pltpu.VMEM((16, 8, S), jnp.float32),

time: 74.2 us -> 73.1 us (0.985)
  the two profiles are of different devices: /device:TPU:452 before, /device:TPU:202 now
where the time goes in v5:
time: 73.1 us; the launch traced here: 72.8 us
  Pallas kernels  47.2 us (65%)
  starting transfers between devices  18.7 us (26%)
  waiting for transfers between devices  3.92 us (5%)
  local copies, waits for them, and re-layouts  2.13 us (3%)
  between operations  0.76 us (1%)
    pallas_call x1, Pallas kernels, per_device(): call(finish, (f32(SX, SY, SZ, S), f32(3, SX, SY, SZ, S)), (VMEM, VMEM), [...  14.4 us
    ppermute x3, starting transfers between devices, neighbours(): low = lax.ppermute(up, axis, pairs_)  11.2 us
    pallas_call x1, Pallas kernels, per_device(): call(local_first, f32(16, 8, S), VMEM, [SMEM, VMEM], work(SX * SY, 48), 8)  11 us
    pallas_call x1, Pallas kernels, per_device(): call(local_second, f32(16, 8, S), VMEM, [SMEM, VMEM, VMEM, ANY], work(SX...  8.84 us
    ppermute x3, starting transfers between devices, neighbours(): high = lax.ppermute(down, axis, [(j, i) for i, j in pairs_])  7.48 us
    pallas_call x1, Pallas kernels, per_device(): call(slab_faces, (f32(Y_ROWS, S), f32(Y_ROWS, S), f32(SLAB_MOST, 8, S), f...  5.57 us
    pallas_call x1, Pallas kernels, per_device(): call(pack, (f32(OWN_ROWS, S), f32(Z_ROWS, S), f32(Z_ROWS, S), i32(32)), (...  4.73 us
    pallas_call x1, Pallas kernels, per_device(): call(slab_inside, (f32(SLAB_MOST, 8, S), f32(16, 8, S)), (VMEM, VMEM), [S...  2.53 us
  transfers between devices with their start and end apart: 6, of which 2 were waited for; matrix products, arithmetic and copies ran while one was open for 0% of the time, Pallas kernels for 31%

profile of v5, /device:TPU:202, one launch (start us, length us, event | category | flops | bytes accessed | tf_op | source)
XLA Modules:
  0.0 72.8 jit_solution(8347336233791322578)
XLA Ops:
  0.6 4.7 %shard_map.86 = (f32[3472,128]{1,0:T(8,128)}, f32[728,128]{1,0:T(8,128)}, f32[728,128]{1,0:T(8,128)}, s32[32]{0:T(128)}) custom-call(s32[6,6,12]{2,1,0:T(8,128)} %bitcast.2, s32[6,6,12]{2,1,0:T(8,128)} %bitcast.3, f32[3,12,6,6,128]{4,3,2,1,0:T(8,128)} %pos_in.1, f32[12,6,6,128]{3,2,1,0:T(8,128)} %mass_in.1, f32[12,6,6,128]{3,2,1,0:T(8,128)} %support_in.1, ...), custom_call_target="tpu_custom_call" | custom-call | flops 20000000 | bytes 4000000 | tf_op jit(solution)/shard_map/pallas_call | solution.py:770
  5.4 5.4 %collective-permute-start = (f32[728,128]{1,0:T(8,128)}, f32[728,128]{1,0:T(8,128)S(1)}, u32[]{:S(2)}, u32[]{:S(2)}) collective-permute-start(f32[728,128]{1,0:T(8,128)} %get-tuple-element.16), channel_id=1, source_target_pairs={{0,1},{1,2},{2,3},{3,4},{4,5},{5,6},{6,7},{8,9},{9,10},{10,11},{11... | collective-permute-start | bytes 1118216 | tf_op jit(solution)/shard_map/ppermute | solution.py:736
  10.8 1.9 %collective-permute-start.1 = (f32[728,128]{1,0:T(8,128)}, f32[728,128]{1,0:T(8,128)S(1)}, u32[]{:S(2)}, u32[]{:S(2)}) collective-permute-start(f32[728,128]{1,0:T(8,128)} %get-tuple-element.17), channel_id=1, source_target_pairs={{1,0},{2,1},{3,2},{4,3},{5,4},{6,5},{7,6},{9,8},{10,9},{11,10},{12... | collective-permute-start | bytes 1118216 | tf_op jit(solution)/shard_map/ppermute | solution.py:737
  12.7 0.0 copy-start
  12.7 1.5 %copy-done = f32[3472,128]{1,0:T(8,128)S(1)} copy-done((f32[3472,128]{1,0:T(8,128)S(1)}, f32[3472,128]{1,0:T(8,128)}, u32[]{:S(2)}) %copy-start) | copy-done | bytes 1777688
  14.2 0.0 copy-start.2
  14.2 0.7 copy-done.2
  14.8 11.0 %shard_map.87._.before = f32[16,8,128]{2,1,0:T(8,128)S(1)} custom-call(s32[32]{0:T(128)S(1)} %copy-done.2, f32[3472,128]{1,0:T(8,128)S(1)} %copy-done), custom_call_target="tpu_custom_call" | custom-call | flops 80000000 | bytes 16000000 | tf_op jit(solution)/shard_map/pallas_call | solution.py:786
  25.9 0.0 collective-permute-done.zlo
  25.9 0.0 collective-permute-done.1.zhi
  25.9 0.1 shard_map.88
  26.0 1.9 %collective-permute-start.3 = (f32[584,128]{1,0:T(8,128)S(1)}, f32[584,128]{1,0:T(8,128)S(1)}, u32[]{:S(2)}, u32[]{:S(2)}) collective-permute-start(f32[584,128]{1,0:T(8,128)S(1)} %get-tuple-element.20), channel_id=1, source_target_pairs={{64,0},{128,64},{192,128},{256,192},{320,256},{384,320},{448,384},... | collective-permute-start | bytes 897032 | tf_op jit(solution)/shard_map/ppermute | solution.py:737
  28.0 3.9 %collective-permute-start.2 = (f32[584,128]{1,0:T(8,128)S(1)}, f32[584,128]{1,0:T(8,128)S(1)}, u32[]{:S(2)}, u32[]{:S(2)}) collective-permute-start(f32[584,128]{1,0:T(8,128)S(1)} %get-tuple-element.19._), channel_id=1, source_target_pairs={{0,64},{64,128},{128,192},{192,256},{256,320},{320,384},{384,448},... | collective-permute-start | bytes 897032 | tf_op jit(solution)/shard_map/ppermute | solution.py:736
  31.9 8.8 %shard_map.89.before = f32[16,8,128]{2,1,0:T(8,128)S(1)} custom-call(s32[32]{0:T(128)S(1)} %copy-done.2, f32[3472,128]{1,0:T(8,128)S(1)} %copy-done, f32[16,8,128]{2,1,0:T(8,128)S(1)} %shard_map.87._.before, f32[584,128]{1,0:T(8,128)S(1)} %get-tuple-element.19._), custom_call_target="tpu_custom_call" | custom-call | flops 80000000 | bytes 16000000 | tf_op jit(solution)/shard_map/pallas_call | solution.py:793
  40.7 0.0 collective-permute-done.3.xhi
  40.7 0.0 collective-permute-done.2.xlo
  40.7 5.6 %shard_map.90 = (f32[984,128]{1,0:T(8,128)S(1)}, f32[984,128]{1,0:T(8,128)S(1)}, f32[96,8,128]{2,1,0:T(8,128)S(1)}, f32[16,8,128]{2,1,0:T(8,128)S(1)}, s32[8,128]{1,0:T(8,128)S(1)}) custom-call(f32[3472,128]{1,0:T(8,128)S(1)} %copy-done, f32[728,128]{1,0:T(8,128)S(1)} %collective-permute-done.zlo, f32[728,128]{1,0:T(8,128)S(1)} %collective-permute-done.1.zhi, ...), custom_call_target="tpu_custom_call" | custom-call | flops 40000000 | bytes 8000000 | tf_op jit(solution)/shard_map/pallas_call | solution.py:801
  46.3 1.9 %collective-permute-start.4 = (f32[984,128]{1,0:T(8,128)S(1)}, f32[984,128]{1,0:T(8,128)S(1)}, u32[]{:S(2)}, u32[]{:S(2)}) collective-permute-start(f32[984,128]{1,0:T(8,128)S(1)} %get-tuple-element.22.up), channel_id=1, source_target_pairs={{0,8},{8,16},{16,24},{24,32},{32,40},{40,48},{48,56},{1,9},{9,17},... | collective-permute-start | bytes 1511432 | tf_op jit(solution)/shard_map/ppermute | solution.py:736
  48.2 3.6 %collective-permute-start.5 = (f32[984,128]{1,0:T(8,128)S(1)}, f32[984,128]{1,0:T(8,128)S(1)}, u32[]{:S(2)}, u32[]{:S(2)}) collective-permute-start(f32[984,128]{1,0:T(8,128)S(1)} %get-tuple-element.23.down), channel_id=1, source_target_pairs={{8,0},{16,8},{24,16},{32,24},{40,32},{48,40},{56,48},{9,1},{17,9},... | collective-permute-start | bytes 1511432 | tf_op jit(solution)/shard_map/ppermute | solution.py:737
  51.9 0.0 copy-start.1
  51.9 2.5 %shard_map.91 = (f32[96,8,128]{2,1,0:T(8,128)S(1)}, f32[16,8,128]{2,1,0:T(8,128)S(1)}) custom-call(s32[8,128]{1,0:T(8,128)S(1)} %get-tuple-element.21.places.places_in, f32[3472,128]{1,0:T(8,128)S(1)} %copy-done, f32[728,128]{1,0:T(8,128)S(1)} %collective-permute-done.zlo, f32[728,128]{1,0:T(8,128)S(1)} %collective-permute-done.1.zhi, ...), custom_call_target="tpu_custom_call" | custom-call | flops 60000000 | bytes 12000000 | tf_op jit(solution)/shard_map/pallas_call | solution.py:816
  54.5 2.1 %collective-permute-done.4.ylo = f32[984,128]{1,0:T(8,128)S(1)} collective-permute-done((f32[984,128]{1,0:T(8,128)S(1)}, f32[984,128]{1,0:T(8,128)S(1)}, u32[]{:S(2)}, u32[]{:S(2)}) %collective-permute-start.4) | collective-permute-done | bytes 503840 | tf_op jit(solution)/shard_map/ppermute | solution.py:736
  56.6 1.8 %collective-permute-done.5.yhi = f32[984,128]{1,0:T(8,128)S(1)} collective-permute-done((f32[984,128]{1,0:T(8,128)S(1)}, f32[984,128]{1,0:T(8,128)S(1)}, u32[]{:S(2)}, u32[]{:S(2)}) %collective-permute-start.5) | collective-permute-done | bytes 503840 | tf_op jit(solution)/shard_map/ppermute | solution.py:737
  58.4 0.0 copy-done.1
  58.4 14.4 %shard_map.92 = (f32[12,6,6,128]{3,2,1,0:T(8,128)}, f32[3,12,6,6,128]{4,3,2,1,0:T(8,128)}) custom-call(s32[8,128]{1,0:T(8,128)S(1)} %get-tuple-element.21.places.places_in, f32[984,128]{1,0:T(8,128)S(1)} %collective-permute-done.4.ylo, f32[984,128]{1,0:T(8,128)S(1)} %collective-permute-done.5.yhi, f32[984,128]{1,0:T(8,128)S(1)} %get-tuple-element.22.up, ...), custom_call_target="tpu_custom_call" | custom-call | flops 80000000 | bytes 16000000 | tf_op jit(solution)/shard_map/pallas_call | solution.py:824
Async XLA Ops:
  5.4 20.5 %collective-permute-start = (f32[728,128]{1,0:T(8,128)}, f32[728,128]{1,0:T(8,128)S(1)}, u32[]{:S(2)}, u32[]{:S(2)}) collective-permute-start(f32[728,128]{1,0:T(8,128)} %get-tuple-element.16), channel_id=1, source_target_pairs={{0,1},{1,2},{2,3},{3,4},{4,5},{5,6},{6,7},{8,9},{9,10},{10,11},{11... | collective-permute-start | bytes 1118216 | tf_op jit(solution)/shard_map/ppermute | solution.py:736
  10.8 15.1 %collective-permute-start.1 = (f32[728,128]{1,0:T(8,128)}, f32[728,128]{1,0:T(8,128)S(1)}, u32[]{:S(2)}, u32[]{:S(2)}) collective-permute-start(f32[728,128]{1,0:T(8,128)} %get-tuple-element.17), channel_id=1, source_target_pairs={{1,0},{2,1},{3,2},{4,3},{5,4},{6,5},{7,6},{9,8},{10,9},{11,10},{12... | collective-permute-start | bytes 1118216 | tf_op jit(solution)/shard_map/ppermute | solution.py:737
  12.7 1.5 %copy-start = (f32[3472,128]{1,0:T(8,128)S(1)}, f32[3472,128]{1,0:T(8,128)}, u32[]{:S(2)}) copy-start(f32[3472,128]{1,0:T(8,128)} %get-tuple-element.15.own) | copy-start | bytes 5332996
  14.2 0.7 copy-start.2
  26.0 14.7 %collective-permute-start.3 = (f32[584,128]{1,0:T(8,128)S(1)}, f32[584,128]{1,0:T(8,128)S(1)}, u32[]{:S(2)}, u32[]{:S(2)}) collective-permute-start(f32[584,128]{1,0:T(8,128)S(1)} %get-tuple-element.20), channel_id=1, source_target_pairs={{64,0},{128,64},{192,128},{256,192},{320,256},{384,320},{448,384},... | collective-permute-start | bytes 897032 | tf_op jit(solution)/shard_map/ppermute | solution.py:737
  28.0 12.8 %collective-permute-start.2 = (f32[584,128]{1,0:T(8,128)S(1)}, f32[584,128]{1,0:T(8,128)S(1)}, u32[]{:S(2)}, u32[]{:S(2)}) collective-permute-start(f32[584,128]{1,0:T(8,128)S(1)} %get-tuple-element.19._), channel_id=1, source_target_pairs={{0,64},{64,128},{128,192},{192,256},{256,320},{320,384},{384,448},... | collective-permute-start | bytes 897032 | tf_op jit(solution)/shard_map/ppermute | solution.py:736
  46.3 10.3 %collective-permute-start.4 = (f32[984,128]{1,0:T(8,128)S(1)}, f32[984,128]{1,0:T(8,128)S(1)}, u32[]{:S(2)}, u32[]{:S(2)}) collective-permute-start(f32[984,128]{1,0:T(8,128)S(1)} %get-tuple-element.22.up), channel_id=1, source_target_pairs={{0,8},{8,16},{16,24},{24,32},{32,40},{40,48},{48,56},{1,9},{9,17},... | collective-permute-start | bytes 1511432 | tf_op jit(solution)/shard_map/ppermute | solution.py:736
  48.2 10.1 %collective-permute-start.5 = (f32[984,128]{1,0:T(8,128)S(1)}, f32[984,128]{1,0:T(8,128)S(1)}, u32[]{:S(2)}, u32[]{:S(2)}) collective-permute-start(f32[984,128]{1,0:T(8,128)S(1)} %get-tuple-element.23.down), channel_id=1, source_target_pairs={{8,0},{16,8},{24,16},{32,24},{40,32},{48,40},{56,48},{9,1},{17,9},... | collective-permute-start | bytes 1511432 | tf_op jit(solution)/shard_map/ppermute | solution.py:737
  51.9 6.5 %copy-start.1 = (f32[12,6,6,128]{3,2,1,0:T(8,128)S(1)}, f32[12,6,6,128]{3,2,1,0:T(8,128)}, u32[]{:S(2)}) copy-start(f32[12,6,6,128]{3,2,1,0:T(8,128)} %old.1) | copy-start | bytes 663556

commit v6 on v5

--- a/solution.py
+++ b/solution.py
@@ -27,6 +27,7 @@
 XHI = XLO + X_ROWS
 SLAB = XHI + X_ROWS
 
+FIRST_PART = 8000
 SLAB_MOST = 96
 ALL_MOST = 256
 
@@ -65,8 +66,8 @@
 GROUPS = {"all": 2, "density": 2, "near": 8}
 
 
-def pairs(mode, src, four, two, use, count, used, tile, cols, table):
-    many, regs = NEAR[mode], GROUPS[mode]
+def pairs(mode, src, four, two, use, count, used, tile, cols, table, many=None):
+    many, regs = many or NEAR[mode], GROUPS[mode]
     for u in range(many - 1):
         four[count + u] = jnp.int32(0)
         if two is not None:
@@ -147,8 +148,8 @@
 
 
 def pack(
-    counts_in, active_in, pos_in, mass_in, support_in, entropy_in, old_in, own, up, down, ids,
-    counts, active, pos, mass, support, entropy, old, sems,
+    counts_in, active_in, pos_in, mass_in, support_in, entropy_in, old_in, own_out, up, down, ids,
+    counts, active, pos, mass, support, entropy, old, own, sems, out_sems,
 ):
     given = (active_in, counts_in, pos_in, mass_in, support_in, entropy_in, old_in)
     held = (active, counts, pos, mass, support, entropy, old)
@@ -157,42 +158,28 @@
         copy.start()
     copies[0].wait()
 
-    def scan(q, n):
-        y, z = lax.div(q, SZ), lax.rem(q, SZ)
-        for x in range(SX):
-            ids[n] = x * 64 + y * 8 + z
-            n = n + active[y, z, x]
-        return n
-
-    number = lax.fori_loop(0, SY * SZ, scan, jnp.int32(0))
-    ids[15] = number
-    copies[1].wait()
-    lane = lax.broadcasted_iota(jnp.int32, (8, 128), 1)
-
-    def tell(s, tail):
-        code = ids[s]
-        x, y, z = corner(code)
-        ids[16 + s] = counts[y, z, x]
-        tail = jnp.where(lane == s, code, tail)
-        return jnp.where(lane == 16 + s, counts[y, z, x], tail)
-
-    tail = lax.fori_loop(0, number, tell, jnp.where(lane == 15, number, 0)).astype(jnp.float32)
+    for copy in copies[1:]:
+        copy.wait()
     own[ZERO : ZERO + 8] = jnp.zeros((8, 128), jnp.float32)
-    own[OWN_TAIL : OWN_TAIL + 8] = tail
-    up[Z_TAIL : Z_TAIL + 8] = tail
-    down[Z_TAIL : Z_TAIL + 8] = tail
-    for copy in copies[2:]:
-        copy.wait()
+    size = SY * SZ * 8
+
+    def plane(x):
+        spot = pl.ds(pl.multiple_of(x * size, 8), size)
+        return pltpu.make_async_copy(own.at[spot], own_out.at[spot], out_sems.at[x])
+
     sub = lax.broadcasted_iota(jnp.int32, (SZ, 128), 0)
     slot = lax.broadcasted_iota(jnp.int32, (SZ, 128), 1)
 
-    def cells(x, _):
+    def cells(x, n):
         for y in range(SY):
             many = jnp.zeros((SZ, 128), jnp.int32)
             act = jnp.zeros((SZ, 128), jnp.int32)
             for z in range(SZ):
                 many = jnp.where(sub == z, counts[y, z, x], many)
-                act = jnp.where(sub == z, active[y, z, x], act)
+                here = active[y, z, x]
+                act = jnp.where(sub == z, here, act)
+                ids[n] = x * 64 + y * 8 + z
+                n = n + here
             h = support[x, y]
             inv = 1.0 / h
             inv2 = inv * inv
@@ -206,9 +193,26 @@
                 (pos[0, x, y], pos[1, x, y], pos[2, x, y], m, h, weight, gain)
             ):
                 own[pl.ds(base + c, SZ, stride=8), :] = value
-        return 0
-
-    lax.fori_loop(0, SX, cells, 0)
+        plane(x).start()
+        return n
+
+    number = lax.fori_loop(0, SX, cells, jnp.int32(0))
+    ids[15] = number
+    lane = lax.broadcasted_iota(jnp.int32, (8, 128), 1)
+
+    def tell(s, tail):
+        code = ids[s]
+        x, y, z = corner(code)
+        ids[16 + s] = counts[y, z, x]
+        tail = jnp.where(lane == s, code, tail)
+        return jnp.where(lane == 16 + s, counts[y, z, x], tail)
+
+    tail = lax.fori_loop(0, number, tell, jnp.where(lane == 15, number, 0)).astype(jnp.float32)
+    own[OWN_TAIL : OWN_TAIL + 8] = tail
+    up[Z_TAIL : Z_TAIL + 8] = tail
+    down[Z_TAIL : Z_TAIL + 8] = tail
+    rest = pltpu.make_async_copy(own.at[pl.ds(ZERO, 16)], own_out.at[pl.ds(ZERO, 16)], out_sems.at[SX])
+    rest.start()
 
     def faces(x2, _):
         for u in range(2):
@@ -224,6 +228,13 @@
 
     lax.fori_loop(0, SX // 2, faces, 0)
 
+    def finished(x, _):
+        plane(x).wait()
+        return 0
+
+    lax.fori_loop(0, SX, finished, 0)
+    rest.wait()
+
 
 def own_row(x, y, z):
     return ((x * SY + y) * SZ + z) * 8
@@ -231,7 +242,25 @@
 
 def local(part, ids, own, before, sums, four, two, use, flags, cols, table):
     number = ids[15]
-    half = lax.div(number + 1, 2)
+
+    def price(s):
+        x, y, z = corner(ids[s])
+
+        def span(at, size):
+            return 3 - (at == 0).astype(jnp.int32) - (at == size - 1).astype(jnp.int32)
+
+        near = span(x, SX) * span(y, SY) * span(z, SZ)
+        return near * lax.shift_right_logical(ids[16 + s] + 15, 4) * 14 + 400
+
+    total = lax.fori_loop(0, number, lambda s, n: n + price(s), jnp.int32(0))
+    limit = jnp.maximum(jnp.int32(FIRST_PART), lax.shift_right_logical(total, 1))
+
+    def fits(s, state):
+        n, spent = state
+        spent = spent + price(s)
+        return n + (spent <= limit).astype(jnp.int32), spent
+
+    half, _ = lax.fori_loop(0, number, fits, (jnp.int32(0), jnp.int32(0)))
 
     clear(flags, SX * SY)
 
@@ -261,7 +290,7 @@
                     use[count] = jnp.where(known > 0, jnp.float32(0.5), jnp.float32(1.0))
                     count = count + (inside & in_z[n]).astype(jnp.int32)
         tile = own[pl.ds(pl.multiple_of(own_row(a, b, d), 8), 8), :]
-        sums[s] = pairs("all", own, four, None, use, count, ids[16 + s], tile, cols, table)
+        sums[s] = pairs("all", own, four, None, use, count, ids[16 + s], tile, cols, table, 6)
         return 0
 
     if part == 0:
@@ -405,6 +434,29 @@
     return (y == 0) | (y == SY - 1)
 
 
+def weigh(cells, total):
+    def some(q, _):
+        base = pl.multiple_of(q * 64, 64)
+
+        def get(c):
+            return cells[pl.ds(base + c, 8, stride=8), :]
+
+        good = get(3) > 0.0
+        inv = 1.0 / jnp.where(good, get(4), 1.0)
+        inv2 = inv * inv
+        inv4 = inv2 * inv2
+        fresh = (4.0 * KC) * (inv4 * inv4) * get(6)
+        safe = jnp.where(good, fresh, 1.0)
+        power = jnp.exp(jnp.log(safe) * (-1.0 / 3.0))
+        weight = get(5) * power
+        cells[pl.ds(base + 5, 8, stride=8), :] = jnp.where(good, weight, 0.0)
+        cells[pl.ds(base + 6, 8, stride=8), :] = safe
+        cells[pl.ds(base + 7, 8, stride=8), :] = power
+        return 0
+
+    lax.fori_loop(0, lax.div(total + 7, 8), some, 0)
+
+
 def slab_faces(
     own, zlo, zhi, xlo, xhi, before, up, down, tiles, sums, places,
     rows, tails, lists, sem, four, two, use, flags, cols, table,
@@ -525,7 +577,7 @@
 
 def slab_inside(
     places, own, zlo, zhi, xlo, xhi, tiles_in, sums_in, tiles, sums,
-    rows, four, two, use, flags, cols, table,
+    cells, rows, four, two, use, flags, cols, table,
 ):
     gather(rows, own, zlo, zhi, xlo, xhi)
     tiles[...] = tiles_in[...]
@@ -565,6 +617,40 @@
 
     lax.fori_loop(0, mine, own_slot, 0)
     lax.fori_loop(mine, number, halo_slot, 0)
+
+    def take(s, _):
+        cells[pl.ds(pl.multiple_of(s * 8, 8), 8), :] = tiles[s]
+        return 0
+
+    lax.fori_loop(0, number, take, 0)
+    weigh(cells, number)
+
+    def inner(s, _):
+        x, y, z = places[0, s], places[1, s], places[2, s]
+
+        def check(t, n):
+            close = (
+                (jnp.abs(places[0, t] - x) <= 1)
+                & (jnp.abs(places[1, t] - y) <= 1)
+                & (jnp.abs(places[2, t] - z) <= 1)
+                & jnp.logical_not(on_face(places[1, t]))
+            )
+            four[n] = t * 8
+            use[n] = jnp.float32(1.0)
+            return n + close.astype(jnp.int32)
+
+        count = lax.fori_loop(0, number, check, jnp.int32(0))
+
+        @pl.when(count > 0)
+        def _():
+            tile = cells[pl.ds(pl.multiple_of(s * 8, 8), 8), :]
+            sums[s, 4:7] = sums[s, 4:7] + pairs(
+                "near", cells, four, None, use, count, places[3, s], tile, cols, table
+            )[4:7]
+
+        return 0
+
+    lax.fori_loop(0, mine, inner, 0)
 
 
 def finish(
@@ -647,7 +733,7 @@
             spot = pl.multiple_of(s * 8, 8)
             tile = cells[pl.ds(spot, 8), :]
             count = jnp.int32(9)
-            result = pairs("all", rows, four, two, use, count, spots[3, s], tile, cols, table)
+            result = pairs("all", rows, four, two, use, count, spots[3, s], tile, cols, table, 9)
             final[s, 0:7] = final[s, 0:7] + result[0:7]
             cells[pl.ds(spot + 6, 1), :] = tile[6:7] + result[0:1]
 
@@ -670,26 +756,7 @@
     lax.fori_loop(0, mine, across_own, 0)
     lax.fori_loop(mine, total, across_halo, 0)
 
-    def weigh(q, _):
-        base = pl.multiple_of(q * 64, 64)
-
-        def get(c):
-            return cells[pl.ds(base + c, 8, stride=8), :]
-
-        good = get(3) > 0.0
-        inv = 1.0 / jnp.where(good, get(4), 1.0)
-        inv2 = inv * inv
-        inv4 = inv2 * inv2
-        fresh = (4.0 * KC) * (inv4 * inv4) * get(6)
-        safe = jnp.where(good, fresh, 1.0)
-        power = jnp.exp(jnp.log(safe) * (-1.0 / 3.0))
-        weight = get(5) * power
-        cells[pl.ds(base + 5, 8, stride=8), :] = jnp.where(good, weight, 0.0)
-        cells[pl.ds(base + 6, 8, stride=8), :] = safe
-        cells[pl.ds(base + 7, 8, stride=8), :] = power
-        return 0
-
-    lax.fori_loop(0, lax.div(total + 7, 8), weigh, 0)
+    weigh(cells, total)
 
     def last(s, _):
         x, y, z = spots[0, s], spots[1, s], spots[2, s]
@@ -699,6 +766,7 @@
                 (jnp.abs(spots[0, t] - x) <= 1)
                 & (jnp.abs(spots[1, t] - y) <= 1)
                 & (jnp.abs(spots[2, t] - z) <= 1)
+                & ((spots[1, t] <= 0) | (spots[1, t] >= SY - 1))
             )
             four[n] = t * 8
             use[n] = jnp.float32(1.0)
@@ -707,15 +775,19 @@
         count = lax.fori_loop(0, total, check, jnp.int32(0))
         spot = pl.multiple_of(s * 8, 8)
         tile = cells[pl.ds(spot, 8), :]
-        result = final[s] + pairs(
-            "near", cells, four, None, use, count, spots[3, s], tile, cols, table
-        )
+
+        @pl.when(count > 0)
+        def _():
+            final[s, 4:7] = final[s, 4:7] + pairs(
+                "near", cells, four, None, use, count, spots[3, s], tile, cols, table
+            )[4:7]
+
         good = tile[3:4] > 0.0
         own = final[s, 7:8] * tile[7:8]
         place = (x, y, pl.ds(z, 1), slice(None))
         density[place] = jnp.where(good, tile[6:7], old[place])
         for c in range(3):
-            push = (20.0 * KC) * (own * final[s, 1 + c : 2 + c] + result[4 + c : 5 + c])
+            push = (20.0 * KC) * (own * final[s, 1 + c : 2 + c] + final[s, 4 + c : 5 + c])
             accel[(c, *place)] = jnp.where(good, push, 0.0)
         return 0
 
@@ -770,7 +842,7 @@
     own, z_up, z_down, ids = call(
         pack,
         (f32(OWN_ROWS, S), f32(Z_ROWS, S), f32(Z_ROWS, S), i32(32)),
-        (VMEM, VMEM, VMEM, SMEM),
+        (ANY, VMEM, VMEM, SMEM),
         [ANY] * 7,
         [
             pltpu.SMEM((SY, SZ, SX), jnp.int32),
@@ -778,7 +850,11 @@
             pltpu.VMEM((3, SX, SY, SZ, S), jnp.float32),
         ]
         + [pltpu.VMEM((SX, SY, SZ, S), jnp.float32)] * 4
-        + [pltpu.SemaphoreType.DMA((7,))],
+        + [
+            pltpu.VMEM((OWN_ROWS, S), jnp.float32),
+            pltpu.SemaphoreType.DMA((7,)),
+            pltpu.SemaphoreType.DMA((SX + 1,)),
+        ],
         2,
         56,
     )(*small, positions, mass, support, entropy, density_old)
@@ -818,7 +894,8 @@
         (f32(SLAB_MOST, 8, S), f32(16, 8, S)),
         (VMEM, VMEM),
         [SMEM] + [VMEM] * 7,
-        [pltpu.VMEM((SLAB, S), jnp.float32)] + work((SX + 2) * SY, 48),
+        [pltpu.VMEM((SLAB_MOST * 8, S), jnp.float32), pltpu.VMEM((SLAB, S), jnp.float32)]
+        + work((SX + 2) * SY, SLAB_MOST + 16),
         6,
     )(places, own, zlo, zhi, xlo, xhi, tiles, sums)
     return call(

time: 73.1 us -> 65.8 us (0.900)
  the two profiles are of different devices: /device:TPU:202 before, /device:TPU:27 now
where the time goes in v6:
time: 65.8 us; the launch traced here: 65.5 us
  Pallas kernels  45.8 us (70%)
  starting transfers between devices  16.1 us (24%)
  local copies, waits for them, and re-layouts  2.13 us (3%)
  between operations  0.76 us (1%)
  waiting for transfers between devices  0.75 us (1%)
    pallas_call x1, Pallas kernels, per_device(): call(finish, (f32(SX, SY, SZ, S), f32(3, SX, SY, SZ, S)), (VMEM, VMEM), [...  10.8 us
    ppermute x3, starting transfers between devices, neighbours(): low = lax.ppermute(up, axis, pairs_)  10.3 us
    pallas_call x1, Pallas kernels, per_device(): call(local_second, f32(16, 8, S), VMEM, [SMEM, VMEM, VMEM, ANY], work(SX...  10.1 us
    pallas_call x1, Pallas kernels, per_device(): call(local_first, f32(16, 8, S), VMEM, [SMEM, VMEM], work(SX * SY, 48), 8)  8.69 us
    pallas_call x1, Pallas kernels, per_device(): call(slab_inside, (f32(SLAB_MOST, 8, S), f32(16, 8, S)), (VMEM, VMEM), [S...  7.24 us
    ppermute x3, starting transfers between devices, neighbours(): high = lax.ppermute(down, axis, [(j, i) for i, j in pairs_])  5.75 us
    pallas_call x1, Pallas kernels, per_device(): call(slab_faces, (f32(Y_ROWS, S), f32(Y_ROWS, S), f32(SLAB_MOST, 8, S), f...  4.48 us
    pallas_call x1, Pallas kernels, per_device(): call(pack, (f32(OWN_ROWS, S), f32(Z_ROWS, S), f32(Z_ROWS, S), i32(32)), (...  4.36 us
  transfers between devices with their start and end apart: 6, of which 2 were waited for; matrix products, arithmetic and copies ran while one was open for 0% of the time, Pallas kernels for 40%

profile of v6, /device:TPU:27, one launch (start us, length us, event | category | flops | bytes accessed | tf_op | source)
XLA Modules:
  0.0 65.5 jit_solution(3654351072296629068)
XLA Ops:
  0.6 4.4 %shard_map.86 = (f32[3472,128]{1,0:T(8,128)}, f32[728,128]{1,0:T(8,128)}, f32[728,128]{1,0:T(8,128)}, s32[32]{0:T(128)}) custom-call(s32[6,6,12]{2,1,0:T(8,128)} %bitcast.2, s32[6,6,12]{2,1,0:T(8,128)} %bitcast.3, f32[3,12,6,6,128]{4,3,2,1,0:T(8,128)} %pos_in.1, f32[12,6,6,128]{3,2,1,0:T(8,128)} %mass_in.1, f32[12,6,6,128]{3,2,1,0:T(8,128)} %support_in.1, ...), custom_call_target="tpu_custom_call" | custom-call | flops 20000000 | bytes 4000000 | tf_op jit(solution)/shard_map/pallas_call | solution.py:842
  5.0 4.0 %collective-permute-start = (f32[728,128]{1,0:T(8,128)}, f32[728,128]{1,0:T(8,128)S(1)}, u32[]{:S(2)}, u32[]{:S(2)}) collective-permute-start(f32[728,128]{1,0:T(8,128)} %get-tuple-element.16), channel_id=1, source_target_pairs={{0,1},{1,2},{2,3},{3,4},{4,5},{5,6},{6,7},{8,9},{9,10},{10,11},{11... | collective-permute-start | bytes 1118216 | tf_op jit(solution)/shard_map/ppermute | solution.py:808
  9.0 1.3 %collective-permute-start.1 = (f32[728,128]{1,0:T(8,128)}, f32[728,128]{1,0:T(8,128)S(1)}, u32[]{:S(2)}, u32[]{:S(2)}) collective-permute-start(f32[728,128]{1,0:T(8,128)} %get-tuple-element.17), channel_id=1, source_target_pairs={{1,0},{2,1},{3,2},{4,3},{5,4},{6,5},{7,6},{9,8},{10,9},{11,10},{12... | collective-permute-start | bytes 1118216 | tf_op jit(solution)/shard_map/ppermute | solution.py:809
  10.3 0.0 copy-start
  10.3 1.5 %copy-done = f32[3472,128]{1,0:T(8,128)S(1)} copy-done((f32[3472,128]{1,0:T(8,128)S(1)}, f32[3472,128]{1,0:T(8,128)}, u32[]{:S(2)}) %copy-start) | copy-done | bytes 1777688
  11.8 0.0 copy-start.2
  11.8 0.7 copy-done.2
  12.4 8.7 %shard_map.87._.before = f32[16,8,128]{2,1,0:T(8,128)S(1)} custom-call(s32[32]{0:T(128)S(1)} %copy-done.2, f32[3472,128]{1,0:T(8,128)S(1)} %copy-done), custom_call_target="tpu_custom_call" | custom-call | flops 80000000 | bytes 16000000 | tf_op jit(solution)/shard_map/pallas_call | solution.py:862
  21.1 0.0 collective-permute-done.zlo
  21.1 0.1 collective-permute-done.1.zhi
  21.3 0.1 shard_map.88
  21.4 2.1 %collective-permute-start.3 = (f32[584,128]{1,0:T(8,128)S(1)}, f32[584,128]{1,0:T(8,128)S(1)}, u32[]{:S(2)}, u32[]{:S(2)}) collective-permute-start(f32[584,128]{1,0:T(8,128)S(1)} %get-tuple-element.20), channel_id=1, source_target_pairs={{64,0},{128,64},{192,128},{256,192},{320,256},{384,320},{448,384},... | collective-permute-start | bytes 897032 | tf_op jit(solution)/shard_map/ppermute | solution.py:809
  23.4 4.4 %collective-permute-start.2 = (f32[584,128]{1,0:T(8,128)S(1)}, f32[584,128]{1,0:T(8,128)S(1)}, u32[]{:S(2)}, u32[]{:S(2)}) collective-permute-start(f32[584,128]{1,0:T(8,128)S(1)} %get-tuple-element.19._), channel_id=1, source_target_pairs={{0,64},{64,128},{128,192},{192,256},{256,320},{320,384},{384,448},... | collective-permute-start | bytes 897032 | tf_op jit(solution)/shard_map/ppermute | solution.py:808
  27.9 10.1 %shard_map.89.before = f32[16,8,128]{2,1,0:T(8,128)S(1)} custom-call(s32[32]{0:T(128)S(1)} %copy-done.2, f32[3472,128]{1,0:T(8,128)S(1)} %copy-done, f32[16,8,128]{2,1,0:T(8,128)S(1)} %shard_map.87._.before, f32[584,128]{1,0:T(8,128)S(1)} %get-tuple-element.19._), custom_call_target="tpu_custom_call" | custom-call | flops 80000000 | bytes 16000000 | tf_op jit(solution)/shard_map/pallas_call | solution.py:869
  38.0 0.0 collective-permute-done.3.xhi
  38.0 0.0 collective-permute-done.2.xlo
  38.0 4.5 %shard_map.90 = (f32[984,128]{1,0:T(8,128)S(1)}, f32[984,128]{1,0:T(8,128)S(1)}, f32[96,8,128]{2,1,0:T(8,128)S(1)}, f32[16,8,128]{2,1,0:T(8,128)S(1)}, s32[8,128]{1,0:T(8,128)S(1)}) custom-call(f32[3472,128]{1,0:T(8,128)S(1)} %copy-done, f32[728,128]{1,0:T(8,128)S(1)} %collective-permute-done.zlo, f32[728,128]{1,0:T(8,128)S(1)} %collective-permute-done.1.zhi, ...), custom_call_target="tpu_custom_call" | custom-call | flops 40000000 | bytes 8000000 | tf_op jit(solution)/shard_map/pallas_call | solution.py:877
  42.5 1.9 %collective-permute-start.4 = (f32[984,128]{1,0:T(8,128)S(1)}, f32[984,128]{1,0:T(8,128)S(1)}, u32[]{:S(2)}, u32[]{:S(2)}) collective-permute-start(f32[984,128]{1,0:T(8,128)S(1)} %get-tuple-element.22.up), channel_id=1, source_target_pairs={{0,8},{8,16},{16,24},{24,32},{32,40},{40,48},{48,56},{1,9},{9,17},... | collective-permute-start | bytes 1511432 | tf_op jit(solution)/shard_map/ppermute | solution.py:808
  44.4 2.4 %collective-permute-start.5 = (f32[984,128]{1,0:T(8,128)S(1)}, f32[984,128]{1,0:T(8,128)S(1)}, u32[]{:S(2)}, u32[]{:S(2)}) collective-permute-start(f32[984,128]{1,0:T(8,128)S(1)} %get-tuple-element.23.down), channel_id=1, source_target_pairs={{8,0},{16,8},{24,16},{32,24},{40,32},{48,40},{56,48},{9,1},{17,9},... | collective-permute-start | bytes 1511432 | tf_op jit(solution)/shard_map/ppermute | solution.py:809
  46.8 0.0 copy-start.1
  46.9 7.2 %shard_map.91 = (f32[96,8,128]{2,1,0:T(8,128)S(1)}, f32[16,8,128]{2,1,0:T(8,128)S(1)}) custom-call(s32[8,128]{1,0:T(8,128)S(1)} %get-tuple-element.21.places.places_in, f32[3472,128]{1,0:T(8,128)S(1)} %copy-done, f32[728,128]{1,0:T(8,128)S(1)} %collective-permute-done.zlo, f32[728,128]{1,0:T(8,128)S(1)} %collective-permute-done.1.zhi, ...), custom_call_target="tpu_custom_call" | custom-call | flops 60000000 | bytes 12000000 | tf_op jit(solution)/shard_map/pallas_call | solution.py:892
  54.1 0.0 collective-permute-done.4.ylo
  54.1 0.6 collective-permute-done.5.yhi
  54.7 0.0 copy-done.1
  54.7 10.8 %shard_map.92 = (f32[12,6,6,128]{3,2,1,0:T(8,128)}, f32[3,12,6,6,128]{4,3,2,1,0:T(8,128)}) custom-call(s32[8,128]{1,0:T(8,128)S(1)} %get-tuple-element.21.places.places_in, f32[984,128]{1,0:T(8,128)S(1)} %collective-permute-done.4.ylo, f32[984,128]{1,0:T(8,128)S(1)} %collective-permute-done.5.yhi, f32[984,128]{1,0:T(8,128)S(1)} %get-tuple-element.22.up, ...), custom_call_target="tpu_custom_call" | custom-call | flops 80000000 | bytes 16000000 | tf_op jit(solution)/shard_map/pallas_call | solution.py:901
Async XLA Ops:
  5.0 16.1 %collective-permute-start = (f32[728,128]{1,0:T(8,128)}, f32[728,128]{1,0:T(8,128)S(1)}, u32[]{:S(2)}, u32[]{:S(2)}) collective-permute-start(f32[728,128]{1,0:T(8,128)} %get-tuple-element.16), channel_id=1, source_target_pairs={{0,1},{1,2},{2,3},{3,4},{4,5},{5,6},{6,7},{8,9},{9,10},{10,11},{11... | collective-permute-start | bytes 1118216 | tf_op jit(solution)/shard_map/ppermute | solution.py:808
  9.0 12.3 %collective-permute-start.1 = (f32[728,128]{1,0:T(8,128)}, f32[728,128]{1,0:T(8,128)S(1)}, u32[]{:S(2)}, u32[]{:S(2)}) collective-permute-start(f32[728,128]{1,0:T(8,128)} %get-tuple-element.17), channel_id=1, source_target_pairs={{1,0},{2,1},{3,2},{4,3},{5,4},{6,5},{7,6},{9,8},{10,9},{11,10},{12... | collective-permute-start | bytes 1118216 | tf_op jit(solution)/shard_map/ppermute | solution.py:809
  10.3 1.5 %copy-start = (f32[3472,128]{1,0:T(8,128)S(1)}, f32[3472,128]{1,0:T(8,128)}, u32[]{:S(2)}) copy-start(f32[3472,128]{1,0:T(8,128)} %get-tuple-element.15.own) | copy-start | bytes 5332996
  11.8 0.7 copy-start.2
  21.4 16.6 %collective-permute-start.3 = (f32[584,128]{1,0:T(8,128)S(1)}, f32[584,128]{1,0:T(8,128)S(1)}, u32[]{:S(2)}, u32[]{:S(2)}) collective-permute-start(f32[584,128]{1,0:T(8,128)S(1)} %get-tuple-element.20), channel_id=1, source_target_pairs={{64,0},{128,64},{192,128},{256,192},{320,256},{384,320},{448,384},... | collective-permute-start | bytes 897032 | tf_op jit(solution)/shard_map/ppermute | solution.py:809
  23.4 14.6 %collective-permute-start.2 = (f32[584,128]{1,0:T(8,128)S(1)}, f32[584,128]{1,0:T(8,128)S(1)}, u32[]{:S(2)}, u32[]{:S(2)}) collective-permute-start(f32[584,128]{1,0:T(8,128)S(1)} %get-tuple-element.19._), channel_id=1, source_target_pairs={{0,64},{64,128},{128,192},{192,256},{256,320},{320,384},{384,448},... | collective-permute-start | bytes 897032 | tf_op jit(solution)/shard_map/ppermute | solution.py:808
  42.5 11.6 %collective-permute-start.4 = (f32[984,128]{1,0:T(8,128)S(1)}, f32[984,128]{1,0:T(8,128)S(1)}, u32[]{:S(2)}, u32[]{:S(2)}) collective-permute-start(f32[984,128]{1,0:T(8,128)S(1)} %get-tuple-element.22.up), channel_id=1, source_target_pairs={{0,8},{8,16},{16,24},{24,32},{32,40},{40,48},{48,56},{1,9},{9,17},... | collective-permute-start | bytes 1511432 | tf_op jit(solution)/shard_map/ppermute | solution.py:808
  44.4 10.3 %collective-permute-start.5 = (f32[984,128]{1,0:T(8,128)S(1)}, f32[984,128]{1,0:T(8,128)S(1)}, u32[]{:S(2)}, u32[]{:S(2)}) collective-permute-start(f32[984,128]{1,0:T(8,128)S(1)} %get-tuple-element.23.down), channel_id=1, source_target_pairs={{8,0},{16,8},{24,16},{32,24},{40,32},{48,40},{56,48},{9,1},{17,9},... | collective-permute-start | bytes 1511432 | tf_op jit(solution)/shard_map/ppermute | solution.py:809
  46.8 7.9 %copy-start.1 = (f32[12,6,6,128]{3,2,1,0:T(8,128)S(1)}, f32[12,6,6,128]{3,2,1,0:T(8,128)}, u32[]{:S(2)}) copy-start(f32[12,6,6,128]{3,2,1,0:T(8,128)} %old.1) | copy-start | bytes 663556
